TPU v7x, 256 devices: a whole 4x4x8 slice. The times are simulated.
256 devices in a mesh: dp: 256 (over z, y, x, core).
Axes of the slice: x: 4, y: 4, z: 8, core: 2. Of those that a mesh axis runs over, the one named last changes fastest.
Arguments:
- activations: bfloat16 [32768, 8192], P('dp'), may hold values from -6 to 6
- cotangent: bfloat16 [32768, 2048], P('dp'), may hold values from -0.5 to 0.5
- kept_tiles: int32 [256, 8], replicated, may hold values from 0 to 1023, as said below
- kept_counts: int32 [256], replicated, may hold values from 1 to 8
- chosen: int32 [256], replicated, may hold values from 0 to 1023, as said below
Outputs:
- summed_tiles: bfloat16 [256, 128, 128], replicated
Inputs may be any that keep to these rules, and one draw needn't show every extreme that they name: `kept_tiles`: the 8 ids of one row lie in 8 different regions, where region of tile t is t // (1024 / 256); entries past the row's count are padding and name tiles too. `chosen`: entry q is a tile of region q.
All inputs are finite; a program needn't handle non-finite values.
Results may differ from a plain program's by a relative error of at most 0.001.
Values may be sent and summed in bfloat16 or wider, within the bound.
No kernel may reach another device: no remote copies, remote signals or barrier semaphores. Data moves between devices by JAX's collectives and lax.ppermute only.
A program may use at most 128 MiB of HBM per device.

v0:
```python
import jax
import jax.numpy as jnp
from jax import lax
from jax.sharding import PartitionSpec as P

TILE = 128
KEPT = 8


def local(activations, cotangent, kept_tiles, kept_counts, chosen):
    me = lax.axis_index("dp")
    tok_rows, ffw = activations.shape
    dwin = cotangent.shape[1]
    col_blocks = dwin // TILE
    own_ids = lax.dynamic_index_in_dim(kept_tiles, me, 0, keepdims=False)
    own_count = lax.dynamic_index_in_dim(kept_counts, me, 0, keepdims=False)
    live = jnp.arange(KEPT, dtype=jnp.int32) < own_count
    left = jnp.take(activations.reshape(tok_rows, ffw // TILE, TILE), own_ids // col_blocks, axis=1)
    right = jnp.take(cotangent.reshape(tok_rows, col_blocks, TILE), own_ids % col_blocks, axis=1)
    tiles = jnp.einsum("skr,skc->krc", left, right, preferred_element_type=jnp.float32)
    tiles = tiles * live[:, None, None].astype(jnp.float32)
    match = ((own_ids[None, :] == chosen[:, None]) & live[None, :]).astype(jnp.float32)
    terms = jnp.dot(match, tiles.reshape(KEPT, TILE * TILE), precision=lax.Precision.HIGHEST)
    summed = lax.psum_scatter(
        terms.reshape(lax.axis_size("dp") * 1, TILE, TILE), "dp", scatter_dimension=0, tiled=True
    )
    rounded = summed.astype(jnp.bfloat16)
    return lax.all_gather(rounded, "dp", axis=0, tiled=True)


def solution(mesh):
    return jax.shard_map(
        local,
        mesh=mesh,
        in_specs=(P("dp", None), P("dp", None), P(), P(), P()),
        out_specs=P(),
        check_vma=False,
    )
```

profile of v0, /device:TPU:1, one launch (start us, length us, event | category | flops | bytes accessed | tf_op | source)
XLA Modules:
  0.0 1481.0 jit_solution(6170729813284497407)
XLA Ops:
  6.5 0.0 copy-start
  6.5 0.0 copy-start.1
  6.5 0.0 reduce-scatter.2.cloned.1.call-start
  6.5 0.7 copy-done
  7.2 0.2 dynamic-slice_reduce_fusion
  7.5 1.3 dynamic_slice.9
  8.7 0.6 iota_compare_fusion
  9.4 1.3 copy.18
  10.7 0.3 copy.19
  11.0 3.2 copy.16
  14.2 2.9 copy.17
  17.1 0.6 gather_fusion.1
  17.7 2.2 gather_fusion
  19.9 0.4 fusion
  20.3 0.0 copy-done.1
  20.3 6.8 fusion.1
  27.1 20.2 %copy.21 = f32[256,128,128]{2,1,0:T(8,128)} copy(f32[256,128,128]{2,0,1:T(8,128)S(1)} %fusion.1) | data formatting | bytes 33554432 | tf_op jit(solution)/shard_map/dot_general | solution.py:23
  47.3 0.0 reduce-scatter.2.cloned.1.call-update
  47.4 0.0 all-gather.2.cloned.1.call-start
  47.4 1292.7 %reduce-scatter.2.cloned.1.call-done = f32[1,128,128]{2,1,0:T(8,128)} async-done(((f32[256,128,128]{2,1,0:T(8,128)}), f32[1,128,128]{2,1,0:T(8,128)}) %reduce-scatter.2.cloned.1.call-update) | async-done | bytes 65552 | tf_op jit(solution)/shard_map/reduce_scatter | solution.py:24
  1340.1 1.5 convert_element_type.13
  1341.6 0.0 all-gather.2.cloned.1.call-update
  1341.6 122.0 %all-gather.2.cloned.1.call-done = bf16[256,128,128]{2,1,0:T(8,128)(2,1)} async-done(((bf16[1,128,128]{2,1,0:T(8,128)(2,1)}), bf16[256,128,128]{2,1,0:T(8,128)(2,1)}) %all-gather.2.cloned.1.call-update) | async-done | bytes 8388624 | tf_op jit(solution)/shard_map/all_gather | solution.py:28
  1463.7 10.5 copy.29
  (3 shorter events, 0.0 us)
Async XLA Ops:
  6.5 0.7 copy-start
  6.5 13.8 copy-start.1
  6.5 1333.6 %reduce-scatter.2.cloned.1.call-start = ((), (), s32[]{:S(2)}) async-start(), calls=%async_computation.1 | async-start | bytes 16842752 | tf_op jit(solution)/shard_map/reduce_scatter | solution.py:24
  47.4 1416.3 %all-gather.2.cloned.1.call-start = ((), (), s32[]{:S(2)}) async-start(), calls=%async_computation.2 | async-start | bytes 8421376 | tf_op jit(solution)/shard_map/all_gather | solution.py:28
Sparse Core Ops, SparseCore 0:
  47.5 1292.6 reduce-scatter.1
  1344.3 119.3 all-gather.1
where the time goes:
time: 1480 us
  waiting for transfers between devices  1410 us (95%)
  local copies, waits for them, and re-layouts  43.4 us (3%)
    reduce_scatter x1, waiting for transfers between devices, local(): lax.psum_scatter(terms.reshape(lax.axis_size('dp') * 1, TILE, TILE), 'dp'...  1290 us
    all_gather x1, waiting for transfers between devices, local(): return lax.all_gather(rounded, 'dp', axis=0, tiled=True)  122 us
  transfers between devices with their start and end apart: 2, of which 2 were waited for; matrix products, arithmetic and copies ran while one was open for 0% of the time, Pallas kernels for 0%

commit v1 on v0

v1 whole, which is shorter than its diff:
```python
import jax
import jax.numpy as jnp
from jax import lax
from jax.experimental import pallas as pl
from jax.experimental.pallas import tpu as pltpu
from jax.sharding import PartitionSpec as P

TILE = 128
KEPT = 8
N_DP = 256
COLS = 16
ZN, YN, XN, CN = 8, 4, 4, 2
CHIPS = 128
HALF = 128
HALF_TILES = 512
VMEM_LIMIT = 48 * 1024 * 1024


def dev(z, y, x, c):
    return ((z * YN + y) * XN + x) * CN + c


DEVS = [(z, y, x, c) for z in range(ZN) for y in range(YN) for x in range(XN) for c in range(CN)]
CHIP_GROUPS = [[chip * CN + c for chip in range(CHIPS)] for c in range(CN)]
Z_GROUPS = [[dev(z, y, x, c) for z in range(ZN)] for y in range(YN) for x in range(XN) for c in range(CN)]
SWAP = [(d, d ^ 1) for d in range(N_DP)]


def ring(step, turn):
    pairs = []
    for z, y, x, c in DEVS:
        if (c + turn) % 2 == 0:
            pairs.append((dev(z, y, x, c), dev(z, (y + step) % YN, x, c)))
        else:
            pairs.append((dev(z, y, x, c), dev(z, y, (x + step) % XN, c)))
    return pairs


def tiles_kernel(ids_ref, act_ref, cot_ref, out_ref, lefts, rights, stage, sems):
    copies = []
    for k in range(KEPT):
        tile = ids_ref[k]
        row = pl.multiple_of((tile // COLS) * TILE, TILE)
        col = pl.multiple_of((tile % COLS) * TILE, TILE)
        a = pltpu.make_async_copy(act_ref.at[:, pl.ds(row, TILE)], lefts.at[k], sems.at[k, 0])
        b = pltpu.make_async_copy(cot_ref.at[:, pl.ds(col, TILE)], rights.at[k], sems.at[k, 1])
        a.start()
        b.start()
        copies.append((a, b))
    for k in range(KEPT):
        a, b = copies[k]
        a.wait()
        b.wait()
        half = ids_ref[k] // HALF_TILES
        tile = lax.dot_general(
            lefts[k], rights[k], (((0,), (0,)), ((), ())), preferred_element_type=jnp.float32
        )
        for p in range(4):
            for q in range(4):
                there = jnp.where(half == 0, p * 32 + q * 8, q * 32 + p * 8) + k * TILE
                here = p * 32 + q * 8
                stage[pl.ds(pl.multiple_of(there, 8), 8), :] = tile[here:here + 8, :]
    for chip in range(CHIPS):
        z, y, x = chip // 16, (chip // 4) % 4, chip % 4
        out_ref[chip] = stage[pl.ds(x * 32 + y * 8 + z, KEPT, stride=TILE), :]


def own_tiles(ids, activations, cotangent):
    return pl.pallas_call(
        tiles_kernel,
        out_shape=jax.ShapeDtypeStruct((CHIPS, KEPT, TILE), jnp.float32),
        in_specs=[
            pl.BlockSpec(memory_space=pltpu.SMEM),
            pl.BlockSpec(memory_space=pl.ANY),
            pl.BlockSpec(memory_space=pl.ANY),
        ],
        out_specs=pl.BlockSpec(memory_space=pltpu.VMEM),
        scratch_shapes=[
            pltpu.VMEM((KEPT, TILE, TILE), jnp.bfloat16),
            pltpu.VMEM((KEPT, TILE, TILE), jnp.bfloat16),
            pltpu.VMEM((KEPT * TILE, TILE), jnp.float32),
            pltpu.SemaphoreType.DMA((KEPT, 2)),
        ],
        compiler_params=pltpu.CompilerParams(vmem_limit_bytes=VMEM_LIMIT),
        name="own_tiles",
    )(ids, activations, cotangent)


def rows_kernel(place_ref, p0, p1, p2, p3, out_ref, wide):
    for step, piece in enumerate((p0, p1, p2, p3)):
        slot = place_ref[step]
        wide[pl.ds(pl.multiple_of(slot * ZN * HALF, ZN * HALF), ZN * HALF), :] = (
            piece[...].astype(jnp.float32).reshape(ZN * HALF, TILE)
        )

    def body(t, carry):
        rows = [wide[pl.ds(q * ZN * HALF + t, ZN, stride=HALF), :] for q in range(4)]
        out_ref[t] = jnp.concatenate(rows, axis=0).astype(jnp.bfloat16)
        return carry

    lax.fori_loop(0, HALF, body, 0, unroll=8)


def by_rows(place, pieces):
    return pl.pallas_call(
        rows_kernel,
        out_shape=jax.ShapeDtypeStruct((HALF, 4 * ZN, TILE), jnp.bfloat16),
        in_specs=[pl.BlockSpec(memory_space=pltpu.SMEM)] + [pl.BlockSpec(memory_space=pltpu.VMEM)] * 4,
        out_specs=pl.BlockSpec(memory_space=pltpu.VMEM),
        scratch_shapes=[pltpu.VMEM((4 * ZN * HALF, TILE), jnp.float32)],
        compiler_params=pltpu.CompilerParams(vmem_limit_bytes=VMEM_LIMIT),
        name="by_rows",
    )(place, *pieces)


def join_kernel(place_ref, *refs):
    pieces, out_ref, sems = refs[:8], refs[8], refs[9]
    copies = []
    for i, piece in enumerate(pieces):
        half = place_ref[8 + i]
        slot = place_ref[i]
        copies.append(pltpu.make_async_copy(
            piece, out_ref.at[pl.ds(pl.multiple_of(half * HALF, HALF), HALF), slot], sems.at[i]
        ))
    for copy in copies:
        copy.start()
    for copy in copies:
        copy.wait()


def join(place, pieces):
    return pl.pallas_call(
        join_kernel,
        out_shape=jax.ShapeDtypeStruct((N_DP, 4, 32, TILE), jnp.bfloat16),
        in_specs=[pl.BlockSpec(memory_space=pltpu.SMEM)] + [pl.BlockSpec(memory_space=pl.ANY)] * 8,
        out_specs=pl.BlockSpec(memory_space=pl.ANY),
        scratch_shapes=[pltpu.SemaphoreType.DMA((8,))],
        name="join",
    )(place, *pieces)


def local(activations, cotangent, kept_tiles, kept_counts, chosen):
    me = lax.axis_index("dp")
    core = me % CN
    x = (me // CN) % XN
    y = (me // (CN * XN)) % YN
    own_ids = lax.dynamic_index_in_dim(kept_tiles, me, 0, keepdims=False)
    sent = own_tiles(own_ids, activations, cotangent)
    got = lax.all_to_all(sent, "dp", 0, 0, axis_index_groups=CHIP_GROUPS, tiled=True)

    live = jnp.arange(KEPT, dtype=jnp.int32)[None, :] < kept_counts[:, None]
    ids = jnp.where(live, kept_tiles, -1).reshape(CHIPS, CN, KEPT)
    ids = lax.dynamic_index_in_dim(ids, core, 1, keepdims=False).reshape(CHIPS * KEPT)
    match = (chosen[:, None] == ids[None, :]).astype(jnp.float32)
    part = jnp.dot(match, got.reshape(CHIPS * KEPT, TILE), precision=lax.Precision.HIGHEST)
    part = part.reshape(CN, HALF, TILE)
    mine = lax.dynamic_index_in_dim(part, core, 0, keepdims=False)
    theirs = lax.dynamic_index_in_dim(part, 1 - core, 0, keepdims=False)
    row = (mine + lax.ppermute(theirs, "dp", SWAP)).astype(jnp.bfloat16)

    rows = lax.all_to_all(
        jnp.broadcast_to(row[None], (ZN, HALF, TILE)), "dp", 0, 0, axis_index_groups=Z_GROUPS, tiled=True
    )
    steps = (0, 1, 3, 2)
    at0 = jnp.where(core == 0, y, x)
    at1 = jnp.where(core == 0, x, y)
    pieces = [rows] + [lax.ppermute(rows, "dp", ring(s, 0)) for s in steps[1:]]
    block = by_rows(jnp.stack([(at0 - s) % 4 for s in steps]), pieces)
    blocks = [block] + [lax.ppermute(block, "dp", ring(s, 1)) for s in steps[1:]]
    other = [lax.ppermute(b, "dp", SWAP) for b in blocks]
    place = jnp.stack(
        [(at1 - s) % 4 for s in steps] + [(at0 - s) % 4 for s in steps] + [core] * 4 + [1 - core] * 4
    )
    return join(place, blocks + other).reshape(N_DP, TILE, TILE)


def solution(mesh):
    return jax.shard_map(
        local,
        mesh=mesh,
        in_specs=(P("dp", None), P("dp", None), P(), P(), P()),
        out_specs=P(),
        check_vma=False,
    )
```

time: 1480 us -> 362 us (0.24)
  waiting for transfers between devices: 1410 us -> 44 us
  Pallas kernels: 0 us -> 261 us
  local copies, waits for them, and re-layouts: 43.4 us -> 4.56 us
  starting transfers between devices: 0.04 us -> 34.8 us
  blocking collectives: 0 us -> 14.8 us
    reduce_scatter x1 -> x0, waiting for transfers between devices: 1290 us -> none  [local(): lax.psum_scatter(terms.reshape(lax.axis_size('dp') * 1, TILE, TILE), 'dp'...]
    pallas_call x0 -> x3, Pallas kernels: none -> 261 us  [the longest x1 256 us: join(): pl.pallas_call(join_kernel, out_shape=jax.ShapeDtypeStruct((N_DP, 4, 32,...]
    all_gather x1 -> x0, waiting for transfers between devices: 122 us -> none  [local(): return lax.all_gather(rounded, 'dp', axis=0, tiled=True)]
    ppermute x0 -> x11, waiting for transfers between devices: none -> 26.9 us  [the longest x3 16.9 us: local(): lax.ppermute(block, 'dp', ring(s, 1))]
    dot_general x1 -> x0, local copies, waits for them, and re-layouts: 20.2 us -> none  [local(): jnp.dot(match, tiles.reshape(KEPT, TILE * TILE), precision=lax.Precision....]
    ppermute x0 -> x11, starting transfers between devices: none -> 18.5 us  [the longest x4 9.84 us: local(): other = [lax.ppermute(b, 'dp', SWAP) for b in blocks]]
    all_to_all x0 -> x1, waiting for transfers between devices: none -> 17.1 us  [local(): lax.all_to_all(sent, 'dp', 0, 0, axis_index_groups=CHIP_GROUPS, tiled=True)]
    all_to_all x0 -> x1, starting transfers between devices: none -> 16.3 us  [local(): lax.all_to_all(sent, 'dp', 0, 0, axis_index_groups=CHIP_GROUPS, tiled=True)]
  transfers between devices with their start and end apart: 2 -> 12, of which waited for: 2 -> 8; matrix products, arithmetic and copies ran while one was open for 0% -> 0% of each run, Pallas kernels for 0% -> 0%
where the time goes in v1:
time: 362 us
  Pallas kernels  261 us (72%)
  waiting for transfers between devices  44 us (12%)
  starting transfers between devices  34.8 us (10%)
  blocking collectives  14.8 us (4%)
  local copies, waits for them, and re-layouts  4.56 us (1%)
    pallas_call x1, Pallas kernels, join(): pl.pallas_call(join_kernel, out_shape=jax.ShapeDtypeStruct((N_DP, 4, 32,...  256 us
    all_to_all x1, waiting for transfers between devices, local(): lax.all_to_all(sent, 'dp', 0, 0, axis_index_groups=CHIP_GROUPS, tiled=True)  17.1 us
    ppermute x3, waiting for transfers between devices, local(): lax.ppermute(block, 'dp', ring(s, 1))  16.9 us
    all_to_all x1, starting transfers between devices, local(): lax.all_to_all(sent, 'dp', 0, 0, axis_index_groups=CHIP_GROUPS, tiled=True)  16.3 us
    all_to_all x1, blocking collectives, local(): lax.all_to_all(jnp.broadcast_to(row[None], (ZN, HALF, TILE)), 'dp', 0, 0,...  14.8 us
    ppermute x4, starting transfers between devices, local(): other = [lax.ppermute(b, 'dp', SWAP) for b in blocks]  9.84 us
  transfers between devices with their start and end apart: 12, of which 8 were waited for; matrix products, arithmetic and copies ran while one was open for 0% of the time, Pallas kernels for 0%

profile of v1, /device:TPU:1, one launch (start us, length us, event | category | flops | bytes accessed | tf_op | source)
XLA Modules:
  0.0 361.8 jit_solution(7954271470352683416)
XLA Ops:
  0.0 0.9 dynamic-slice_reduce_fusion.1.ids_ref
  0.9 1.6 copy-done.1
  2.5 1.0 copy-done.2
  3.5 3.5 own_tiles.1
  7.0 16.3 %all-to-all-start = ((f32[128,8,128]{2,1,0:T(8,128)}), f32[128,8,128]{2,1,0:T(8,128)S(1)}, u32[]{:S(2)}, u32[]{:S(2)}) async-start(f32[128,8,128]{2,1,0:T(8,128)} %own_tiles.1), calls=%async_computation | async-start | bytes 1048576 | tf_op jit(solution)/shard_map/all_to_all | solution.py:149
  24.5 17.1 %all-to-all-done = f32[128,8,128]{2,1,0:T(8,128)S(1)} async-done(((f32[128,8,128]{2,1,0:T(8,128)}), f32[128,8,128]{2,1,0:T(8,128)S(1)}, u32[]{:S(2)}, u32[]{:S(2)}) %all-to-all-start) | async-done | bytes 524320 | tf_op jit(solution)/shard_map/all_to_all | solution.py:149
  41.6 1.3 fusion
  43.0 3.4 collective-permute-start
  46.4 0.9 collective-permute-done
  47.4 14.8 %all_to_all.10.p0 = bf16[8,128,128]{2,1,0:T(8,128)(2,1)S(1)} all-to-all(bf16[8,128,128]{2,1,0:T(8,128)(2,1)S(1)} %broadcast_in_dim.7), channel_id=1, replica_groups={{0,32,64,96,128,160,192,224},{1,33,65,97,129,161,193,225},{2,34,66,98,1..., dimensions={0} | all-to-all | bytes 524288 | tf_op jit(solution)/shard_map/all_to_all | solution.py:161
  62.1 2.7 collective-permute-start.2
  64.9 4.3 %collective-permute-done.3.p3 = bf16[8,128,128]{2,1,0:T(8,128)(2,1)S(1)} collective-permute-done((bf16[8,128,128]{2,1,0:T(8,128)(2,1)S(1)}, bf16[8,128,128]{2,1,0:T(8,128)(2,1)S(1)}, u32[]{:S(2)}, u32[]{:S(2)}) %collective-permute-start.3) | collective-permute-done | bytes 262176 | tf_op jit(solution)/shard_map/ppermute | solution.py:167
  69.2 1.1 collective-permute-done.2.p2
  70.2 1.8 collective-permute-done.1.p1
  72.0 1.9 by_rows.1.refs_0_
  74.0 2.4 collective-permute-start.5
  76.5 2.1 collective-permute-start.7
  78.6 10.9 %collective-permute-done.6.refs_3_ = bf16[128,32,128]{2,1,0:T(8,128)(2,1)S(1)} collective-permute-done((bf16[128,32,128]{2,1,0:T(8,128)(2,1)S(1)}, bf16[128,32,128]{2,1,0:T(8,128)(2,1)S(1)}, u32[]{:S(2)}, u32[]{:S(2)}) %collective-permute-start.6) | collective-permute-done | bytes 1048608 | tf_op jit(solution)/shard_map/ppermute | solution.py:169
  89.5 2.5 collective-permute-start.10
  92.0 6.0 %collective-permute-done.5.refs_2_ = bf16[128,32,128]{2,1,0:T(8,128)(2,1)S(1)} collective-permute-done((bf16[128,32,128]{2,1,0:T(8,128)(2,1)S(1)}, bf16[128,32,128]{2,1,0:T(8,128)(2,1)S(1)}, u32[]{:S(2)}, u32[]{:S(2)}) %collective-permute-start.5) | collective-permute-done | bytes 1048608 | tf_op jit(solution)/shard_map/ppermute | solution.py:169
  97.9 3.2 collective-permute-start.9
  101.2 2.0 collective-permute-start.8
  103.8 2.0 collective-permute-done.8.refs_5_
  105.8 256.0 %join.1 = bf16[256,4,32,128]{3,2,1,0:T(8,128)(2,1)} custom-call(s32[16]{0:T(128)} %stack.56.place_ref, bf16[128,32,128]{2,1,0:T(8,128)(2,1)} %copy-done, bf16[128,32,128]{2,1,0:T(8,128)(2,1)} %collective-permute-done.4.refs_1_, bf16[128,32,128]{2,1,0:T(8,128)(2,1)} %copy-done.4, bf16[128,32,128]{2,1,0:T(8,128)(2,1)} %copy-done.3, ...), custom_call_target="tpu_custom_call" | custom-call | tf_op jit(solution)/shard_map/join/pallas_call | solution.py:132
  (25 shorter events, 2.0 us)
Async XLA Ops:
  0.9 1.6 copy-start.1
  2.5 1.0 copy-start.2
  7.0 34.7 %all-to-all-start = ((f32[128,8,128]{2,1,0:T(8,128)}), f32[128,8,128]{2,1,0:T(8,128)S(1)}, u32[]{:S(2)}, u32[]{:S(2)}) async-start(f32[128,8,128]{2,1,0:T(8,128)} %own_tiles.1), calls=%async_computation | async-start | bytes 1048576 | tf_op jit(solution)/shard_map/all_to_all | solution.py:149
  43.0 4.3 %collective-permute-start = (f32[128,128]{1,0:T(8,128)S(1)}, f32[128,128]{1,0:T(8,128)S(1)}, u32[]{:S(2)}, u32[]{:S(2)}) collective-permute-start(f32[128,128]{1,0:T(8,128)S(1)} %dynamic-slice_bitcast_fusion), channel_id=1, source_target_pairs={{0,1},{1,0},{2,3},{3,2},{4,5},{5,4},{6,7},{7,6},{8,9},{9,8},{10,11... | collective-permute-start | bytes 196616 | tf_op jit(solution)/shard_map/ppermute | solution.py:159
  62.1 7.0 %collective-permute-start.3 = (bf16[8,128,128]{2,1,0:T(8,128)(2,1)S(1)}, bf16[8,128,128]{2,1,0:T(8,128)(2,1)S(1)}, u32[]{:S(2)}, u32[]{:S(2)}) collective-permute-start(bf16[8,128,128]{2,1,0:T(8,128)(2,1)S(1)} %all_to_all.10.p0), channel_id=1, source_target_pairs={{0,16},{1,5},{2,18},{3,7},{4,20},{5,1},{6,22},{7,3},{8,24},{9,13},... | collective-permute-start | bytes 786440 | tf_op jit(solution)/shard_map/ppermute | solution.py:167
  62.1 8.1 %collective-permute-start.2 = (bf16[8,128,128]{2,1,0:T(8,128)(2,1)S(1)}, bf16[8,128,128]{2,1,0:T(8,128)(2,1)S(1)}, u32[]{:S(2)}, u32[]{:S(2)}) collective-permute-start(bf16[8,128,128]{2,1,0:T(8,128)(2,1)S(1)} %all_to_all.10.p0), channel_id=1, source_target_pairs={{0,24},{1,7},{2,26},{3,1},{4,28},{5,3},{6,30},{7,5},{8,0},{9,15},{... | collective-permute-start | bytes 786440 | tf_op jit(solution)/shard_map/ppermute | solution.py:167
  64.8 7.1 %collective-permute-start.1 = (bf16[8,128,128]{2,1,0:T(8,128)(2,1)S(1)}, bf16[8,128,128]{2,1,0:T(8,128)(2,1)S(1)}, u32[]{:S(2)}, u32[]{:S(2)}) collective-permute-start(bf16[8,128,128]{2,1,0:T(8,128)(2,1)S(1)} %all_to_all.10.p0), channel_id=1, source_target_pairs={{0,8},{1,3},{2,10},{3,5},{4,12},{5,7},{6,14},{7,1},{8,16},{9,11},{... | collective-permute-start | bytes 786440 | tf_op jit(solution)/shard_map/ppermute | solution.py:167
  73.9 31.9 %copy-start = (bf16[128,32,128]{2,1,0:T(8,128)(2,1)}, bf16[128,32,128]{2,1,0:T(8,128)(2,1)S(1)}, u32[]{:S(2)}) copy-start(bf16[128,32,128]{2,1,0:T(8,128)(2,1)S(1)} %by_rows.1.refs_0_) | copy-start | bytes 3145732
  73.9 15.6 %collective-permute-start.6 = (bf16[128,32,128]{2,1,0:T(8,128)(2,1)S(1)}, bf16[128,32,128]{2,1,0:T(8,128)(2,1)S(1)}, u32[]{:S(2)}, u32[]{:S(2)}) collective-permute-start(bf16[128,32,128]{2,1,0:T(8,128)(2,1)S(1)} %by_rows.1.refs_0_), channel_id=1, source_target_pairs={{0,4},{1,17},{2,6},{3,19},{4,0},{5,21},{6,2},{7,23},{8,12},{9,25},... | collective-permute-start | bytes 3145736 | tf_op jit(solution)/shard_map/ppermute | solution.py:169
  74.0 23.9 %collective-permute-start.5 = (bf16[128,32,128]{2,1,0:T(8,128)(2,1)S(1)}, bf16[128,32,128]{2,1,0:T(8,128)(2,1)S(1)}, u32[]{:S(2)}, u32[]{:S(2)}) collective-permute-start(bf16[128,32,128]{2,1,0:T(8,128)(2,1)S(1)} %by_rows.1.refs_0_), channel_id=1, source_target_pairs={{0,6},{1,25},{2,0},{3,27},{4,2},{5,29},{6,4},{7,31},{8,14},{9,1},{... | collective-permute-start | bytes 3145736 | tf_op jit(solution)/shard_map/ppermute | solution.py:169
  76.5 24.7 %collective-permute-start.4 = (bf16[128,32,128]{2,1,0:T(8,128)(2,1)S(1)}, bf16[128,32,128]{2,1,0:T(8,128)(2,1)}, u32[]{:S(2)}, u32[]{:S(2)}) collective-permute-start(bf16[128,32,128]{2,1,0:T(8,128)(2,1)S(1)} %by_rows.1.refs_0_), channel_id=1, source_target_pairs={{0,2},{1,9},{2,4},{3,11},{4,6},{5,13},{6,0},{7,15},{8,10},{9,17},{... | collective-permute-start | bytes 3145736 | tf_op jit(solution)/shard_map/ppermute | solution.py:169
  76.5 27.3 %collective-permute-start.7 = (bf16[128,32,128]{2,1,0:T(8,128)(2,1)S(1)}, bf16[128,32,128]{2,1,0:T(8,128)(2,1)}, u32[]{:S(2)}, u32[]{:S(2)}) collective-permute-start(bf16[128,32,128]{2,1,0:T(8,128)(2,1)S(1)} %by_rows.1.refs_0_), channel_id=1, source_target_pairs={{0,1},{1,0},{2,3},{3,2},{4,5},{5,4},{6,7},{7,6},{8,9},{9,8},{10,11... | collective-permute-start | bytes 3145736 | tf_op jit(solution)/shard_map/ppermute | solution.py:170
  89.5 16.3 %copy-start.3 = (bf16[128,32,128]{2,1,0:T(8,128)(2,1)}, bf16[128,32,128]{2,1,0:T(8,128)(2,1)S(1)}, u32[]{:S(2)}) copy-start(bf16[128,32,128]{2,1,0:T(8,128)(2,1)S(1)} %collective-permute-done.6.refs_3_) | copy-start | bytes 3145732
  89.5 14.3 %collective-permute-start.10 = (bf16[128,32,128]{2,1,0:T(8,128)(2,1)S(1)}, bf16[128,32,128]{2,1,0:T(8,128)(2,1)}, u32[]{:S(2)}, u32[]{:S(2)}) collective-permute-start(bf16[128,32,128]{2,1,0:T(8,128)(2,1)S(1)} %collective-permute-done.6.refs_3_), channel_id=1, source_target_pairs={{0,1},{1,0},{2,3},{3,2},{4,5},{5,4},{6,7},{7,6},{8,9},{9,8},{10,11... | collective-permute-start | bytes 3145736 | tf_op jit(solution)/shard_map/ppermute | solution.py:170
  97.9 7.9 %copy-start.4 = (bf16[128,32,128]{2,1,0:T(8,128)(2,1)}, bf16[128,32,128]{2,1,0:T(8,128)(2,1)S(1)}, u32[]{:S(2)}) copy-start(bf16[128,32,128]{2,1,0:T(8,128)(2,1)S(1)} %collective-permute-done.5.refs_2_) | copy-start | bytes 3145732
  97.9 5.8 %collective-permute-start.9 = (bf16[128,32,128]{2,1,0:T(8,128)(2,1)S(1)}, bf16[128,32,128]{2,1,0:T(8,128)(2,1)}, u32[]{:S(2)}, u32[]{:S(2)}) collective-permute-start(bf16[128,32,128]{2,1,0:T(8,128)(2,1)S(1)} %collective-permute-done.5.refs_2_), channel_id=1, source_target_pairs={{0,1},{1,0},{2,3},{3,2},{4,5},{5,4},{6,7},{7,6},{8,9},{9,8},{10,11... | collective-permute-start | bytes 3145736 | tf_op jit(solution)/shard_map/ppermute | solution.py:170
  101.2 4.7 %collective-permute-start.8 = (bf16[128,32,128]{2,1,0:T(8,128)(2,1)}, bf16[128,32,128]{2,1,0:T(8,128)(2,1)}, u32[]{:S(2)}, u32[]{:S(2)}) collective-permute-start(bf16[128,32,128]{2,1,0:T(8,128)(2,1)} %collective-permute-done.4.refs_1_), channel_id=1, source_target_pairs={{0,1},{1,0},{2,3},{3,2},{4,5},{5,4},{6,7},{7,6},{8,9},{9,8},{10,11... | collective-permute-start | bytes 3145736 | tf_op jit(solution)/shard_map/ppermute | solution.py:170

commit v2 on v1

--- a/solution.py
+++ b/solution.py
@@ -13,6 +13,7 @@
 CHIPS = 128
 HALF = 128
 HALF_TILES = 512
+JOIN = 16
 VMEM_LIMIT = 48 * 1024 * 1024
 
 
@@ -114,27 +115,26 @@
 
 
 def join_kernel(place_ref, *refs):
-    pieces, out_ref, sems = refs[:8], refs[8], refs[9]
-    copies = []
-    for i, piece in enumerate(pieces):
-        half = place_ref[8 + i]
-        slot = place_ref[i]
-        copies.append(pltpu.make_async_copy(
-            piece, out_ref.at[pl.ds(pl.multiple_of(half * HALF, HALF), HALF), slot], sems.at[i]
-        ))
-    for copy in copies:
-        copy.start()
-    for copy in copies:
-        copy.wait()
+    pieces, out_ref = refs[:8], refs[8]
+    rows = pl.ds(pl.program_id(1) * JOIN, JOIN)
+    for g in range(2):
+        @pl.when(pl.program_id(0) == g)
+        def _():
+            for j in range(4 * g, 4 * g + 4):
+                out_ref[0, :, place_ref[j]] = pieces[j][rows]
 
 
 def join(place, pieces):
     return pl.pallas_call(
         join_kernel,
-        out_shape=jax.ShapeDtypeStruct((N_DP, 4, 32, TILE), jnp.bfloat16),
-        in_specs=[pl.BlockSpec(memory_space=pltpu.SMEM)] + [pl.BlockSpec(memory_space=pl.ANY)] * 8,
-        out_specs=pl.BlockSpec(memory_space=pl.ANY),
-        scratch_shapes=[pltpu.SemaphoreType.DMA((8,))],
+        grid_spec=pltpu.PrefetchScalarGridSpec(
+            num_scalar_prefetch=1,
+            grid=(2, HALF // JOIN),
+            in_specs=[pl.BlockSpec(memory_space=pltpu.VMEM)] * 8,
+            out_specs=pl.BlockSpec((1, JOIN, 4, 32, TILE), lambda g, i, place: (place[8 + g], i, 0, 0, 0)),
+        ),
+        out_shape=jax.ShapeDtypeStruct((2, HALF, 4, 32, TILE), jnp.bfloat16),
+        compiler_params=pltpu.CompilerParams(vmem_limit_bytes=VMEM_LIMIT),
         name="join",
     )(place, *pieces)
 
@@ -169,7 +169,7 @@
     blocks = [block] + [lax.ppermute(block, "dp", ring(s, 1)) for s in steps[1:]]
     other = [lax.ppermute(b, "dp", SWAP) for b in blocks]
     place = jnp.stack(
-        [(at1 - s) % 4 for s in steps] + [(at0 - s) % 4 for s in steps] + [core] * 4 + [1 - core] * 4
+        [(at1 - s) % 4 for s in steps] + [(at0 - s) % 4 for s in steps] + [core, 1 - core]
     )
     return join(place, blocks + other).reshape(N_DP, TILE, TILE)
 

time: 362 us -> 116 us (0.32)
  Pallas kernels: 261 us -> 15.3 us
    pallas_call x1, Pallas kernels: 256 us -> 9.92 us  [join(): pl.pallas_call(join_kernel, grid_spec=pltpu.PrefetchScalarGridSpec(num_sc...]
  transfers between devices with their start and end apart: 12 -> 12, of which waited for: 8 -> 9; matrix products, arithmetic and copies ran while one was open for 0% -> 1% of each run, Pallas kernels for 0% -> 0%
where the time goes in v2:
time: 116 us
  waiting for transfers between devices  44.5 us (38%)
  starting transfers between devices  34.8 us (30%)
  Pallas kernels  15.3 us (13%)
  blocking collectives  14.8 us (13%)
  local copies, waits for them, and re-layouts  4.05 us (3%)
  matrix products  1.33 us (1%)
    all_to_all x1, waiting for transfers between devices, local(): lax.all_to_all(sent, 'dp', 0, 0, axis_index_groups=CHIP_GROUPS, tiled=True)  17.1 us
    ppermute x3, waiting for transfers between devices, local(): lax.ppermute(block, 'dp', ring(s, 1))  16.9 us
    all_to_all x1, starting transfers between devices, local(): lax.all_to_all(sent, 'dp', 0, 0, axis_index_groups=CHIP_GROUPS, tiled=True)  16.3 us
    all_to_all x1, blocking collectives, local(): lax.all_to_all(jnp.broadcast_to(row[None], (ZN, HALF, TILE)), 'dp', 0, 0,...  14.8 us
    pallas_call x1, Pallas kernels, join(): pl.pallas_call(join_kernel, grid_spec=pltpu.PrefetchScalarGridSpec(num_sc...  9.92 us
    ppermute x4, starting transfers between devices, local(): other = [lax.ppermute(b, 'dp', SWAP) for b in blocks]  9.84 us
    ppermute x3, waiting for transfers between devices, local(): pieces = [rows] + [lax.ppermute(rows, 'dp', ring(s, 0)) for s in steps[1:]]  7.06 us
    pallas_call x1, Pallas kernels, own_tiles(): pl.pallas_call(tiles_kernel, out_shape=jax.ShapeDtypeStruct((CHIPS, KEPT,...  3.48 us
  transfers between devices with their start and end apart: 12, of which 9 were waited for; matrix products, arithmetic and copies ran while one was open for 1% of the time, Pallas kernels for 0%

profile of v2, /device:TPU:1, one launch (start us, length us, event | category | flops | bytes accessed | tf_op | source)
XLA Modules:
  0.0 115.7 jit_solution(6572747789733661005)
XLA Ops:
  0.0 0.9 dynamic-slice_reduce_fusion.1.ids_ref
  0.9 1.6 %copy-done = bf16[128,8192]{1,0:T(8,128)(2,1)S(1)} copy-done((bf16[128,8192]{1,0:T(8,128)(2,1)S(1)}, bf16[128,8192]{1,0:T(8,128)(2,1)}, u32[]{:S(2)}) %copy-start) | copy-done | bytes 2097176
  2.5 1.0 copy-done.1
  3.5 3.5 %own_tiles.1 = f32[128,8,128]{2,1,0:T(8,128)} custom-call(s32[8]{0:T(128)S(1)} %dynamic-slice_reduce_fusion.1.ids_ref, bf16[128,8192]{1,0:T(8,128)(2,1)S(1)} %copy-done, bf16[128,2048]{1,0:T(8,128)(2,1)S(1)} %copy-done.1), custom_call_target="tpu_custom_call" | custom-call | tf_op jit(solution)/shard_map/own_tiles/pallas_call | solution.py:70
  7.0 16.3 %all-to-all-start = ((f32[128,8,128]{2,1,0:T(8,128)}), f32[128,8,128]{2,1,0:T(8,128)S(1)}, u32[]{:S(2)}, u32[]{:S(2)}) async-start(f32[128,8,128]{2,1,0:T(8,128)} %own_tiles.1), calls=%async_computation | async-start | bytes 1048576 | tf_op jit(solution)/shard_map/all_to_all | solution.py:149
  24.5 17.1 %all-to-all-done = f32[128,8,128]{2,1,0:T(8,128)S(1)} async-done(((f32[128,8,128]{2,1,0:T(8,128)}), f32[128,8,128]{2,1,0:T(8,128)S(1)}, u32[]{:S(2)}, u32[]{:S(2)}) %all-to-all-start) | async-done | bytes 524320 | tf_op jit(solution)/shard_map/all_to_all | solution.py:149
  41.7 1.3 %fusion = f32[2,128,128]{2,1,0:T(8,128)S(1)} fusion(f32[128,8,128]{2,1,0:T(8,128)S(1)} %all-to-all-done, s32[1024]{0:T(1024)S(1)} %eq.45, s32[2,128]{1,0:T(2,128)} %bitcast.25), kind=kOutput, calls=%fused_computation | convolution fusion | flops 402915328 | bytes 660480 | tf_op jit(solution)/shard_map/dot_general | solution.py:155
  43.0 3.4 %collective-permute-start = (f32[128,128]{1,0:T(8,128)S(1)}, f32[128,128]{1,0:T(8,128)S(1)}, u32[]{:S(2)}, u32[]{:S(2)}) collective-permute-start(f32[128,128]{1,0:T(8,128)S(1)} %dynamic-slice_bitcast_fusion), channel_id=1, source_target_pairs={{0,1},{1,0},{2,3},{3,2},{4,5},{5,4},{6,7},{7,6},{8,9},{9,8},{10,11... | collective-permute-start | bytes 196616 | tf_op jit(solution)/shard_map/ppermute | solution.py:159
  46.4 0.9 collective-permute-done
  47.4 14.8 %all_to_all.10.p0 = bf16[8,128,128]{2,1,0:T(8,128)(2,1)S(1)} all-to-all(bf16[8,128,128]{2,1,0:T(8,128)(2,1)S(1)} %broadcast_in_dim.7), channel_id=1, replica_groups={{0,32,64,96,128,160,192,224},{1,33,65,97,129,161,193,225},{2,34,66,98,1..., dimensions={0} | all-to-all | bytes 524288 | tf_op jit(solution)/shard_map/all_to_all | solution.py:161
  62.1 2.7 %collective-permute-start.2 = (bf16[8,128,128]{2,1,0:T(8,128)(2,1)S(1)}, bf16[8,128,128]{2,1,0:T(8,128)(2,1)S(1)}, u32[]{:S(2)}, u32[]{:S(2)}) collective-permute-start(bf16[8,128,128]{2,1,0:T(8,128)(2,1)S(1)} %all_to_all.10.p0), channel_id=1, source_target_pairs={{0,24},{1,7},{2,26},{3,1},{4,28},{5,3},{6,30},{7,5},{8,0},{9,15},{... | collective-permute-start | bytes 786440 | tf_op jit(solution)/shard_map/ppermute | solution.py:167
  64.9 4.3 %collective-permute-done.3.p3 = bf16[8,128,128]{2,1,0:T(8,128)(2,1)S(1)} collective-permute-done((bf16[8,128,128]{2,1,0:T(8,128)(2,1)S(1)}, bf16[8,128,128]{2,1,0:T(8,128)(2,1)S(1)}, u32[]{:S(2)}, u32[]{:S(2)}) %collective-permute-start.3) | collective-permute-done | bytes 262176 | tf_op jit(solution)/shard_map/ppermute | solution.py:167
  69.2 1.1 collective-permute-done.2.p2
  70.2 1.8 %collective-permute-done.1.p1 = bf16[8,128,128]{2,1,0:T(8,128)(2,1)S(1)} collective-permute-done((bf16[8,128,128]{2,1,0:T(8,128)(2,1)S(1)}, bf16[8,128,128]{2,1,0:T(8,128)(2,1)S(1)}, u32[]{:S(2)}, u32[]{:S(2)}) %collective-permute-start.1) | collective-permute-done | bytes 262176 | tf_op jit(solution)/shard_map/ppermute | solution.py:167
  72.0 1.9 %by_rows.1.refs_0_ = bf16[128,32,128]{2,1,0:T(8,128)(2,1)S(1)} custom-call(s32[4]{0:T(128)S(1)} %pad_add_fusion.place_ref, bf16[8,128,128]{2,1,0:T(8,128)(2,1)S(1)} %all_to_all.10.p0, bf16[8,128,128]{2,1,0:T(8,128)(2,1)S(1)} %collective-permute-done.1.p1, bf16[8,128,128]{2,1,0:T(8,128)(2,1)S(1)} %collective-permute-done.2.p2, ...), custom_call_target="tpu_custom_call" | custom-call | tf_op jit(solution)/shard_map/by_rows/pallas_call | solution.py:106
  74.0 2.4 %collective-permute-start.5 = (bf16[128,32,128]{2,1,0:T(8,128)(2,1)S(1)}, bf16[128,32,128]{2,1,0:T(8,128)(2,1)S(1)}, u32[]{:S(2)}, u32[]{:S(2)}) collective-permute-start(bf16[128,32,128]{2,1,0:T(8,128)(2,1)S(1)} %by_rows.1.refs_0_), channel_id=1, source_target_pairs={{0,6},{1,25},{2,0},{3,27},{4,2},{5,29},{6,4},{7,31},{8,14},{9,1},{... | collective-permute-start | bytes 3145736 | tf_op jit(solution)/shard_map/ppermute | solution.py:169
  76.5 2.1 %collective-permute-start.7 = (bf16[128,32,128]{2,1,0:T(8,128)(2,1)S(1)}, bf16[128,32,128]{2,1,0:T(8,128)(2,1)}, u32[]{:S(2)}, u32[]{:S(2)}) collective-permute-start(bf16[128,32,128]{2,1,0:T(8,128)(2,1)S(1)} %by_rows.1.refs_0_), channel_id=1, source_target_pairs={{0,1},{1,0},{2,3},{3,2},{4,5},{5,4},{6,7},{7,6},{8,9},{9,8},{10,11... | collective-permute-start | bytes 3145736 | tf_op jit(solution)/shard_map/ppermute | solution.py:170
  78.6 10.9 %collective-permute-done.6.refs_3_ = bf16[128,32,128]{2,1,0:T(8,128)(2,1)S(1)} collective-permute-done((bf16[128,32,128]{2,1,0:T(8,128)(2,1)S(1)}, bf16[128,32,128]{2,1,0:T(8,128)(2,1)S(1)}, u32[]{:S(2)}, u32[]{:S(2)}) %collective-permute-start.6) | collective-permute-done | bytes 1048608 | tf_op jit(solution)/shard_map/ppermute | solution.py:169
  89.5 2.5 %collective-permute-start.10 = (bf16[128,32,128]{2,1,0:T(8,128)(2,1)S(1)}, bf16[128,32,128]{2,1,0:T(8,128)(2,1)}, u32[]{:S(2)}, u32[]{:S(2)}) collective-permute-start(bf16[128,32,128]{2,1,0:T(8,128)(2,1)S(1)} %collective-permute-done.6.refs_3_), channel_id=1, source_target_pairs={{0,1},{1,0},{2,3},{3,2},{4,5},{5,4},{6,7},{7,6},{8,9},{9,8},{10,11... | collective-permute-start | bytes 3145736 | tf_op jit(solution)/shard_map/ppermute | solution.py:170
  91.9 6.0 %collective-permute-done.5.refs_2_ = bf16[128,32,128]{2,1,0:T(8,128)(2,1)S(1)} collective-permute-done((bf16[128,32,128]{2,1,0:T(8,128)(2,1)S(1)}, bf16[128,32,128]{2,1,0:T(8,128)(2,1)S(1)}, u32[]{:S(2)}, u32[]{:S(2)}) %collective-permute-start.5) | collective-permute-done | bytes 1048608 | tf_op jit(solution)/shard_map/ppermute | solution.py:169
  97.9 3.2 %collective-permute-start.9 = (bf16[128,32,128]{2,1,0:T(8,128)(2,1)S(1)}, bf16[128,32,128]{2,1,0:T(8,128)(2,1)}, u32[]{:S(2)}, u32[]{:S(2)}) collective-permute-start(bf16[128,32,128]{2,1,0:T(8,128)(2,1)S(1)} %collective-permute-done.5.refs_2_), channel_id=1, source_target_pairs={{0,1},{1,0},{2,3},{3,2},{4,5},{5,4},{6,7},{7,6},{8,9},{9,8},{10,11... | collective-permute-start | bytes 3145736 | tf_op jit(solution)/shard_map/ppermute | solution.py:170
  101.2 2.0 %collective-permute-start.8 = (bf16[128,32,128]{2,1,0:T(8,128)(2,1)}, bf16[128,32,128]{2,1,0:T(8,128)(2,1)}, u32[]{:S(2)}, u32[]{:S(2)}) collective-permute-start(bf16[128,32,128]{2,1,0:T(8,128)(2,1)} %collective-permute-done.4.refs_1_), channel_id=1, source_target_pairs={{0,1},{1,0},{2,3},{3,2},{4,5},{5,4},{6,7},{7,6},{8,9},{9,8},{10,11... | collective-permute-start | bytes 3145736 | tf_op jit(solution)/shard_map/ppermute | solution.py:170
  103.6 2.2 %collective-permute-done.8.refs_5_ = bf16[128,32,128]{2,1,0:T(8,128)(2,1)} collective-permute-done((bf16[128,32,128]{2,1,0:T(8,128)(2,1)}, bf16[128,32,128]{2,1,0:T(8,128)(2,1)}, u32[]{:S(2)}, u32[]{:S(2)}) %collective-permute-start.8) | collective-permute-done | bytes 1048608 | tf_op jit(solution)/shard_map/ppermute | solution.py:170
  105.8 9.9 %join.1 = bf16[2,128,4,32,128]{4,3,2,1,0:T(8,128)(2,1)} custom-call(s32[10]{0:T(128)S(1)} %stack.50.place_ref, bf16[128,32,128]{2,1,0:T(8,128)(2,1)S(1)} %by_rows.1.refs_0_, bf16[128,32,128]{2,1,0:T(8,128)(2,1)} %collective-permute-done.4.refs_1_, bf16[128,32,128]{2,1,0:T(8,128)(2,1)S(1)} %collective-permute-done.5.refs_2_, ...), custom_call_target="tpu_custom_call" | custom-call | tf_op jit(solution)/shard_map/join/pallas_call | solution.py:128
  (19 shorter events, 1.7 us)
Async XLA Ops:
  0.9 1.6 %copy-start = (bf16[128,8192]{1,0:T(8,128)(2,1)S(1)}, bf16[128,8192]{1,0:T(8,128)(2,1)}, u32[]{:S(2)}) copy-start(bf16[128,8192]{1,0:T(8,128)(2,1)} %act_ref.1) | copy-start | bytes 6291460
  2.5 1.0 copy-start.1
  7.0 34.7 %all-to-all-start = ((f32[128,8,128]{2,1,0:T(8,128)}), f32[128,8,128]{2,1,0:T(8,128)S(1)}, u32[]{:S(2)}, u32[]{:S(2)}) async-start(f32[128,8,128]{2,1,0:T(8,128)} %own_tiles.1), calls=%async_computation | async-start | bytes 1048576 | tf_op jit(solution)/shard_map/all_to_all | solution.py:149
  43.0 4.3 %collective-permute-start = (f32[128,128]{1,0:T(8,128)S(1)}, f32[128,128]{1,0:T(8,128)S(1)}, u32[]{:S(2)}, u32[]{:S(2)}) collective-permute-start(f32[128,128]{1,0:T(8,128)S(1)} %dynamic-slice_bitcast_fusion), channel_id=1, source_target_pairs={{0,1},{1,0},{2,3},{3,2},{4,5},{5,4},{6,7},{7,6},{8,9},{9,8},{10,11... | collective-permute-start | bytes 196616 | tf_op jit(solution)/shard_map/ppermute | solution.py:159
  62.1 7.0 %collective-permute-start.3 = (bf16[8,128,128]{2,1,0:T(8,128)(2,1)S(1)}, bf16[8,128,128]{2,1,0:T(8,128)(2,1)S(1)}, u32[]{:S(2)}, u32[]{:S(2)}) collective-permute-start(bf16[8,128,128]{2,1,0:T(8,128)(2,1)S(1)} %all_to_all.10.p0), channel_id=1, source_target_pairs={{0,16},{1,5},{2,18},{3,7},{4,20},{5,1},{6,22},{7,3},{8,24},{9,13},... | collective-permute-start | bytes 786440 | tf_op jit(solution)/shard_map/ppermute | solution.py:167
  62.1 8.1 %collective-permute-start.2 = (bf16[8,128,128]{2,1,0:T(8,128)(2,1)S(1)}, bf16[8,128,128]{2,1,0:T(8,128)(2,1)S(1)}, u32[]{:S(2)}, u32[]{:S(2)}) collective-permute-start(bf16[8,128,128]{2,1,0:T(8,128)(2,1)S(1)} %all_to_all.10.p0), channel_id=1, source_target_pairs={{0,24},{1,7},{2,26},{3,1},{4,28},{5,3},{6,30},{7,5},{8,0},{9,15},{... | collective-permute-start | bytes 786440 | tf_op jit(solution)/shard_map/ppermute | solution.py:167
  64.8 7.1 %collective-permute-start.1 = (bf16[8,128,128]{2,1,0:T(8,128)(2,1)S(1)}, bf16[8,128,128]{2,1,0:T(8,128)(2,1)S(1)}, u32[]{:S(2)}, u32[]{:S(2)}) collective-permute-start(bf16[8,128,128]{2,1,0:T(8,128)(2,1)S(1)} %all_to_all.10.p0), channel_id=1, source_target_pairs={{0,8},{1,3},{2,10},{3,5},{4,12},{5,7},{6,14},{7,1},{8,16},{9,11},{... | collective-permute-start | bytes 786440 | tf_op jit(solution)/shard_map/ppermute | solution.py:167
  73.9 15.6 %collective-permute-start.6 = (bf16[128,32,128]{2,1,0:T(8,128)(2,1)S(1)}, bf16[128,32,128]{2,1,0:T(8,128)(2,1)S(1)}, u32[]{:S(2)}, u32[]{:S(2)}) collective-permute-start(bf16[128,32,128]{2,1,0:T(8,128)(2,1)S(1)} %by_rows.1.refs_0_), channel_id=1, source_target_pairs={{0,4},{1,17},{2,6},{3,19},{4,0},{5,21},{6,2},{7,23},{8,12},{9,25},... | collective-permute-start | bytes 3145736 | tf_op jit(solution)/shard_map/ppermute | solution.py:169
  74.0 23.9 %collective-permute-start.5 = (bf16[128,32,128]{2,1,0:T(8,128)(2,1)S(1)}, bf16[128,32,128]{2,1,0:T(8,128)(2,1)S(1)}, u32[]{:S(2)}, u32[]{:S(2)}) collective-permute-start(bf16[128,32,128]{2,1,0:T(8,128)(2,1)S(1)} %by_rows.1.refs_0_), channel_id=1, source_target_pairs={{0,6},{1,25},{2,0},{3,27},{4,2},{5,29},{6,4},{7,31},{8,14},{9,1},{... | collective-permute-start | bytes 3145736 | tf_op jit(solution)/shard_map/ppermute | solution.py:169
  76.5 24.7 %collective-permute-start.4 = (bf16[128,32,128]{2,1,0:T(8,128)(2,1)S(1)}, bf16[128,32,128]{2,1,0:T(8,128)(2,1)}, u32[]{:S(2)}, u32[]{:S(2)}) collective-permute-start(bf16[128,32,128]{2,1,0:T(8,128)(2,1)S(1)} %by_rows.1.refs_0_), channel_id=1, source_target_pairs={{0,2},{1,9},{2,4},{3,11},{4,6},{5,13},{6,0},{7,15},{8,10},{9,17},{... | collective-permute-start | bytes 3145736 | tf_op jit(solution)/shard_map/ppermute | solution.py:169
  76.5 26.8 %collective-permute-start.7 = (bf16[128,32,128]{2,1,0:T(8,128)(2,1)S(1)}, bf16[128,32,128]{2,1,0:T(8,128)(2,1)}, u32[]{:S(2)}, u32[]{:S(2)}) collective-permute-start(bf16[128,32,128]{2,1,0:T(8,128)(2,1)S(1)} %by_rows.1.refs_0_), channel_id=1, source_target_pairs={{0,1},{1,0},{2,3},{3,2},{4,5},{5,4},{6,7},{7,6},{8,9},{9,8},{10,11... | collective-permute-start | bytes 3145736 | tf_op jit(solution)/shard_map/ppermute | solution.py:170
  89.5 13.8 %collective-permute-start.10 = (bf16[128,32,128]{2,1,0:T(8,128)(2,1)S(1)}, bf16[128,32,128]{2,1,0:T(8,128)(2,1)}, u32[]{:S(2)}, u32[]{:S(2)}) collective-permute-start(bf16[128,32,128]{2,1,0:T(8,128)(2,1)S(1)} %collective-permute-done.6.refs_3_), channel_id=1, source_target_pairs={{0,1},{1,0},{2,3},{3,2},{4,5},{5,4},{6,7},{7,6},{8,9},{9,8},{10,11... | collective-permute-start | bytes 3145736 | tf_op jit(solution)/shard_map/ppermute | solution.py:170
  97.9 5.6 %collective-permute-start.9 = (bf16[128,32,128]{2,1,0:T(8,128)(2,1)S(1)}, bf16[128,32,128]{2,1,0:T(8,128)(2,1)}, u32[]{:S(2)}, u32[]{:S(2)}) collective-permute-start(bf16[128,32,128]{2,1,0:T(8,128)(2,1)S(1)} %collective-permute-done.5.refs_2_), channel_id=1, source_target_pairs={{0,1},{1,0},{2,3},{3,2},{4,5},{5,4},{6,7},{7,6},{8,9},{9,8},{10,11... | collective-permute-start | bytes 3145736 | tf_op jit(solution)/shard_map/ppermute | solution.py:170
  101.2 4.7 %collective-permute-start.8 = (bf16[128,32,128]{2,1,0:T(8,128)(2,1)}, bf16[128,32,128]{2,1,0:T(8,128)(2,1)}, u32[]{:S(2)}, u32[]{:S(2)}) collective-permute-start(bf16[128,32,128]{2,1,0:T(8,128)(2,1)} %collective-permute-done.4.refs_1_), channel_id=1, source_target_pairs={{0,1},{1,0},{2,3},{3,2},{4,5},{5,4},{6,7},{7,6},{8,9},{9,8},{10,11... | collective-permute-start | bytes 3145736 | tf_op jit(solution)/shard_map/ppermute | solution.py:170

commit v3 on v1

v3 whole, which is shorter than its diff:
```python
import functools

import jax
import jax.numpy as jnp
from jax import lax
from jax.experimental import pallas as pl
from jax.experimental.pallas import tpu as pltpu
from jax.sharding import PartitionSpec as P

TILE = 128
KEPT = 8
N_DP = 256
COLS = 16
ZN, YN, XN, CN = 8, 4, 4, 2
CHIPS = 128
HALF = 128
HALF_TILES = 512
MIB = 1024 * 1024
PART = 64
STEPS = (0, 1, 3, 2)


def dev(z, y, x, c):
    return ((z * YN + y) * XN + x) * CN + c


DEVS = [(z, y, x, c) for z in range(ZN) for y in range(YN) for x in range(XN) for c in range(CN)]
CHIP_GROUPS = [[dev(z, y, x, c) for x in range(XN) for y in range(YN) for z in range(ZN)] for c in range(CN)]
Z_GROUPS = [[dev(z, y, x, c) for z in range(ZN)] for y in range(YN) for x in range(XN) for c in range(CN)]
SWAP = [(d, d ^ 1) for d in range(N_DP)]


def ring(step, turn):
    pairs = []
    for z, y, x, c in DEVS:
        if (c + turn) % 2 == 0:
            pairs.append((dev(z, y, x, c), dev(z, (y + step) % YN, x, c)))
        else:
            pairs.append((dev(z, y, x, c), dev(z, y, (x + step) % XN, c)))
    return pairs


def spot():
    me = lax.axis_index("dp")
    core = me % CN
    x = (me // CN) % XN
    y = (me // (CN * XN)) % YN
    return core, jnp.where(core == 0, y, x), jnp.where(core == 0, x, y)


def tiles_kernel(kept_ref, act_ref, cot_ref, out_ref, lefts, rights, stage, sems):
    me = lax.axis_index("dp")
    copies = []
    for k in range(KEPT):
        tile = kept_ref[k, me]
        row = pl.multiple_of((tile // COLS) * TILE, TILE)
        col = pl.multiple_of((tile % COLS) * TILE, TILE)
        a = pltpu.make_async_copy(act_ref.at[:, pl.ds(row, TILE)], lefts.at[k], sems.at[k, 0])
        b = pltpu.make_async_copy(cot_ref.at[:, pl.ds(col, TILE)], rights.at[k], sems.at[k, 1])
        a.start()
        b.start()
        copies.append((a, b))
    for k in range(KEPT):
        a, b = copies[k]
        a.wait()
        b.wait()
        half = kept_ref[k, me] // HALF_TILES
        tile = lax.dot_general(
            lefts[k], rights[k], (((0,), (0,)), ((), ())), preferred_element_type=jnp.float32
        )
        for p in range(4):
            for q in range(4):
                there = jnp.where(half == 0, p * 32 + q * 8, q * 32 + p * 8) + k * TILE
                here = p * 32 + q * 8
                stage[pl.ds(pl.multiple_of(there, 8), 8), :] = tile[here:here + 8, :]
    for chip in range(CHIPS):
        out_ref[chip] = stage[pl.ds(chip, KEPT, stride=TILE), :]


def own_tiles(kept, activations, cotangent):
    return pl.pallas_call(
        tiles_kernel,
        out_shape=jax.ShapeDtypeStruct((CHIPS, KEPT, TILE), jnp.float32),
        in_specs=[
            pl.BlockSpec(memory_space=pltpu.SMEM),
            pl.BlockSpec(memory_space=pltpu.HBM),
            pl.BlockSpec(memory_space=pltpu.HBM),
        ],
        out_specs=pl.BlockSpec(memory_space=pltpu.VMEM),
        scratch_shapes=[
            pltpu.VMEM((KEPT, TILE, TILE), jnp.bfloat16),
            pltpu.VMEM((KEPT, TILE, TILE), jnp.bfloat16),
            pltpu.VMEM((KEPT * TILE, TILE), jnp.float32),
            pltpu.SemaphoreType.DMA((KEPT, 2)),
        ],
        compiler_params=pltpu.CompilerParams(vmem_limit_bytes=62 * MIB),
        name="own_tiles",
    )(kept, activations, cotangent)


def rows_kernel(p0, p1, p2, p3, a_ref, b_ref, wide):
    at = spot()[1]
    for step, piece in zip(STEPS, (p0, p1, p2, p3)):
        start = pl.multiple_of((at + 4 - step) % 4 * ZN * HALF, ZN * HALF)
        wide[pl.ds(start, ZN * HALF), :] = piece[...].astype(jnp.float32).reshape(ZN * HALF, TILE)

    for part, out_ref in enumerate((a_ref, b_ref)):
        def body(t, carry):
            rows = [wide[pl.ds(q * ZN * HALF + part * PART + t, ZN, stride=HALF), :] for q in range(4)]
            out_ref[t] = jnp.concatenate(rows, axis=0).astype(jnp.bfloat16)
            return carry

        lax.fori_loop(0, PART, body, 0, unroll=8)


def by_rows(pieces):
    return pl.pallas_call(
        rows_kernel,
        out_shape=[jax.ShapeDtypeStruct((PART, 4 * ZN, TILE), jnp.bfloat16)] * 2,
        in_specs=[pl.BlockSpec(memory_space=pltpu.VMEM)] * 4,
        out_specs=[pl.BlockSpec(memory_space=pltpu.VMEM)] * 2,
        scratch_shapes=[pltpu.VMEM((4 * ZN * HALF, TILE), jnp.float32)],
        compiler_params=pltpu.CompilerParams(vmem_limit_bytes=8 * MIB),
        name="by_rows",
    )(*pieces)


def join_kernel(spots, *refs):
    out_ref, sems = refs[-2], refs[-1]
    core, at0, at1 = spot()
    copies = []
    for i, (other, part, step) in enumerate(spots):
        half, at = (1 - core, at0) if other else (core, at1)
        copies.append(pltpu.make_async_copy(refs[i], out_ref.at[half, part, :, (at + 4 - step) % 4], sems.at[i]))
    for copy in copies:
        copy.start()
    for copy in copies:
        copy.wait()


def join(spots, pieces, out=None):
    n = len(spots)
    more = [] if out is None else [out]
    size = n * PART * 32 * TILE * 2
    return pl.pallas_call(
        functools.partial(join_kernel, spots),
        out_shape=jax.ShapeDtypeStruct((2, 2, PART, 4, 32, TILE), jnp.bfloat16),
        in_specs=[pl.BlockSpec(memory_space=pltpu.VMEM)] * n + [pl.BlockSpec(memory_space=pltpu.HBM)] * len(more),
        out_specs=pl.BlockSpec(memory_space=pltpu.HBM),
        scratch_shapes=[pltpu.SemaphoreType.DMA((n,))],
        input_output_aliases={} if out is None else {n: 0},
        compiler_params=pltpu.CompilerParams(vmem_limit_bytes=2 * MIB),
        cost_estimate=pl.CostEstimate(flops=0, bytes_accessed=2 * size, transcendentals=0),
        name="join",
    )(*pieces, *more)


def local(activations, cotangent, kept_tiles, kept_counts, chosen):
    me = lax.axis_index("dp")
    core = me % CN
    sent = own_tiles(kept_tiles.T, activations, cotangent)
    live = jnp.arange(KEPT, dtype=jnp.int32)[None, :] < kept_counts[:, None]
    ids = jnp.where(live, kept_tiles, -1).reshape(ZN, YN, XN, CN, KEPT)
    ids = lax.dynamic_index_in_dim(ids, core, 3, keepdims=False)
    ids = ids.transpose(2, 1, 0, 3).reshape(CHIPS * KEPT)
    got = lax.all_to_all(sent, "dp", 0, 0, axis_index_groups=CHIP_GROUPS, tiled=True)

    match = (chosen[:, None] == ids[None, :]).astype(jnp.float32)
    part = jnp.dot(match, got.reshape(CHIPS * KEPT, TILE), precision=lax.Precision.HIGHEST)
    part = part.reshape(CN, HALF, TILE)
    mine = lax.dynamic_index_in_dim(part, core, 0, keepdims=False)
    theirs = lax.dynamic_index_in_dim(part, 1 - core, 0, keepdims=False)
    row = (mine + lax.ppermute(theirs, "dp", SWAP)).astype(jnp.bfloat16)

    rows = lax.all_to_all(
        jnp.broadcast_to(row[None], (ZN, HALF, TILE)), "dp", 0, 0, axis_index_groups=Z_GROUPS, tiled=True
    )
    def swap(blocks):
        return [lax.ppermute(b, "dp", SWAP) for b in blocks]

    a0, b0 = by_rows([rows] + [lax.ppermute(rows, "dp", ring(s, 0)) for s in STEPS[1:]])
    a1 = lax.ppermute(a0, "dp", ring(1, 1))
    b3 = lax.ppermute(b0, "dp", ring(3, 1))
    b1 = lax.ppermute(b0, "dp", ring(1, 1))
    a3 = lax.ppermute(a0, "dp", ring(3, 1))
    a2 = lax.ppermute(a1, "dp", ring(1, 1))
    b2 = lax.ppermute(b3, "dp", ring(3, 1))
    out = None
    for steps, blocks in (
        ((0, 0), (a0, b0)),
        ((1, 3, 1, 3), (a1, a3, b1, b3)),
        ((2, 2), (a2, b2)),
    ):
        n = len(steps)
        spots = tuple((o, i * 2 // n, steps[i]) for o in range(2) for i in range(n))
        out = join(spots, list(blocks) + swap(blocks), out)
    return out.reshape(N_DP, TILE, TILE)


def solution(mesh):
    return jax.shard_map(
        local,
        mesh=mesh,
        in_specs=(P("dp", None), P("dp", None), P(), P(), P()),
        out_specs=P(),
        check_vma=False,
    )
```

time: 362 us -> 99.7 us (0.28)
  Pallas kernels: 261 us -> 10.5 us
  waiting for transfers between devices: 44 us -> 36.5 us
    pallas_call x2 -> x4, Pallas kernels: 258 us -> 6.24 us  [the longest x3 4.82 us: join(): pl.pallas_call(functools.partial(join_kernel, spots), out_shape=jax.Shape...]
    ppermute x10 -> x17, waiting for transfers between devices: 26 us -> 18.3 us  [the longest x3 7.02 us: local(): lax.ppermute(rows, 'dp', ring(s, 0))]
    ppermute x10 -> x17, starting transfers between devices: 15.1 us -> 15.1 us  [the longest x8 5.79 us: swap(): return [lax.ppermute(b, 'dp', SWAP) for b in blocks]]
  transfers between devices with their start and end apart: 12 -> 19, of which waited for: 8 -> 8; matrix products, arithmetic and copies ran while one was open for 0% -> 2% of each run, Pallas kernels for 0% -> 3%
where the time goes in v3:
time: 99.7 us; the launch traced here: 99.3 us
  waiting for transfers between devices  36.5 us (37%)
  starting transfers between devices  34.1 us (34%)
  blocking collectives  14.8 us (15%)
  Pallas kernels  10.5 us (11%)
  matrix products  1.33 us (1%)
  local copies, waits for them, and re-layouts  1.06 us (1%)
    all_to_all x1, waiting for transfers between devices, local(): lax.all_to_all(sent, 'dp', 0, 0, axis_index_groups=CHIP_GROUPS, tiled=True)  17.3 us
    all_to_all x1, starting transfers between devices, local(): lax.all_to_all(sent, 'dp', 0, 0, axis_index_groups=CHIP_GROUPS, tiled=True)  16.4 us
    all_to_all x1, blocking collectives, local(): lax.all_to_all(jnp.broadcast_to(row[None], (ZN, HALF, TILE)), 'dp', 0, 0,...  14.8 us
    ppermute x3, waiting for transfers between devices, local(): lax.ppermute(rows, 'dp', ring(s, 0))  7.02 us
    ppermute x8, starting transfers between devices, swap(): return [lax.ppermute(b, 'dp', SWAP) for b in blocks]  5.79 us
    ppermute x1, waiting for transfers between devices, local(): a1 = lax.ppermute(a0, 'dp', ring(1, 1))  5.39 us
    pallas_call x3, Pallas kernels, join(): pl.pallas_call(functools.partial(join_kernel, spots), out_shape=jax.Shape...  4.82 us
    ppermute x1, waiting for transfers between devices, local(): a2 = lax.ppermute(a1, 'dp', ring(1, 1))  4.6 us
  transfers between devices with their start and end apart: 19, of which 8 were waited for; matrix products, arithmetic and copies ran while one was open for 2% of the time, Pallas kernels for 3%

profile of v3, /device:TPU:1, one launch (start us, length us, event | category | flops | bytes accessed | tf_op | source)
XLA Modules:
  0.0 99.3 jit_solution(8958587892301772797)
XLA Ops:
  0.0 4.3 %own_tiles.1 = f32[128,8,128]{2,1,0:T(8,128)} custom-call(s32[8,256]{1,0:T(8,128)} %bitcast.24, bf16[128,8192]{1,0:T(8,128)(2,1)} %act_ref.1, bf16[128,2048]{1,0:T(8,128)(2,1)} %cot_ref.1), custom_call_target="tpu_custom_call" | custom-call | tf_op jit(solution)/shard_map/own_tiles/pallas_call | solution.py:81
  4.3 16.4 %all-to-all-start = ((f32[128,8,128]{2,1,0:T(8,128)}), f32[128,8,128]{2,1,0:T(8,128)S(1)}, u32[]{:S(2)}, u32[]{:S(2)}) async-start(f32[128,8,128]{2,1,0:T(8,128)} %own_tiles.1), calls=%async_computation | async-start | bytes 1048576 | tf_op jit(solution)/shard_map/all_to_all | solution.py:166
  22.5 17.3 %all-to-all-done = f32[128,8,128]{2,1,0:T(8,128)S(1)} async-done(((f32[128,8,128]{2,1,0:T(8,128)}), f32[128,8,128]{2,1,0:T(8,128)S(1)}, u32[]{:S(2)}, u32[]{:S(2)}) %all-to-all-start) | async-done | bytes 524320 | tf_op jit(solution)/shard_map/all_to_all | solution.py:166
  39.7 1.3 %fusion = f32[2,128,128]{2,1,0:T(8,128)S(1)} fusion(f32[128,8,128]{2,1,0:T(8,128)S(1)} %all-to-all-done, s32[1024]{0:T(1024)S(1)} %eq.26, s32[2,128]{1,0:T(2,128)} %bitcast.25), kind=kOutput, calls=%fused_computation | convolution fusion | flops 402915328 | bytes 660480 | tf_op jit(solution)/shard_map/dot_general | solution.py:169
  41.1 2.6 %collective-permute-start = (f32[128,128]{1,0:T(8,128)S(1)}, f32[128,128]{1,0:T(8,128)S(1)}, u32[]{:S(2)}, u32[]{:S(2)}) collective-permute-start(f32[128,128]{1,0:T(8,128)S(1)} %dynamic-slice_bitcast_fusion), channel_id=1, source_target_pairs={{0,1},{1,0},{2,3},{3,2},{4,5},{5,4},{6,7},{7,6},{8,9},{9,8},{10,11... | collective-permute-start | bytes 196616 | tf_op jit(solution)/shard_map/ppermute | solution.py:173
  43.7 0.9 collective-permute-done
  44.7 14.8 %all_to_all.10.p0 = bf16[8,128,128]{2,1,0:T(8,128)(2,1)S(1)} all-to-all(bf16[8,128,128]{2,1,0:T(8,128)(2,1)S(1)} %broadcast_in_dim.7), channel_id=1, replica_groups={{0,32,64,96,128,160,192,224},{1,33,65,97,129,161,193,225},{2,34,66,98,1..., dimensions={0} | all-to-all | bytes 524288 | tf_op jit(solution)/shard_map/all_to_all | solution.py:175
  59.5 2.7 %collective-permute-start.2 = (bf16[8,128,128]{2,1,0:T(8,128)(2,1)S(1)}, bf16[8,128,128]{2,1,0:T(8,128)(2,1)S(1)}, u32[]{:S(2)}, u32[]{:S(2)}) collective-permute-start(bf16[8,128,128]{2,1,0:T(8,128)(2,1)S(1)} %all_to_all.10.p0), channel_id=1, source_target_pairs={{0,24},{1,7},{2,26},{3,1},{4,28},{5,3},{6,30},{7,5},{8,0},{9,15},{... | collective-permute-start | bytes 786440 | tf_op jit(solution)/shard_map/ppermute | solution.py:181
  62.1 4.0 %collective-permute-done.1.p1 = bf16[8,128,128]{2,1,0:T(8,128)(2,1)S(1)} collective-permute-done((bf16[8,128,128]{2,1,0:T(8,128)(2,1)S(1)}, bf16[8,128,128]{2,1,0:T(8,128)(2,1)S(1)}, u32[]{:S(2)}, u32[]{:S(2)}) %collective-permute-start.1) | collective-permute-done | bytes 262176 | tf_op jit(solution)/shard_map/ppermute | solution.py:181
  66.2 2.1 %collective-permute-done.2.p2 = bf16[8,128,128]{2,1,0:T(8,128)(2,1)S(1)} collective-permute-done((bf16[8,128,128]{2,1,0:T(8,128)(2,1)S(1)}, bf16[8,128,128]{2,1,0:T(8,128)(2,1)S(1)}, u32[]{:S(2)}, u32[]{:S(2)}) %collective-permute-start.2) | collective-permute-done | bytes 262176 | tf_op jit(solution)/shard_map/ppermute | solution.py:181
  69.1 1.4 %by_rows.1 = (bf16[64,32,128]{2,1,0:T(8,128)(2,1)S(1)}, bf16[64,32,128]{2,1,0:T(8,128)(2,1)S(1)}) custom-call(bf16[8,128,128]{2,1,0:T(8,128)(2,1)S(1)} %all_to_all.10.p0, bf16[8,128,128]{2,1,0:T(8,128)(2,1)S(1)} %collective-permute-done.1.p1, bf16[8,128,128]{2,1,0:T(8,128)(2,1)S(1)} %collective-permute-done.2.p2, ...), custom_call_target="tpu_custom_call" | custom-call | tf_op jit(solution)/shard_map/by_rows/pallas_call | solution.py:117
  70.6 2.0 %collective-permute-start.16 = (bf16[64,32,128]{2,1,0:T(8,128)(2,1)S(1)}, bf16[64,32,128]{2,1,0:T(8,128)(2,1)S(1)}, u32[]{:S(2)}, u32[]{:S(2)}) collective-permute-start(bf16[64,32,128]{2,1,0:T(8,128)(2,1)S(1)} %get-tuple-element.7.refs_0_), channel_id=1, source_target_pairs={{0,1},{1,0},{2,3},{3,2},{4,5},{5,4},{6,7},{7,6},{8,9},{9,8},{10,11... | collective-permute-start | bytes 1572872 | tf_op jit(solution)/shard_map/ppermute | solution.py:179
  72.7 2.5 %collective-permute-start.6 = (bf16[64,32,128]{2,1,0:T(8,128)(2,1)S(1)}, bf16[64,32,128]{2,1,0:T(8,128)(2,1)S(1)}, u32[]{:S(2)}, u32[]{:S(2)}) collective-permute-start(bf16[64,32,128]{2,1,0:T(8,128)(2,1)S(1)} %get-tuple-element.8.refs_1_), channel_id=1, source_target_pairs={{0,6},{1,25},{2,0},{3,27},{4,2},{5,29},{6,4},{7,31},{8,14},{9,1},{... | collective-permute-start | bytes 1572872 | tf_op jit(solution)/shard_map/ppermute | solution.py:183
  75.2 1.0 %collective-permute-start.10 = (bf16[64,32,128]{2,1,0:T(8,128)(2,1)S(1)}, bf16[64,32,128]{2,1,0:T(8,128)(2,1)S(1)}, u32[]{:S(2)}, u32[]{:S(2)}) collective-permute-start(bf16[64,32,128]{2,1,0:T(8,128)(2,1)S(1)} %get-tuple-element.7.refs_0_), channel_id=1, source_target_pairs={{0,6},{1,25},{2,0},{3,27},{4,2},{5,29},{6,4},{7,31},{8,14},{9,1},{... | collective-permute-start | bytes 1572872 | tf_op jit(solution)/shard_map/ppermute | solution.py:185
  76.7 5.4 %collective-permute-done.4.refs_0_ = bf16[64,32,128]{2,1,0:T(8,128)(2,1)S(1)} collective-permute-done((bf16[64,32,128]{2,1,0:T(8,128)(2,1)S(1)}, bf16[64,32,128]{2,1,0:T(8,128)(2,1)S(1)}, u32[]{:S(2)}, u32[]{:S(2)}) %collective-permute-start.4) | collective-permute-done | bytes 524320 | tf_op jit(solution)/shard_map/ppermute | solution.py:182
  82.1 0.9 collective-permute-start.12
  83.0 2.7 %collective-permute-start.7 = (bf16[64,32,128]{2,1,0:T(8,128)(2,1)S(1)}, bf16[64,32,128]{2,1,0:T(8,128)(2,1)S(1)}, u32[]{:S(2)}, u32[]{:S(2)}) collective-permute-start(bf16[64,32,128]{2,1,0:T(8,128)(2,1)S(1)} %collective-permute-done.6.refs_3_), channel_id=1, source_target_pairs={{0,6},{1,25},{2,0},{3,27},{4,2},{5,29},{6,4},{7,31},{8,14},{9,1},{... | collective-permute-start | bytes 1572872 | tf_op jit(solution)/shard_map/ppermute | solution.py:187
  85.7 1.3 %collective-permute-done.10.refs_1_ = bf16[64,32,128]{2,1,0:T(8,128)(2,1)S(1)} collective-permute-done((bf16[64,32,128]{2,1,0:T(8,128)(2,1)S(1)}, bf16[64,32,128]{2,1,0:T(8,128)(2,1)S(1)}, u32[]{:S(2)}, u32[]{:S(2)}) %collective-permute-start.10) | collective-permute-done | bytes 524320 | tf_op jit(solution)/shard_map/ppermute | solution.py:185
  87.0 1.2 %collective-permute-start.15 = (bf16[64,32,128]{2,1,0:T(8,128)(2,1)S(1)}, bf16[64,32,128]{2,1,0:T(8,128)(2,1)S(1)}, u32[]{:S(2)}, u32[]{:S(2)}) collective-permute-start(bf16[64,32,128]{2,1,0:T(8,128)(2,1)S(1)} %collective-permute-done.6.refs_3_), channel_id=1, source_target_pairs={{0,1},{1,0},{2,3},{3,2},{4,5},{5,4},{6,7},{7,6},{8,9},{9,8},{10,11... | collective-permute-start | bytes 1572872 | tf_op jit(solution)/shard_map/ppermute | solution.py:179
  88.7 4.6 %collective-permute-done.5.refs_0_ = bf16[64,32,128]{2,1,0:T(8,128)(2,1)S(1)} collective-permute-done((bf16[64,32,128]{2,1,0:T(8,128)(2,1)S(1)}, bf16[64,32,128]{2,1,0:T(8,128)(2,1)S(1)}, u32[]{:S(2)}, u32[]{:S(2)}) %collective-permute-start.5) | collective-permute-done | bytes 524320 | tf_op jit(solution)/shard_map/ppermute | solution.py:186
  93.3 0.9 collective-permute-start.8
  94.3 1.3 %join.3.refs_8_ = bf16[2,2,64,4,32,128]{5,4,3,2,1,0:T(8,128)(2,1)} custom-call(bf16[64,32,128]{2,1,0:T(8,128)(2,1)S(1)} %get-tuple-element.7.refs_0_, bf16[64,32,128]{2,1,0:T(8,128)(2,1)S(1)} %get-tuple-element.8.refs_1_, bf16[64,32,128]{2,1,0:T(8,128)(2,1)S(1)} %collective-permute-done.16.refs_2_, bf16[64,32,128]{2,1,0:T(8,128)(2,1)S(1)} %collective-permute-done.17.refs_3_), custom_call_target="tpu_custom_call" | custom-call | bytes 4194304 | tf_op jit(solution)/shard_map/join/pallas_call | solution.py:145
  95.7 2.1 %join.4.refs_4_ = bf16[2,2,64,4,32,128]{5,4,3,2,1,0:T(8,128)(2,1)} custom-call(bf16[64,32,128]{2,1,0:T(8,128)(2,1)S(1)} %collective-permute-done.4.refs_0_, bf16[64,32,128]{2,1,0:T(8,128)(2,1)S(1)} %collective-permute-done.10.refs_1_, bf16[64,32,128]{2,1,0:T(8,128)(2,1)S(1)} %collective-permute-done.11.refs_2_, ...), custom_call_target="tpu_custom_call", output_to_operand_aliasing={{}: (8, {})} | custom-call | bytes 8388608 | tf_op jit(solution)/shard_map/join/pallas_call | solution.py:145
  97.8 1.4 %join.5 = bf16[2,2,64,4,32,128]{5,4,3,2,1,0:T(8,128)(2,1)} custom-call(bf16[64,32,128]{2,1,0:T(8,128)(2,1)S(1)} %collective-permute-done.5.refs_0_, bf16[64,32,128]{2,1,0:T(8,128)(2,1)S(1)} %collective-permute-done.7.refs_1_, bf16[64,32,128]{2,1,0:T(8,128)(2,1)S(1)} %collective-permute-done.8.refs_2_, ...), custom_call_target="tpu_custom_call", output_to_operand_aliasing={{}: (4, {})} | custom-call | bytes 4194304 | tf_op jit(solution)/shard_map/join/pallas_call | solution.py:145
  (29 shorter events, 3.9 us)
Async XLA Ops:
  4.3 35.5 %all-to-all-start = ((f32[128,8,128]{2,1,0:T(8,128)}), f32[128,8,128]{2,1,0:T(8,128)S(1)}, u32[]{:S(2)}, u32[]{:S(2)}) async-start(f32[128,8,128]{2,1,0:T(8,128)} %own_tiles.1), calls=%async_computation | async-start | bytes 1048576 | tf_op jit(solution)/shard_map/all_to_all | solution.py:166
  41.1 3.5 %collective-permute-start = (f32[128,128]{1,0:T(8,128)S(1)}, f32[128,128]{1,0:T(8,128)S(1)}, u32[]{:S(2)}, u32[]{:S(2)}) collective-permute-start(f32[128,128]{1,0:T(8,128)S(1)} %dynamic-slice_bitcast_fusion), channel_id=1, source_target_pairs={{0,1},{1,0},{2,3},{3,2},{4,5},{5,4},{6,7},{7,6},{8,9},{9,8},{10,11... | collective-permute-start | bytes 196616 | tf_op jit(solution)/shard_map/ppermute | solution.py:173
  59.4 6.7 %collective-permute-start.1 = (bf16[8,128,128]{2,1,0:T(8,128)(2,1)S(1)}, bf16[8,128,128]{2,1,0:T(8,128)(2,1)S(1)}, u32[]{:S(2)}, u32[]{:S(2)}) collective-permute-start(bf16[8,128,128]{2,1,0:T(8,128)(2,1)S(1)} %all_to_all.10.p0), channel_id=1, source_target_pairs={{0,8},{1,3},{2,10},{3,5},{4,12},{5,7},{6,14},{7,1},{8,16},{9,11},{... | collective-permute-start | bytes 786440 | tf_op jit(solution)/shard_map/ppermute | solution.py:181
  59.5 8.8 %collective-permute-start.2 = (bf16[8,128,128]{2,1,0:T(8,128)(2,1)S(1)}, bf16[8,128,128]{2,1,0:T(8,128)(2,1)S(1)}, u32[]{:S(2)}, u32[]{:S(2)}) collective-permute-start(bf16[8,128,128]{2,1,0:T(8,128)(2,1)S(1)} %all_to_all.10.p0), channel_id=1, source_target_pairs={{0,24},{1,7},{2,26},{3,1},{4,28},{5,3},{6,30},{7,5},{8,0},{9,15},{... | collective-permute-start | bytes 786440 | tf_op jit(solution)/shard_map/ppermute | solution.py:181
  62.1 7.0 %collective-permute-start.3 = (bf16[8,128,128]{2,1,0:T(8,128)(2,1)S(1)}, bf16[8,128,128]{2,1,0:T(8,128)(2,1)S(1)}, u32[]{:S(2)}, u32[]{:S(2)}) collective-permute-start(bf16[8,128,128]{2,1,0:T(8,128)(2,1)S(1)} %all_to_all.10.p0), channel_id=1, source_target_pairs={{0,16},{1,5},{2,18},{3,7},{4,20},{5,1},{6,22},{7,3},{8,24},{9,13},... | collective-permute-start | bytes 786440 | tf_op jit(solution)/shard_map/ppermute | solution.py:181
  70.6 5.7 %collective-permute-start.16 = (bf16[64,32,128]{2,1,0:T(8,128)(2,1)S(1)}, bf16[64,32,128]{2,1,0:T(8,128)(2,1)S(1)}, u32[]{:S(2)}, u32[]{:S(2)}) collective-permute-start(bf16[64,32,128]{2,1,0:T(8,128)(2,1)S(1)} %get-tuple-element.7.refs_0_), channel_id=1, source_target_pairs={{0,1},{1,0},{2,3},{3,2},{4,5},{5,4},{6,7},{7,6},{8,9},{9,8},{10,11... | collective-permute-start | bytes 1572872 | tf_op jit(solution)/shard_map/ppermute | solution.py:179
  72.5 9.5 %collective-permute-start.4 = (bf16[64,32,128]{2,1,0:T(8,128)(2,1)S(1)}, bf16[64,32,128]{2,1,0:T(8,128)(2,1)S(1)}, u32[]{:S(2)}, u32[]{:S(2)}) collective-permute-start(bf16[64,32,128]{2,1,0:T(8,128)(2,1)S(1)} %get-tuple-element.7.refs_0_), channel_id=1, source_target_pairs={{0,2},{1,9},{2,4},{3,11},{4,6},{5,13},{6,0},{7,15},{8,10},{9,17},{... | collective-permute-start | bytes 1572872 | tf_op jit(solution)/shard_map/ppermute | solution.py:182
  72.5 10.5 %collective-permute-start.17 = (bf16[64,32,128]{2,1,0:T(8,128)(2,1)S(1)}, bf16[64,32,128]{2,1,0:T(8,128)(2,1)S(1)}, u32[]{:S(2)}, u32[]{:S(2)}) collective-permute-start(bf16[64,32,128]{2,1,0:T(8,128)(2,1)S(1)} %get-tuple-element.8.refs_1_), channel_id=1, source_target_pairs={{0,1},{1,0},{2,3},{3,2},{4,5},{5,4},{6,7},{7,6},{8,9},{9,8},{10,11... | collective-permute-start | bytes 1572872 | tf_op jit(solution)/shard_map/ppermute | solution.py:179
  72.7 10.3 %collective-permute-start.6 = (bf16[64,32,128]{2,1,0:T(8,128)(2,1)S(1)}, bf16[64,32,128]{2,1,0:T(8,128)(2,1)S(1)}, u32[]{:S(2)}, u32[]{:S(2)}) collective-permute-start(bf16[64,32,128]{2,1,0:T(8,128)(2,1)S(1)} %get-tuple-element.8.refs_1_), channel_id=1, source_target_pairs={{0,6},{1,25},{2,0},{3,27},{4,2},{5,29},{6,4},{7,31},{8,14},{9,1},{... | collective-permute-start | bytes 1572872 | tf_op jit(solution)/shard_map/ppermute | solution.py:183
  75.2 11.7 %collective-permute-start.10 = (bf16[64,32,128]{2,1,0:T(8,128)(2,1)S(1)}, bf16[64,32,128]{2,1,0:T(8,128)(2,1)S(1)}, u32[]{:S(2)}, u32[]{:S(2)}) collective-permute-start(bf16[64,32,128]{2,1,0:T(8,128)(2,1)S(1)} %get-tuple-element.7.refs_0_), channel_id=1, source_target_pairs={{0,6},{1,25},{2,0},{3,27},{4,2},{5,29},{6,4},{7,31},{8,14},{9,1},{... | collective-permute-start | bytes 1572872 | tf_op jit(solution)/shard_map/ppermute | solution.py:185
  76.3 11.9 %collective-permute-start.11 = (bf16[64,32,128]{2,1,0:T(8,128)(2,1)S(1)}, bf16[64,32,128]{2,1,0:T(8,128)(2,1)S(1)}, u32[]{:S(2)}, u32[]{:S(2)}) collective-permute-start(bf16[64,32,128]{2,1,0:T(8,128)(2,1)S(1)} %get-tuple-element.8.refs_1_), channel_id=1, source_target_pairs={{0,2},{1,9},{2,4},{3,11},{4,6},{5,13},{6,0},{7,15},{8,10},{9,17},{... | collective-permute-start | bytes 1572872 | tf_op jit(solution)/shard_map/ppermute | solution.py:184
  82.1 6.6 %collective-permute-start.12 = (bf16[64,32,128]{2,1,0:T(8,128)(2,1)S(1)}, bf16[64,32,128]{2,1,0:T(8,128)(2,1)S(1)}, u32[]{:S(2)}, u32[]{:S(2)}) collective-permute-start(bf16[64,32,128]{2,1,0:T(8,128)(2,1)S(1)} %collective-permute-done.4.refs_0_), channel_id=1, source_target_pairs={{0,1},{1,0},{2,3},{3,2},{4,5},{5,4},{6,7},{7,6},{8,9},{9,8},{10,11... | collective-permute-start | bytes 1572872 | tf_op jit(solution)/shard_map/ppermute | solution.py:179
  83.0 10.3 %collective-permute-start.5 = (bf16[64,32,128]{2,1,0:T(8,128)(2,1)S(1)}, bf16[64,32,128]{2,1,0:T(8,128)(2,1)S(1)}, u32[]{:S(2)}, u32[]{:S(2)}) collective-permute-start(bf16[64,32,128]{2,1,0:T(8,128)(2,1)S(1)} %collective-permute-done.4.refs_0_), channel_id=1, source_target_pairs={{0,2},{1,9},{2,4},{3,11},{4,6},{5,13},{6,0},{7,15},{8,10},{9,17},{... | collective-permute-start | bytes 1572872 | tf_op jit(solution)/shard_map/ppermute | solution.py:186
  83.0 11.2 %collective-permute-start.7 = (bf16[64,32,128]{2,1,0:T(8,128)(2,1)S(1)}, bf16[64,32,128]{2,1,0:T(8,128)(2,1)S(1)}, u32[]{:S(2)}, u32[]{:S(2)}) collective-permute-start(bf16[64,32,128]{2,1,0:T(8,128)(2,1)S(1)} %collective-permute-done.6.refs_3_), channel_id=1, source_target_pairs={{0,6},{1,25},{2,0},{3,27},{4,2},{5,29},{6,4},{7,31},{8,14},{9,1},{... | collective-permute-start | bytes 1572872 | tf_op jit(solution)/shard_map/ppermute | solution.py:187
  87.0 8.7 %collective-permute-start.15 = (bf16[64,32,128]{2,1,0:T(8,128)(2,1)S(1)}, bf16[64,32,128]{2,1,0:T(8,128)(2,1)S(1)}, u32[]{:S(2)}, u32[]{:S(2)}) collective-permute-start(bf16[64,32,128]{2,1,0:T(8,128)(2,1)S(1)} %collective-permute-done.6.refs_3_), channel_id=1, source_target_pairs={{0,1},{1,0},{2,3},{3,2},{4,5},{5,4},{6,7},{7,6},{8,9},{9,8},{10,11... | collective-permute-start | bytes 1572872 | tf_op jit(solution)/shard_map/ppermute | solution.py:179
  88.2 7.4 %collective-permute-start.13 = (bf16[64,32,128]{2,1,0:T(8,128)(2,1)S(1)}, bf16[64,32,128]{2,1,0:T(8,128)(2,1)S(1)}, u32[]{:S(2)}, u32[]{:S(2)}) collective-permute-start(bf16[64,32,128]{2,1,0:T(8,128)(2,1)S(1)} %collective-permute-done.10.refs_1_), channel_id=1, source_target_pairs={{0,1},{1,0},{2,3},{3,2},{4,5},{5,4},{6,7},{7,6},{8,9},{9,8},{10,11... | collective-permute-start | bytes 1572872 | tf_op jit(solution)/shard_map/ppermute | solution.py:179
  88.7 7.0 %collective-permute-start.14 = (bf16[64,32,128]{2,1,0:T(8,128)(2,1)S(1)}, bf16[64,32,128]{2,1,0:T(8,128)(2,1)S(1)}, u32[]{:S(2)}, u32[]{:S(2)}) collective-permute-start(bf16[64,32,128]{2,1,0:T(8,128)(2,1)S(1)} %collective-permute-done.11.refs_2_), channel_id=1, source_target_pairs={{0,1},{1,0},{2,3},{3,2},{4,5},{5,4},{6,7},{7,6},{8,9},{9,8},{10,11... | collective-permute-start | bytes 1572872 | tf_op jit(solution)/shard_map/ppermute | solution.py:179
  93.3 4.5 %collective-permute-start.8 = (bf16[64,32,128]{2,1,0:T(8,128)(2,1)S(1)}, bf16[64,32,128]{2,1,0:T(8,128)(2,1)S(1)}, u32[]{:S(2)}, u32[]{:S(2)}) collective-permute-start(bf16[64,32,128]{2,1,0:T(8,128)(2,1)S(1)} %collective-permute-done.5.refs_0_), channel_id=1, source_target_pairs={{0,1},{1,0},{2,3},{3,2},{4,5},{5,4},{6,7},{7,6},{8,9},{9,8},{10,11... | collective-permute-start | bytes 1572872 | tf_op jit(solution)/shard_map/ppermute | solution.py:179
  94.3 3.5 %collective-permute-start.9 = (bf16[64,32,128]{2,1,0:T(8,128)(2,1)S(1)}, bf16[64,32,128]{2,1,0:T(8,128)(2,1)S(1)}, u32[]{:S(2)}, u32[]{:S(2)}) collective-permute-start(bf16[64,32,128]{2,1,0:T(8,128)(2,1)S(1)} %collective-permute-done.7.refs_1_), channel_id=1, source_target_pairs={{0,1},{1,0},{2,3},{3,2},{4,5},{5,4},{6,7},{7,6},{8,9},{9,8},{10,11... | collective-permute-start | bytes 1572872 | tf_op jit(solution)/shard_map/ppermute | solution.py:179

commit v4 on v3

--- a/solution.py
+++ b/solution.py
@@ -2,6 +2,7 @@
 
 import jax
 import jax.numpy as jnp
+import numpy as np
 from jax import lax
 from jax.experimental import pallas as pl
 from jax.experimental.pallas import tpu as pltpu
@@ -25,7 +26,7 @@
 
 
 DEVS = [(z, y, x, c) for z in range(ZN) for y in range(YN) for x in range(XN) for c in range(CN)]
-CHIP_GROUPS = [[dev(z, y, x, c) for x in range(XN) for y in range(YN) for z in range(ZN)] for c in range(CN)]
+CHIP_GROUPS = [[dev(z, y, x, c) for y in range(YN) for z in range(ZN) for x in range(XN)] for c in range(CN)]
 Z_GROUPS = [[dev(z, y, x, c) for z in range(ZN)] for y in range(YN) for x in range(XN) for c in range(CN)]
 SWAP = [(d, d ^ 1) for d in range(N_DP)]
 
@@ -50,20 +51,15 @@
 
 def tiles_kernel(kept_ref, act_ref, cot_ref, out_ref, lefts, rights, stage, sems):
     me = lax.axis_index("dp")
-    copies = []
     for k in range(KEPT):
         tile = kept_ref[k, me]
         row = pl.multiple_of((tile // COLS) * TILE, TILE)
         col = pl.multiple_of((tile % COLS) * TILE, TILE)
-        a = pltpu.make_async_copy(act_ref.at[:, pl.ds(row, TILE)], lefts.at[k], sems.at[k, 0])
-        b = pltpu.make_async_copy(cot_ref.at[:, pl.ds(col, TILE)], rights.at[k], sems.at[k, 1])
-        a.start()
-        b.start()
-        copies.append((a, b))
+        pltpu.make_async_copy(act_ref.at[:, pl.ds(row, TILE)], lefts.at[k], sems.at[0]).start()
+        pltpu.make_async_copy(cot_ref.at[:, pl.ds(col, TILE)], rights.at[k], sems.at[1]).start()
+    pltpu.make_async_copy(lefts, lefts, sems.at[0]).wait()
+    pltpu.make_async_copy(rights, rights, sems.at[1]).wait()
     for k in range(KEPT):
-        a, b = copies[k]
-        a.wait()
-        b.wait()
         half = kept_ref[k, me] // HALF_TILES
         tile = lax.dot_general(
             lefts[k], rights[k], (((0,), (0,)), ((), ())), preferred_element_type=jnp.float32
@@ -73,8 +69,8 @@
                 there = jnp.where(half == 0, p * 32 + q * 8, q * 32 + p * 8) + k * TILE
                 here = p * 32 + q * 8
                 stage[pl.ds(pl.multiple_of(there, 8), 8), :] = tile[here:here + 8, :]
-    for chip in range(CHIPS):
-        out_ref[chip] = stage[pl.ds(chip, KEPT, stride=TILE), :]
+    for i, (y, z, x) in enumerate(np.ndindex(YN, ZN, XN)):
+        out_ref[i] = stage[pl.ds(x * 32 + y * 8 + z, KEPT, stride=TILE), :]
 
 
 def own_tiles(kept, activations, cotangent):
@@ -91,7 +87,7 @@
             pltpu.VMEM((KEPT, TILE, TILE), jnp.bfloat16),
             pltpu.VMEM((KEPT, TILE, TILE), jnp.bfloat16),
             pltpu.VMEM((KEPT * TILE, TILE), jnp.float32),
-            pltpu.SemaphoreType.DMA((KEPT, 2)),
+            pltpu.SemaphoreType.DMA((2,)),
         ],
         compiler_params=pltpu.CompilerParams(vmem_limit_bytes=62 * MIB),
         name="own_tiles",
@@ -162,7 +158,7 @@
     live = jnp.arange(KEPT, dtype=jnp.int32)[None, :] < kept_counts[:, None]
     ids = jnp.where(live, kept_tiles, -1).reshape(ZN, YN, XN, CN, KEPT)
     ids = lax.dynamic_index_in_dim(ids, core, 3, keepdims=False)
-    ids = ids.transpose(2, 1, 0, 3).reshape(CHIPS * KEPT)
+    ids = ids.transpose(1, 0, 2, 3).reshape(CHIPS * KEPT)
     got = lax.all_to_all(sent, "dp", 0, 0, axis_index_groups=CHIP_GROUPS, tiled=True)
 
     match = (chosen[:, None] == ids[None, :]).astype(jnp.float32)
@@ -175,25 +171,33 @@
     rows = lax.all_to_all(
         jnp.broadcast_to(row[None], (ZN, HALF, TILE)), "dp", 0, 0, axis_index_groups=Z_GROUPS, tiled=True
     )
-    def swap(blocks):
-        return [lax.ppermute(b, "dp", SWAP) for b in blocks]
-
-    a0, b0 = by_rows([rows] + [lax.ppermute(rows, "dp", ring(s, 0)) for s in STEPS[1:]])
-    a1 = lax.ppermute(a0, "dp", ring(1, 1))
-    b3 = lax.ppermute(b0, "dp", ring(3, 1))
-    b1 = lax.ppermute(b0, "dp", ring(1, 1))
-    a3 = lax.ppermute(a0, "dp", ring(3, 1))
-    a2 = lax.ppermute(a1, "dp", ring(1, 1))
-    b2 = lax.ppermute(b3, "dp", ring(3, 1))
-    out = None
-    for steps, blocks in (
-        ((0, 0), (a0, b0)),
-        ((1, 3, 1, 3), (a1, a3, b1, b3)),
-        ((2, 2), (a2, b2)),
-    ):
+    def swap(name, blocks):
+        with jax.named_scope(name):
+            return [lax.ppermute(b, "dp", SWAP) for b in blocks]
+
+    def send(name, block, step):
+        with jax.named_scope(name):
+            return lax.ppermute(block, "dp", ring(step, 1))
+
+    def both(steps):
         n = len(steps)
-        spots = tuple((o, i * 2 // n, steps[i]) for o in range(2) for i in range(n))
-        out = join(spots, list(blocks) + swap(blocks), out)
+        return tuple((o, i * 2 // n, steps[i]) for o in range(2) for i in range(n))
+
+    with jax.named_scope("s2"):
+        pieces = [rows] + [lax.ppermute(rows, "dp", ring(s, 0)) for s in STEPS[1:]]
+    a0, b0 = by_rows(pieces)
+    a1 = send("a1", a0, 1)
+    b3 = send("b3", b0, 3)
+    b1 = send("b1", b0, 1)
+    a3 = send("a3", a0, 3)
+    own = swap("own", [a0, b0])
+    out = join(both((0, 0)), [a0, b0] + own)
+    a1, b3, out = lax.optimization_barrier((a1, b3, out))
+    a2 = send("a2", a1, 1)
+    b2 = send("b2", b3, 3)
+    near = [a1, a3, b1, b3]
+    out = join(both((1, 3, 1, 3)), near + swap("near", near), out)
+    out = join(both((2, 2)), [a2, b2] + swap("far", [a2, b2]), out)
     return out.reshape(N_DP, TILE, TILE)
 
 

time: 99.7 us -> 97 us (0.973)
  waiting for transfers between devices: 36.5 us -> 31.5 us
  starting transfers between devices: 34.1 us -> 38.1 us
  Pallas kernels: 10.5 us -> 9.5 us
    ppermute x9, waiting for transfers between devices: 18.3 us -> 15.5 us  [the longest x6 9.27 us: send(): return lax.ppermute(block, 'dp', ring(step, 1))]
    all_to_all x1, waiting for transfers between devices: 17.3 us -> 15 us  [local(): lax.all_to_all(sent, 'dp', 0, 0, axis_index_groups=CHIP_GROUPS, tiled=True)]
    ppermute x8, starting transfers between devices: 5.79 us -> 7.86 us  [swap(): return [lax.ppermute(b, 'dp', SWAP) for b in blocks]]
    ppermute x9, starting transfers between devices: 9.31 us -> 10.3 us  [the longest x6 6.82 us: send(): return lax.ppermute(block, 'dp', ring(step, 1))]
  transfers between devices with their start and end apart: 19 -> 19, of which waited for: 8 -> 9; matrix products, arithmetic and copies ran while one was open for 2% -> 2% of each run, Pallas kernels for 3% -> 4%
where the time goes in v4:
time: 97 us; the launch traced here: 96.6 us
  starting transfers between devices  38.1 us (39%)
  waiting for transfers between devices  31.5 us (32%)
  blocking collectives  14 us (14%)
  Pallas kernels  9.5 us (10%)
  matrix products  1.33 us (1%)
  local copies, waits for them, and re-layouts  1.09 us (1%)
    all_to_all x1, starting transfers between devices, local(): lax.all_to_all(sent, 'dp', 0, 0, axis_index_groups=CHIP_GROUPS, tiled=True)  16.3 us
    all_to_all x1, waiting for transfers between devices, local(): lax.all_to_all(sent, 'dp', 0, 0, axis_index_groups=CHIP_GROUPS, tiled=True)  15 us
    all_to_all x1, blocking collectives, local(): lax.all_to_all(jnp.broadcast_to(row[None], (ZN, HALF, TILE)), 'dp', 0, 0,...  14 us
    ppermute x6, waiting for transfers between devices, send(): return lax.ppermute(block, 'dp', ring(step, 1))  9.27 us
    ppermute x8, starting transfers between devices, swap(): return [lax.ppermute(b, 'dp', SWAP) for b in blocks]  7.86 us
    ppermute x6, starting transfers between devices, send(): return lax.ppermute(block, 'dp', ring(step, 1))  6.82 us
    ppermute x3, waiting for transfers between devices, local(): pieces = [rows] + [lax.ppermute(rows, 'dp', ring(s, 0)) for s in STEPS[1:]]  6.19 us
    pallas_call x3, Pallas kernels, join(): pl.pallas_call(functools.partial(join_kernel, spots), out_shape=jax.Shape...  4.79 us
  transfers between devices with their start and end apart: 19, of which 9 were waited for; matrix products, arithmetic and copies ran while one was open for 2% of the time, Pallas kernels for 4%

profile of v4, /device:TPU:1, one launch (start us, length us, event | category | flops | bytes accessed | tf_op | source)
XLA Modules:
  0.0 96.6 jit_solution(6449950705685188453)
XLA Ops:
  0.0 3.3 %own_tiles.1 = f32[128,8,128]{2,1,0:T(8,128)} custom-call(s32[8,256]{1,0:T(8,128)} %bitcast.22, bf16[128,8192]{1,0:T(8,128)(2,1)} %act_ref.1, bf16[128,2048]{1,0:T(8,128)(2,1)} %cot_ref.1), custom_call_target="tpu_custom_call" | custom-call | tf_op jit(solution)/shard_map/own_tiles/pallas_call | solution.py:77
  3.3 16.3 %all-to-all-start = ((f32[128,8,128]{2,1,0:T(8,128)}), f32[128,8,128]{2,1,0:T(8,128)S(1)}, u32[]{:S(2)}, u32[]{:S(2)}) async-start(f32[128,8,128]{2,1,0:T(8,128)} %own_tiles.1), calls=%async_computation | async-start | bytes 1048576 | tf_op jit(solution)/shard_map/all_to_all | solution.py:162
  21.5 15.0 %all-to-all-done = f32[128,8,128]{2,1,0:T(8,128)S(1)} async-done(((f32[128,8,128]{2,1,0:T(8,128)}), f32[128,8,128]{2,1,0:T(8,128)S(1)}, u32[]{:S(2)}, u32[]{:S(2)}) %all-to-all-start) | async-done | bytes 524320 | tf_op jit(solution)/shard_map/all_to_all | solution.py:162
  36.5 1.3 %fusion = f32[2,128,128]{2,1,0:T(8,128)S(1)} fusion(f32[128,8,128]{2,1,0:T(8,128)S(1)} %all-to-all-done, s32[1024]{0:T(1024)S(1)} %eq.26, s32[2,128]{1,0:T(2,128)} %bitcast.23), kind=kOutput, calls=%fused_computation | convolution fusion | flops 402915328 | bytes 660480 | tf_op jit(solution)/shard_map/dot_general | solution.py:165
  37.9 3.5 %collective-permute-start = (f32[128,128]{1,0:T(8,128)S(1)}, f32[128,128]{1,0:T(8,128)S(1)}, u32[]{:S(2)}, u32[]{:S(2)}) collective-permute-start(f32[128,128]{1,0:T(8,128)S(1)} %dynamic-slice_bitcast_fusion), channel_id=1, source_target_pairs={{0,1},{1,0},{2,3},{3,2},{4,5},{5,4},{6,7},{7,6},{8,9},{9,8},{10,11... | collective-permute-start | bytes 196616 | tf_op jit(solution)/shard_map/ppermute | solution.py:169
  41.4 0.9 collective-permute-done
  42.4 14.0 %all_to_all.10.p0 = bf16[8,128,128]{2,1,0:T(8,128)(2,1)S(1)} all-to-all(bf16[8,128,128]{2,1,0:T(8,128)(2,1)S(1)} %broadcast_in_dim.7), channel_id=1, replica_groups={{0,32,64,96,128,160,192,224},{1,33,65,97,129,161,193,225},{2,34,66,98,1..., dimensions={0} | all-to-all | bytes 524288 | tf_op jit(solution)/shard_map/all_to_all | solution.py:171
  56.7 2.4 %collective-permute-start.2 = (bf16[8,128,128]{2,1,0:T(8,128)(2,1)S(1)}, bf16[8,128,128]{2,1,0:T(8,128)(2,1)S(1)}, u32[]{:S(2)}, u32[]{:S(2)}) collective-permute-start(bf16[8,128,128]{2,1,0:T(8,128)(2,1)S(1)} %all_to_all.10.p0), channel_id=1, source_target_pairs={{0,24},{1,7},{2,26},{3,1},{4,28},{5,3},{6,30},{7,5},{8,0},{9,15},{... | collective-permute-start | bytes 786440 | tf_op jit(solution)/shard_map/s2/ppermute | solution.py:187
  59.9 3.2 %collective-permute-done.1.p1 = bf16[8,128,128]{2,1,0:T(8,128)(2,1)S(1)} collective-permute-done((bf16[8,128,128]{2,1,0:T(8,128)(2,1)S(1)}, bf16[8,128,128]{2,1,0:T(8,128)(2,1)S(1)}, u32[]{:S(2)}, u32[]{:S(2)}) %collective-permute-start.1) | collective-permute-done | bytes 262176 | tf_op jit(solution)/shard_map/s2/ppermute | solution.py:187
  63.1 2.1 %collective-permute-done.2.p2 = bf16[8,128,128]{2,1,0:T(8,128)(2,1)S(1)} collective-permute-done((bf16[8,128,128]{2,1,0:T(8,128)(2,1)S(1)}, bf16[8,128,128]{2,1,0:T(8,128)(2,1)S(1)}, u32[]{:S(2)}, u32[]{:S(2)}) %collective-permute-start.2) | collective-permute-done | bytes 262176 | tf_op jit(solution)/shard_map/s2/ppermute | solution.py:187
  66.1 1.4 %by_rows.1 = (bf16[64,32,128]{2,1,0:T(8,128)(2,1)S(1)}, bf16[64,32,128]{2,1,0:T(8,128)(2,1)S(1)}) custom-call(bf16[8,128,128]{2,1,0:T(8,128)(2,1)S(1)} %all_to_all.10.p0, bf16[8,128,128]{2,1,0:T(8,128)(2,1)S(1)} %collective-permute-done.1.p1, bf16[8,128,128]{2,1,0:T(8,128)(2,1)S(1)} %collective-permute-done.2.p2, ...), custom_call_target="tpu_custom_call" | custom-call | tf_op jit(solution)/shard_map/by_rows/pallas_call | solution.py:113
  67.5 3.2 %collective-permute-start.6 = (bf16[64,32,128]{2,1,0:T(8,128)(2,1)S(1)}, bf16[64,32,128]{2,1,0:T(8,128)(2,1)S(1)}, u32[]{:S(2)}, u32[]{:S(2)}) collective-permute-start(bf16[64,32,128]{2,1,0:T(8,128)(2,1)S(1)} %get-tuple-element.10.refs_0_), channel_id=1, source_target_pairs={{0,1},{1,0},{2,3},{3,2},{4,5},{5,4},{6,7},{7,6},{8,9},{9,8},{10,11... | collective-permute-start | bytes 1572872 | tf_op jit(solution)/shard_map/own/ppermute | solution.py:176
  70.8 2.7 %collective-permute-start.5 = (bf16[64,32,128]{2,1,0:T(8,128)(2,1)S(1)}, bf16[64,32,128]{2,1,0:T(8,128)(2,1)S(1)}, u32[]{:S(2)}, u32[]{:S(2)}) collective-permute-start(bf16[64,32,128]{2,1,0:T(8,128)(2,1)S(1)} %get-tuple-element.11.refs_1_), channel_id=1, source_target_pairs={{0,6},{1,25},{2,0},{3,27},{4,2},{5,29},{6,4},{7,31},{8,14},{9,1},{... | collective-permute-start | bytes 1572872 | tf_op jit(solution)/shard_map/b3/ppermute | solution.py:180
  73.5 1.0 %collective-permute-start.12 = (bf16[64,32,128]{2,1,0:T(8,128)(2,1)S(1)}, bf16[64,32,128]{2,1,0:T(8,128)(2,1)S(1)}, u32[]{:S(2)}, u32[]{:S(2)}) collective-permute-start(bf16[64,32,128]{2,1,0:T(8,128)(2,1)S(1)} %get-tuple-element.10.refs_0_), channel_id=1, source_target_pairs={{0,6},{1,25},{2,0},{3,27},{4,2},{5,29},{6,4},{7,31},{8,14},{9,1},{... | collective-permute-start | bytes 1572872 | tf_op jit(solution)/shard_map/a3/ppermute | solution.py:180
  74.9 1.3 %join.3.refs_8_ = bf16[2,2,64,4,32,128]{5,4,3,2,1,0:T(8,128)(2,1)} custom-call(bf16[64,32,128]{2,1,0:T(8,128)(2,1)S(1)} %get-tuple-element.10.refs_0_, bf16[64,32,128]{2,1,0:T(8,128)(2,1)S(1)} %get-tuple-element.11.refs_1_, bf16[64,32,128]{2,1,0:T(8,128)(2,1)S(1)} %collective-permute-done.6.refs_2_, bf16[64,32,128]{2,1,0:T(8,128)(2,1)S(1)} %collective-permute-done.7.refs_3_), custom_call_target="tpu_custom_call" | custom-call | bytes 4194304 | tf_op jit(solution)/shard_map/join/pallas_call | solution.py:141
  76.3 4.0 %collective-permute-done.4.refs_0_ = bf16[64,32,128]{2,1,0:T(8,128)(2,1)S(1)} collective-permute-done((bf16[64,32,128]{2,1,0:T(8,128)(2,1)S(1)}, bf16[64,32,128]{2,1,0:T(8,128)(2,1)S(1)}, u32[]{:S(2)}, u32[]{:S(2)}) %collective-permute-start.4) | collective-permute-done | bytes 524320 | tf_op jit(solution)/shard_map/a1/ppermute | solution.py:180
  80.3 1.3 %collective-permute-start.14 = (bf16[64,32,128]{2,1,0:T(8,128)(2,1)S(1)}, bf16[64,32,128]{2,1,0:T(8,128)(2,1)S(1)}, u32[]{:S(2)}, u32[]{:S(2)}) collective-permute-start(bf16[64,32,128]{2,1,0:T(8,128)(2,1)S(1)} %collective-permute-done.4.refs_0_), channel_id=1, source_target_pairs={{0,1},{1,0},{2,3},{3,2},{4,5},{5,4},{6,7},{7,6},{8,9},{9,8},{10,11... | collective-permute-start | bytes 1572872 | tf_op jit(solution)/shard_map/near/ppermute | solution.py:176
  81.6 2.7 %collective-permute-start.9 = (bf16[64,32,128]{2,1,0:T(8,128)(2,1)S(1)}, bf16[64,32,128]{2,1,0:T(8,128)(2,1)S(1)}, u32[]{:S(2)}, u32[]{:S(2)}) collective-permute-start(bf16[64,32,128]{2,1,0:T(8,128)(2,1)S(1)} %collective-permute-done.5.refs_3_), channel_id=1, source_target_pairs={{0,6},{1,25},{2,0},{3,27},{4,2},{5,29},{6,4},{7,31},{8,14},{9,1},{... | collective-permute-start | bytes 1572872 | tf_op jit(solution)/shard_map/b2/ppermute | solution.py:180
  84.3 0.9 collective-permute-done.12.refs_1_
  85.2 1.5 %collective-permute-start.17 = (bf16[64,32,128]{2,1,0:T(8,128)(2,1)S(1)}, bf16[64,32,128]{2,1,0:T(8,128)(2,1)S(1)}, u32[]{:S(2)}, u32[]{:S(2)}) collective-permute-start(bf16[64,32,128]{2,1,0:T(8,128)(2,1)S(1)} %collective-permute-done.5.refs_3_), channel_id=1, source_target_pairs={{0,1},{1,0},{2,3},{3,2},{4,5},{5,4},{6,7},{7,6},{8,9},{9,8},{10,11... | collective-permute-start | bytes 1572872 | tf_op jit(solution)/shard_map/near/ppermute | solution.py:176
  87.3 4.3 %collective-permute-done.8.refs_0_ = bf16[64,32,128]{2,1,0:T(8,128)(2,1)S(1)} collective-permute-done((bf16[64,32,128]{2,1,0:T(8,128)(2,1)S(1)}, bf16[64,32,128]{2,1,0:T(8,128)(2,1)S(1)}, u32[]{:S(2)}, u32[]{:S(2)}) %collective-permute-start.8) | collective-permute-done | bytes 524320 | tf_op jit(solution)/shard_map/a2/ppermute | solution.py:180
  91.6 1.3 %collective-permute-start.10 = (bf16[64,32,128]{2,1,0:T(8,128)(2,1)S(1)}, bf16[64,32,128]{2,1,0:T(8,128)(2,1)S(1)}, u32[]{:S(2)}, u32[]{:S(2)}) collective-permute-start(bf16[64,32,128]{2,1,0:T(8,128)(2,1)S(1)} %collective-permute-done.8.refs_0_), channel_id=1, source_target_pairs={{0,1},{1,0},{2,3},{3,2},{4,5},{5,4},{6,7},{7,6},{8,9},{9,8},{10,11... | collective-permute-start | bytes 1572872 | tf_op jit(solution)/shard_map/far/ppermute | solution.py:176
  92.9 2.1 %join.4.refs_4_ = bf16[2,2,64,4,32,128]{5,4,3,2,1,0:T(8,128)(2,1)} custom-call(bf16[64,32,128]{2,1,0:T(8,128)(2,1)S(1)} %collective-permute-done.4.refs_0_, bf16[64,32,128]{2,1,0:T(8,128)(2,1)S(1)} %collective-permute-done.12.refs_1_, bf16[64,32,128]{2,1,0:T(8,128)(2,1)S(1)} %collective-permute-done.13.refs_2_, ...), custom_call_target="tpu_custom_call", output_to_operand_aliasing={{}: (8, {})} | custom-call | bytes 8388608 | tf_op jit(solution)/shard_map/join/pallas_call | solution.py:141
  95.1 1.3 %join.5 = bf16[2,2,64,4,32,128]{5,4,3,2,1,0:T(8,128)(2,1)} custom-call(bf16[64,32,128]{2,1,0:T(8,128)(2,1)S(1)} %collective-permute-done.8.refs_0_, bf16[64,32,128]{2,1,0:T(8,128)(2,1)S(1)} %collective-permute-done.9.refs_1_, bf16[64,32,128]{2,1,0:T(8,128)(2,1)S(1)} %collective-permute-done.10.refs_2_, ...), custom_call_target="tpu_custom_call", output_to_operand_aliasing={{}: (4, {})} | custom-call | bytes 4194304 | tf_op jit(solution)/shard_map/join/pallas_call | solution.py:141
  (30 shorter events, 5.1 us)
Async XLA Ops:
  3.3 33.2 %all-to-all-start = ((f32[128,8,128]{2,1,0:T(8,128)}), f32[128,8,128]{2,1,0:T(8,128)S(1)}, u32[]{:S(2)}, u32[]{:S(2)}) async-start(f32[128,8,128]{2,1,0:T(8,128)} %own_tiles.1), calls=%async_computation | async-start | bytes 1048576 | tf_op jit(solution)/shard_map/all_to_all | solution.py:162
  37.9 4.4 %collective-permute-start = (f32[128,128]{1,0:T(8,128)S(1)}, f32[128,128]{1,0:T(8,128)S(1)}, u32[]{:S(2)}, u32[]{:S(2)}) collective-permute-start(f32[128,128]{1,0:T(8,128)S(1)} %dynamic-slice_bitcast_fusion), channel_id=1, source_target_pairs={{0,1},{1,0},{2,3},{3,2},{4,5},{5,4},{6,7},{7,6},{8,9},{9,8},{10,11... | collective-permute-start | bytes 196616 | tf_op jit(solution)/shard_map/ppermute | solution.py:169
  56.4 6.7 %collective-permute-start.1 = (bf16[8,128,128]{2,1,0:T(8,128)(2,1)S(1)}, bf16[8,128,128]{2,1,0:T(8,128)(2,1)S(1)}, u32[]{:S(2)}, u32[]{:S(2)}) collective-permute-start(bf16[8,128,128]{2,1,0:T(8,128)(2,1)S(1)} %all_to_all.10.p0), channel_id=1, source_target_pairs={{0,8},{1,3},{2,10},{3,5},{4,12},{5,7},{6,14},{7,1},{8,16},{9,11},{... | collective-permute-start | bytes 786440 | tf_op jit(solution)/shard_map/s2/ppermute | solution.py:187
  56.7 8.5 %collective-permute-start.2 = (bf16[8,128,128]{2,1,0:T(8,128)(2,1)S(1)}, bf16[8,128,128]{2,1,0:T(8,128)(2,1)S(1)}, u32[]{:S(2)}, u32[]{:S(2)}) collective-permute-start(bf16[8,128,128]{2,1,0:T(8,128)(2,1)S(1)} %all_to_all.10.p0), channel_id=1, source_target_pairs={{0,24},{1,7},{2,26},{3,1},{4,28},{5,3},{6,30},{7,5},{8,0},{9,15},{... | collective-permute-start | bytes 786440 | tf_op jit(solution)/shard_map/s2/ppermute | solution.py:187
  59.1 7.0 %collective-permute-start.3 = (bf16[8,128,128]{2,1,0:T(8,128)(2,1)S(1)}, bf16[8,128,128]{2,1,0:T(8,128)(2,1)S(1)}, u32[]{:S(2)}, u32[]{:S(2)}) collective-permute-start(bf16[8,128,128]{2,1,0:T(8,128)(2,1)S(1)} %all_to_all.10.p0), channel_id=1, source_target_pairs={{0,16},{1,5},{2,18},{3,7},{4,20},{5,1},{6,22},{7,3},{8,24},{9,13},... | collective-permute-start | bytes 786440 | tf_op jit(solution)/shard_map/s2/ppermute | solution.py:187
  67.5 7.0 %collective-permute-start.6 = (bf16[64,32,128]{2,1,0:T(8,128)(2,1)S(1)}, bf16[64,32,128]{2,1,0:T(8,128)(2,1)S(1)}, u32[]{:S(2)}, u32[]{:S(2)}) collective-permute-start(bf16[64,32,128]{2,1,0:T(8,128)(2,1)S(1)} %get-tuple-element.10.refs_0_), channel_id=1, source_target_pairs={{0,1},{1,0},{2,3},{3,2},{4,5},{5,4},{6,7},{7,6},{8,9},{9,8},{10,11... | collective-permute-start | bytes 1572872 | tf_op jit(solution)/shard_map/own/ppermute | solution.py:176
  70.7 4.3 %collective-permute-start.7 = (bf16[64,32,128]{2,1,0:T(8,128)(2,1)S(1)}, bf16[64,32,128]{2,1,0:T(8,128)(2,1)S(1)}, u32[]{:S(2)}, u32[]{:S(2)}) collective-permute-start(bf16[64,32,128]{2,1,0:T(8,128)(2,1)S(1)} %get-tuple-element.11.refs_1_), channel_id=1, source_target_pairs={{0,1},{1,0},{2,3},{3,2},{4,5},{5,4},{6,7},{7,6},{8,9},{9,8},{10,11... | collective-permute-start | bytes 1572872 | tf_op jit(solution)/shard_map/own/ppermute | solution.py:176
  70.8 9.5 %collective-permute-start.4 = (bf16[64,32,128]{2,1,0:T(8,128)(2,1)S(1)}, bf16[64,32,128]{2,1,0:T(8,128)(2,1)S(1)}, u32[]{:S(2)}, u32[]{:S(2)}) collective-permute-start(bf16[64,32,128]{2,1,0:T(8,128)(2,1)S(1)} %get-tuple-element.10.refs_0_), channel_id=1, source_target_pairs={{0,2},{1,9},{2,4},{3,11},{4,6},{5,13},{6,0},{7,15},{8,10},{9,17},{... | collective-permute-start | bytes 1572872 | tf_op jit(solution)/shard_map/a1/ppermute | solution.py:180
  70.8 9.5 %collective-permute-start.5 = (bf16[64,32,128]{2,1,0:T(8,128)(2,1)S(1)}, bf16[64,32,128]{2,1,0:T(8,128)(2,1)S(1)}, u32[]{:S(2)}, u32[]{:S(2)}) collective-permute-start(bf16[64,32,128]{2,1,0:T(8,128)(2,1)S(1)} %get-tuple-element.11.refs_1_), channel_id=1, source_target_pairs={{0,6},{1,25},{2,0},{3,27},{4,2},{5,29},{6,4},{7,31},{8,14},{9,1},{... | collective-permute-start | bytes 1572872 | tf_op jit(solution)/shard_map/b3/ppermute | solution.py:180
  73.5 11.7 %collective-permute-start.12 = (bf16[64,32,128]{2,1,0:T(8,128)(2,1)S(1)}, bf16[64,32,128]{2,1,0:T(8,128)(2,1)S(1)}, u32[]{:S(2)}, u32[]{:S(2)}) collective-permute-start(bf16[64,32,128]{2,1,0:T(8,128)(2,1)S(1)} %get-tuple-element.10.refs_0_), channel_id=1, source_target_pairs={{0,6},{1,25},{2,0},{3,27},{4,2},{5,29},{6,4},{7,31},{8,14},{9,1},{... | collective-permute-start | bytes 1572872 | tf_op jit(solution)/shard_map/a3/ppermute | solution.py:180
  74.5 12.3 %collective-permute-start.13 = (bf16[64,32,128]{2,1,0:T(8,128)(2,1)S(1)}, bf16[64,32,128]{2,1,0:T(8,128)(2,1)S(1)}, u32[]{:S(2)}, u32[]{:S(2)}) collective-permute-start(bf16[64,32,128]{2,1,0:T(8,128)(2,1)S(1)} %get-tuple-element.11.refs_1_), channel_id=1, source_target_pairs={{0,2},{1,9},{2,4},{3,11},{4,6},{5,13},{6,0},{7,15},{8,10},{9,17},{... | collective-permute-start | bytes 1572872 | tf_op jit(solution)/shard_map/b1/ppermute | solution.py:180
  80.3 6.9 %collective-permute-start.14 = (bf16[64,32,128]{2,1,0:T(8,128)(2,1)S(1)}, bf16[64,32,128]{2,1,0:T(8,128)(2,1)S(1)}, u32[]{:S(2)}, u32[]{:S(2)}) collective-permute-start(bf16[64,32,128]{2,1,0:T(8,128)(2,1)S(1)} %collective-permute-done.4.refs_0_), channel_id=1, source_target_pairs={{0,1},{1,0},{2,3},{3,2},{4,5},{5,4},{6,7},{7,6},{8,9},{9,8},{10,11... | collective-permute-start | bytes 1572872 | tf_op jit(solution)/shard_map/near/ppermute | solution.py:176
  81.6 10.0 %collective-permute-start.8 = (bf16[64,32,128]{2,1,0:T(8,128)(2,1)S(1)}, bf16[64,32,128]{2,1,0:T(8,128)(2,1)S(1)}, u32[]{:S(2)}, u32[]{:S(2)}) collective-permute-start(bf16[64,32,128]{2,1,0:T(8,128)(2,1)S(1)} %collective-permute-done.4.refs_0_), channel_id=1, source_target_pairs={{0,2},{1,9},{2,4},{3,11},{4,6},{5,13},{6,0},{7,15},{8,10},{9,17},{... | collective-permute-start | bytes 1572872 | tf_op jit(solution)/shard_map/a2/ppermute | solution.py:180
  81.6 11.2 %collective-permute-start.9 = (bf16[64,32,128]{2,1,0:T(8,128)(2,1)S(1)}, bf16[64,32,128]{2,1,0:T(8,128)(2,1)S(1)}, u32[]{:S(2)}, u32[]{:S(2)}) collective-permute-start(bf16[64,32,128]{2,1,0:T(8,128)(2,1)S(1)} %collective-permute-done.5.refs_3_), channel_id=1, source_target_pairs={{0,6},{1,25},{2,0},{3,27},{4,2},{5,29},{6,4},{7,31},{8,14},{9,1},{... | collective-permute-start | bytes 1572872 | tf_op jit(solution)/shard_map/b2/ppermute | solution.py:180
  85.2 7.6 %collective-permute-start.17 = (bf16[64,32,128]{2,1,0:T(8,128)(2,1)S(1)}, bf16[64,32,128]{2,1,0:T(8,128)(2,1)S(1)}, u32[]{:S(2)}, u32[]{:S(2)}) collective-permute-start(bf16[64,32,128]{2,1,0:T(8,128)(2,1)S(1)} %collective-permute-done.5.refs_3_), channel_id=1, source_target_pairs={{0,1},{1,0},{2,3},{3,2},{4,5},{5,4},{6,7},{7,6},{8,9},{9,8},{10,11... | collective-permute-start | bytes 1572872 | tf_op jit(solution)/shard_map/near/ppermute | solution.py:176
  86.8 6.1 %collective-permute-start.15 = (bf16[64,32,128]{2,1,0:T(8,128)(2,1)S(1)}, bf16[64,32,128]{2,1,0:T(8,128)(2,1)S(1)}, u32[]{:S(2)}, u32[]{:S(2)}) collective-permute-start(bf16[64,32,128]{2,1,0:T(8,128)(2,1)S(1)} %collective-permute-done.12.refs_1_), channel_id=1, source_target_pairs={{0,1},{1,0},{2,3},{3,2},{4,5},{5,4},{6,7},{7,6},{8,9},{9,8},{10,11... | collective-permute-start | bytes 1572872 | tf_op jit(solution)/shard_map/near/ppermute | solution.py:176
  87.2 5.6 %collective-permute-start.16 = (bf16[64,32,128]{2,1,0:T(8,128)(2,1)S(1)}, bf16[64,32,128]{2,1,0:T(8,128)(2,1)S(1)}, u32[]{:S(2)}, u32[]{:S(2)}) collective-permute-start(bf16[64,32,128]{2,1,0:T(8,128)(2,1)S(1)} %collective-permute-done.13.refs_2_), channel_id=1, source_target_pairs={{0,1},{1,0},{2,3},{3,2},{4,5},{5,4},{6,7},{7,6},{8,9},{9,8},{10,11... | collective-permute-start | bytes 1572872 | tf_op jit(solution)/shard_map/near/ppermute | solution.py:176
  91.6 3.4 %collective-permute-start.10 = (bf16[64,32,128]{2,1,0:T(8,128)(2,1)S(1)}, bf16[64,32,128]{2,1,0:T(8,128)(2,1)S(1)}, u32[]{:S(2)}, u32[]{:S(2)}) collective-permute-start(bf16[64,32,128]{2,1,0:T(8,128)(2,1)S(1)} %collective-permute-done.8.refs_0_), channel_id=1, source_target_pairs={{0,1},{1,0},{2,3},{3,2},{4,5},{5,4},{6,7},{7,6},{8,9},{9,8},{10,11... | collective-permute-start | bytes 1572872 | tf_op jit(solution)/shard_map/far/ppermute | solution.py:176
  92.8 2.3 %collective-permute-start.11 = (bf16[64,32,128]{2,1,0:T(8,128)(2,1)S(1)}, bf16[64,32,128]{2,1,0:T(8,128)(2,1)S(1)}, u32[]{:S(2)}, u32[]{:S(2)}) collective-permute-start(bf16[64,32,128]{2,1,0:T(8,128)(2,1)S(1)} %collective-permute-done.9.refs_1_), channel_id=1, source_target_pairs={{0,1},{1,0},{2,3},{3,2},{4,5},{5,4},{6,7},{7,6},{8,9},{9,8},{10,11... | collective-permute-start | bytes 1572872 | tf_op jit(solution)/shard_map/far/ppermute | solution.py:176

commit v5 on v4

--- a/solution.py
+++ b/solution.py
@@ -16,9 +16,10 @@
 CHIPS = 128
 HALF = 128
 HALF_TILES = 512
+REGION = 4
 MIB = 1024 * 1024
 PART = 64
-STEPS = (0, 1, 3, 2)
+STEPS = (0, 2, 1, 3)
 
 
 def dev(z, y, x, c):
@@ -94,6 +95,31 @@
     )(kept, activations, cotangent)
 
 
+def sum_kernel(region_ref, got_ref, mine_ref, theirs_ref):
+    core = lax.axis_index("dp") % CN
+    rest = got_ref[...]
+    parts = []
+    for _ in range(3):
+        parts.append(rest.astype(jnp.bfloat16))
+        rest = rest - parts[-1].astype(jnp.float32)
+    for ref, half in ((theirs_ref, 1 - core), (mine_ref, core)):
+        tiles = lax.broadcasted_iota(jnp.int32, (HALF, CHIPS * KEPT), 0) + half * HALF
+        match = (tiles == region_ref[...]).astype(jnp.float32).astype(jnp.bfloat16)
+        sums = [jnp.dot(match, part, preferred_element_type=jnp.float32) for part in parts]
+        ref[...] = (sums[2] + sums[1]) + sums[0]
+
+
+def sum_tiles(region, got):
+    return pl.pallas_call(
+        sum_kernel,
+        out_shape=[jax.ShapeDtypeStruct((HALF, TILE), jnp.float32)] * 2,
+        in_specs=[pl.BlockSpec(memory_space=pltpu.VMEM)] * 2,
+        out_specs=[pl.BlockSpec(memory_space=pltpu.VMEM)] * 2,
+        compiler_params=pltpu.CompilerParams(vmem_limit_bytes=16 * MIB),
+        name="sum_tiles",
+    )(region, got)
+
+
 def rows_kernel(p0, p1, p2, p3, a_ref, b_ref, wide):
     at = spot()[1]
     for step, piece in zip(STEPS, (p0, p1, p2, p3)):
@@ -156,16 +182,12 @@
     core = me % CN
     sent = own_tiles(kept_tiles.T, activations, cotangent)
     live = jnp.arange(KEPT, dtype=jnp.int32)[None, :] < kept_counts[:, None]
-    ids = jnp.where(live, kept_tiles, -1).reshape(ZN, YN, XN, CN, KEPT)
-    ids = lax.dynamic_index_in_dim(ids, core, 3, keepdims=False)
-    ids = ids.transpose(1, 0, 2, 3).reshape(CHIPS * KEPT)
+    hit = jnp.any(kept_tiles[:, :, None] == chosen[None, None, :], axis=-1)
+    region = jnp.where(live & hit, kept_tiles // REGION, -1).reshape(ZN, YN, XN, CN, KEPT)
+    region = lax.dynamic_index_in_dim(region, core, 3, keepdims=False)
+    region = region.transpose(1, 0, 2, 3).reshape(1, CHIPS * KEPT)
     got = lax.all_to_all(sent, "dp", 0, 0, axis_index_groups=CHIP_GROUPS, tiled=True)
-
-    match = (chosen[:, None] == ids[None, :]).astype(jnp.float32)
-    part = jnp.dot(match, got.reshape(CHIPS * KEPT, TILE), precision=lax.Precision.HIGHEST)
-    part = part.reshape(CN, HALF, TILE)
-    mine = lax.dynamic_index_in_dim(part, core, 0, keepdims=False)
-    theirs = lax.dynamic_index_in_dim(part, 1 - core, 0, keepdims=False)
+    mine, theirs = sum_tiles(region, got.reshape(CHIPS * KEPT, TILE))
     row = (mine + lax.ppermute(theirs, "dp", SWAP)).astype(jnp.bfloat16)
 
     rows = lax.all_to_all(

time: 97 us -> 95.8 us (0.988)
  waiting for transfers between devices: 31.5 us -> 25 us
  other arithmetic: 0.79 us -> 6.17 us
  matrix products: 1.33 us -> 0 us
    all_to_all x1, waiting for transfers between devices: 15 us -> 9.58 us  [local(): lax.all_to_all(sent, 'dp', 0, 0, axis_index_groups=CHIP_GROUPS, tiled=True)]
    reduce_or x0 -> x1, other arithmetic: none -> 5.38 us  [local(): hit = jnp.any(kept_tiles[:, :, None] == chosen[None, None, :], axis=-1)]
    dot_general x1 -> x0, matrix products: 1.33 us -> none  [local(): jnp.dot(match, got.reshape(CHIPS * KEPT, TILE), precision=lax.Precision.H...]
    ppermute x3, starting transfers between devices: 3.5 us -> 4.71 us  [local(): pieces = [rows] + [lax.ppermute(rows, 'dp', ring(s, 0)) for s in STEPS[1:]]]
    ppermute x3, waiting for transfers between devices: 6.19 us -> 5.12 us  [local(): pieces = [rows] + [lax.ppermute(rows, 'dp', ring(s, 0)) for s in STEPS[1:]]]
  transfers between devices with their start and end apart: 19 -> 19, of which waited for: 9 -> 8; matrix products, arithmetic and copies ran while one was open for 2% -> 8% of each run, Pallas kernels for 4% -> 4%
where the time goes in v5:
time: 95.8 us; the launch traced here: 95.4 us
  starting transfers between devices  38.7 us (40%)
  waiting for transfers between devices  25 us (26%)
  blocking collectives  14 us (15%)
  Pallas kernels  10.1 us (11%)
  other arithmetic  6.17 us (6%)
  local copies, waits for them, and re-layouts  1.08 us (1%)
    all_to_all x1, starting transfers between devices, local(): lax.all_to_all(sent, 'dp', 0, 0, axis_index_groups=CHIP_GROUPS, tiled=True)  16.3 us
    all_to_all x1, blocking collectives, local(): lax.all_to_all(jnp.broadcast_to(row[None], (ZN, HALF, TILE)), 'dp', 0, 0,...  14 us
    all_to_all x1, waiting for transfers between devices, local(): lax.all_to_all(sent, 'dp', 0, 0, axis_index_groups=CHIP_GROUPS, tiled=True)  9.58 us
    ppermute x6, waiting for transfers between devices, send(): return lax.ppermute(block, 'dp', ring(step, 1))  9.27 us
    ppermute x8, starting transfers between devices, swap(): return [lax.ppermute(b, 'dp', SWAP) for b in blocks]  7.29 us
    ppermute x6, starting transfers between devices, send(): return lax.ppermute(block, 'dp', ring(step, 1))  6.82 us
    reduce_or x1, other arithmetic, local(): hit = jnp.any(kept_tiles[:, :, None] == chosen[None, None, :], axis=-1)  5.38 us
    ppermute x3, waiting for transfers between devices, local(): pieces = [rows] + [lax.ppermute(rows, 'dp', ring(s, 0)) for s in STEPS[1:]]  5.12 us
  transfers between devices with their start and end apart: 19, of which 8 were waited for; matrix products, arithmetic and copies ran while one was open for 8% of the time, Pallas kernels for 4%

profile of v5, /device:TPU:1, one launch (start us, length us, event | category | flops | bytes accessed | tf_op | source)
XLA Modules:
  0.0 95.4 jit_solution(10788216955620092584)
XLA Ops:
  0.0 3.3 %own_tiles.1 = f32[128,8,128]{2,1,0:T(8,128)} custom-call(s32[8,256]{1,0:T(8,128)} %bitcast.12, bf16[128,8192]{1,0:T(8,128)(2,1)} %act_ref.1, bf16[128,2048]{1,0:T(8,128)(2,1)} %cot_ref.1), custom_call_target="tpu_custom_call" | custom-call | tf_op jit(solution)/shard_map/own_tiles/pallas_call | solution.py:78
  3.3 16.3 %all-to-all-start = ((f32[128,8,128]{2,1,0:T(8,128)}), f32[128,8,128]{2,1,0:T(8,128)S(1)}, u32[]{:S(2)}, u32[]{:S(2)}) async-start(f32[128,8,128]{2,1,0:T(8,128)} %own_tiles.1), calls=%async_computation | async-start | bytes 1048576 | tf_op jit(solution)/shard_map/all_to_all | solution.py:189
  20.5 5.4 %compare_reduce_fusion = pred[256,8]{1,0:T(8,128)(4,1)S(1)} fusion(s32[256]{0:T(256)} %param.9, s32[256,8]{1,0:T(8,128)S(1)} %copy.22), kind=kLoop, calls=%fused_computation | loop fusion | flops 1046528 | bytes 11264 | tf_op jit(solution)/shard_map/reduce_or | solution.py:185
  26.9 9.6 %all-to-all-done = f32[128,8,128]{2,1,0:T(8,128)S(1)} async-done(((f32[128,8,128]{2,1,0:T(8,128)}), f32[128,8,128]{2,1,0:T(8,128)S(1)}, u32[]{:S(2)}, u32[]{:S(2)}) %all-to-all-start) | async-done | bytes 524320 | tf_op jit(solution)/shard_map/all_to_all | solution.py:189
  37.1 3.5 %collective-permute-start = (f32[128,128]{1,0:T(8,128)S(1)}, f32[128,128]{1,0:T(8,128)S(1)}, u32[]{:S(2)}, u32[]{:S(2)}) collective-permute-start(f32[128,128]{1,0:T(8,128)S(1)} %get-tuple-element.13), channel_id=1, source_target_pairs={{0,1},{1,0},{2,3},{3,2},{4,5},{5,4},{6,7},{7,6},{8,9},{9,8},{10,11... | collective-permute-start | bytes 196616 | tf_op jit(solution)/shard_map/ppermute | solution.py:191
  41.6 14.0 %all_to_all.10.p0 = bf16[8,128,128]{2,1,0:T(8,128)(2,1)S(1)} all-to-all(bf16[8,128,128]{2,1,0:T(8,128)(2,1)S(1)} %broadcast_in_dim.3), channel_id=1, replica_groups={{0,32,64,96,128,160,192,224},{1,33,65,97,129,161,193,225},{2,34,66,98,1..., dimensions={0} | all-to-all | bytes 524288 | tf_op jit(solution)/shard_map/all_to_all | solution.py:193
  55.6 2.0 %collective-permute-start.1 = (bf16[8,128,128]{2,1,0:T(8,128)(2,1)S(1)}, bf16[8,128,128]{2,1,0:T(8,128)(2,1)S(1)}, u32[]{:S(2)}, u32[]{:S(2)}) collective-permute-start(bf16[8,128,128]{2,1,0:T(8,128)(2,1)S(1)} %all_to_all.10.p0), channel_id=1, source_target_pairs={{0,16},{1,5},{2,18},{3,7},{4,20},{5,1},{6,22},{7,3},{8,24},{9,13},... | collective-permute-start | bytes 786440 | tf_op jit(solution)/shard_map/s2/ppermute | solution.py:209
  57.7 2.7 %collective-permute-start.3 = (bf16[8,128,128]{2,1,0:T(8,128)(2,1)S(1)}, bf16[8,128,128]{2,1,0:T(8,128)(2,1)S(1)}, u32[]{:S(2)}, u32[]{:S(2)}) collective-permute-start(bf16[8,128,128]{2,1,0:T(8,128)(2,1)S(1)} %all_to_all.10.p0), channel_id=1, source_target_pairs={{0,24},{1,7},{2,26},{3,1},{4,28},{5,3},{6,30},{7,5},{8,0},{9,15},{... | collective-permute-start | bytes 786440 | tf_op jit(solution)/shard_map/s2/ppermute | solution.py:209
  60.3 2.3 %collective-permute-done.1.p1 = bf16[8,128,128]{2,1,0:T(8,128)(2,1)S(1)} collective-permute-done((bf16[8,128,128]{2,1,0:T(8,128)(2,1)S(1)}, bf16[8,128,128]{2,1,0:T(8,128)(2,1)S(1)}, u32[]{:S(2)}, u32[]{:S(2)}) %collective-permute-start.1) | collective-permute-done | bytes 262176 | tf_op jit(solution)/shard_map/s2/ppermute | solution.py:209
  62.6 2.8 %collective-permute-done.2.p2 = bf16[8,128,128]{2,1,0:T(8,128)(2,1)S(1)} collective-permute-done((bf16[8,128,128]{2,1,0:T(8,128)(2,1)S(1)}, bf16[8,128,128]{2,1,0:T(8,128)(2,1)S(1)}, u32[]{:S(2)}, u32[]{:S(2)}) %collective-permute-start.2) | collective-permute-done | bytes 262176 | tf_op jit(solution)/shard_map/s2/ppermute | solution.py:209
  65.4 1.4 %by_rows.1 = (bf16[64,32,128]{2,1,0:T(8,128)(2,1)S(1)}, bf16[64,32,128]{2,1,0:T(8,128)(2,1)S(1)}) custom-call(bf16[8,128,128]{2,1,0:T(8,128)(2,1)S(1)} %all_to_all.10.p0, bf16[8,128,128]{2,1,0:T(8,128)(2,1)S(1)} %collective-permute-done.1.p1, bf16[8,128,128]{2,1,0:T(8,128)(2,1)S(1)} %collective-permute-done.2.p2, ...), custom_call_target="tpu_custom_call" | custom-call | tf_op jit(solution)/shard_map/by_rows/pallas_call | solution.py:139
  66.9 2.6 %collective-permute-start.6 = (bf16[64,32,128]{2,1,0:T(8,128)(2,1)S(1)}, bf16[64,32,128]{2,1,0:T(8,128)(2,1)S(1)}, u32[]{:S(2)}, u32[]{:S(2)}) collective-permute-start(bf16[64,32,128]{2,1,0:T(8,128)(2,1)S(1)} %get-tuple-element.14.refs_0_), channel_id=1, source_target_pairs={{0,1},{1,0},{2,3},{3,2},{4,5},{5,4},{6,7},{7,6},{8,9},{9,8},{10,11... | collective-permute-start | bytes 1572872 | tf_op jit(solution)/shard_map/own/ppermute | solution.py:198
  70.1 2.2 %collective-permute-start.5 = (bf16[64,32,128]{2,1,0:T(8,128)(2,1)S(1)}, bf16[64,32,128]{2,1,0:T(8,128)(2,1)S(1)}, u32[]{:S(2)}, u32[]{:S(2)}) collective-permute-start(bf16[64,32,128]{2,1,0:T(8,128)(2,1)S(1)} %get-tuple-element.15.refs_1_), channel_id=1, source_target_pairs={{0,6},{1,25},{2,0},{3,27},{4,2},{5,29},{6,4},{7,31},{8,14},{9,1},{... | collective-permute-start | bytes 1572872 | tf_op jit(solution)/shard_map/b3/ppermute | solution.py:202
  72.3 1.4 %collective-permute-start.13 = (bf16[64,32,128]{2,1,0:T(8,128)(2,1)S(1)}, bf16[64,32,128]{2,1,0:T(8,128)(2,1)S(1)}, u32[]{:S(2)}, u32[]{:S(2)}) collective-permute-start(bf16[64,32,128]{2,1,0:T(8,128)(2,1)S(1)} %get-tuple-element.15.refs_1_), channel_id=1, source_target_pairs={{0,2},{1,9},{2,4},{3,11},{4,6},{5,13},{6,0},{7,15},{8,10},{9,17},{... | collective-permute-start | bytes 1572872 | tf_op jit(solution)/shard_map/b1/ppermute | solution.py:202
  73.7 1.3 %join.3.refs_8_ = bf16[2,2,64,4,32,128]{5,4,3,2,1,0:T(8,128)(2,1)} custom-call(bf16[64,32,128]{2,1,0:T(8,128)(2,1)S(1)} %get-tuple-element.14.refs_0_, bf16[64,32,128]{2,1,0:T(8,128)(2,1)S(1)} %get-tuple-element.15.refs_1_, bf16[64,32,128]{2,1,0:T(8,128)(2,1)S(1)} %collective-permute-done.6.refs_2_, bf16[64,32,128]{2,1,0:T(8,128)(2,1)S(1)} %collective-permute-done.7.refs_3_), custom_call_target="tpu_custom_call" | custom-call | bytes 4194304 | tf_op jit(solution)/shard_map/join/pallas_call | solution.py:167
  75.1 4.0 %collective-permute-done.4.refs_0_ = bf16[64,32,128]{2,1,0:T(8,128)(2,1)S(1)} collective-permute-done((bf16[64,32,128]{2,1,0:T(8,128)(2,1)S(1)}, bf16[64,32,128]{2,1,0:T(8,128)(2,1)S(1)}, u32[]{:S(2)}, u32[]{:S(2)}) %collective-permute-start.4) | collective-permute-done | bytes 524320 | tf_op jit(solution)/shard_map/a1/ppermute | solution.py:202
  79.1 1.3 %collective-permute-start.14 = (bf16[64,32,128]{2,1,0:T(8,128)(2,1)S(1)}, bf16[64,32,128]{2,1,0:T(8,128)(2,1)S(1)}, u32[]{:S(2)}, u32[]{:S(2)}) collective-permute-start(bf16[64,32,128]{2,1,0:T(8,128)(2,1)S(1)} %collective-permute-done.4.refs_0_), channel_id=1, source_target_pairs={{0,1},{1,0},{2,3},{3,2},{4,5},{5,4},{6,7},{7,6},{8,9},{9,8},{10,11... | collective-permute-start | bytes 1572872 | tf_op jit(solution)/shard_map/near/ppermute | solution.py:198
  80.9 2.2 %collective-permute-start.9 = (bf16[64,32,128]{2,1,0:T(8,128)(2,1)S(1)}, bf16[64,32,128]{2,1,0:T(8,128)(2,1)S(1)}, u32[]{:S(2)}, u32[]{:S(2)}) collective-permute-start(bf16[64,32,128]{2,1,0:T(8,128)(2,1)S(1)} %collective-permute-done.5.refs_3_), channel_id=1, source_target_pairs={{0,6},{1,25},{2,0},{3,27},{4,2},{5,29},{6,4},{7,31},{8,14},{9,1},{... | collective-permute-start | bytes 1572872 | tf_op jit(solution)/shard_map/b2/ppermute | solution.py:202
  83.1 0.9 collective-permute-done.12.refs_1_
  84.0 1.5 %collective-permute-start.17 = (bf16[64,32,128]{2,1,0:T(8,128)(2,1)S(1)}, bf16[64,32,128]{2,1,0:T(8,128)(2,1)S(1)}, u32[]{:S(2)}, u32[]{:S(2)}) collective-permute-start(bf16[64,32,128]{2,1,0:T(8,128)(2,1)S(1)} %collective-permute-done.5.refs_3_), channel_id=1, source_target_pairs={{0,1},{1,0},{2,3},{3,2},{4,5},{5,4},{6,7},{7,6},{8,9},{9,8},{10,11... | collective-permute-start | bytes 1572872 | tf_op jit(solution)/shard_map/near/ppermute | solution.py:198
  86.1 4.3 %collective-permute-done.8.refs_0_ = bf16[64,32,128]{2,1,0:T(8,128)(2,1)S(1)} collective-permute-done((bf16[64,32,128]{2,1,0:T(8,128)(2,1)S(1)}, bf16[64,32,128]{2,1,0:T(8,128)(2,1)S(1)}, u32[]{:S(2)}, u32[]{:S(2)}) %collective-permute-start.8) | collective-permute-done | bytes 524320 | tf_op jit(solution)/shard_map/a2/ppermute | solution.py:202
  90.4 1.3 %collective-permute-start.10 = (bf16[64,32,128]{2,1,0:T(8,128)(2,1)S(1)}, bf16[64,32,128]{2,1,0:T(8,128)(2,1)S(1)}, u32[]{:S(2)}, u32[]{:S(2)}) collective-permute-start(bf16[64,32,128]{2,1,0:T(8,128)(2,1)S(1)} %collective-permute-done.8.refs_0_), channel_id=1, source_target_pairs={{0,1},{1,0},{2,3},{3,2},{4,5},{5,4},{6,7},{7,6},{8,9},{9,8},{10,11... | collective-permute-start | bytes 1572872 | tf_op jit(solution)/shard_map/far/ppermute | solution.py:198
  91.7 2.1 %join.4.refs_4_ = bf16[2,2,64,4,32,128]{5,4,3,2,1,0:T(8,128)(2,1)} custom-call(bf16[64,32,128]{2,1,0:T(8,128)(2,1)S(1)} %collective-permute-done.4.refs_0_, bf16[64,32,128]{2,1,0:T(8,128)(2,1)S(1)} %collective-permute-done.12.refs_1_, bf16[64,32,128]{2,1,0:T(8,128)(2,1)S(1)} %collective-permute-done.13.refs_2_, ...), custom_call_target="tpu_custom_call", output_to_operand_aliasing={{}: (8, {})} | custom-call | bytes 8388608 | tf_op jit(solution)/shard_map/join/pallas_call | solution.py:167
  93.9 1.3 %join.5 = bf16[2,2,64,4,32,128]{5,4,3,2,1,0:T(8,128)(2,1)} custom-call(bf16[64,32,128]{2,1,0:T(8,128)(2,1)S(1)} %collective-permute-done.8.refs_0_, bf16[64,32,128]{2,1,0:T(8,128)(2,1)S(1)} %collective-permute-done.9.refs_1_, bf16[64,32,128]{2,1,0:T(8,128)(2,1)S(1)} %collective-permute-done.10.refs_2_, ...), custom_call_target="tpu_custom_call", output_to_operand_aliasing={{}: (4, {})} | custom-call | bytes 4194304 | tf_op jit(solution)/shard_map/join/pallas_call | solution.py:167
  (30 shorter events, 5.1 us)
Async XLA Ops:
  3.3 33.2 %all-to-all-start = ((f32[128,8,128]{2,1,0:T(8,128)}), f32[128,8,128]{2,1,0:T(8,128)S(1)}, u32[]{:S(2)}, u32[]{:S(2)}) async-start(f32[128,8,128]{2,1,0:T(8,128)} %own_tiles.1), calls=%async_computation | async-start | bytes 1048576 | tf_op jit(solution)/shard_map/all_to_all | solution.py:189
  37.1 4.4 %collective-permute-start = (f32[128,128]{1,0:T(8,128)S(1)}, f32[128,128]{1,0:T(8,128)S(1)}, u32[]{:S(2)}, u32[]{:S(2)}) collective-permute-start(f32[128,128]{1,0:T(8,128)S(1)} %get-tuple-element.13), channel_id=1, source_target_pairs={{0,1},{1,0},{2,3},{3,2},{4,5},{5,4},{6,7},{7,6},{8,9},{9,8},{10,11... | collective-permute-start | bytes 196616 | tf_op jit(solution)/shard_map/ppermute | solution.py:191
  55.6 7.0 %collective-permute-start.1 = (bf16[8,128,128]{2,1,0:T(8,128)(2,1)S(1)}, bf16[8,128,128]{2,1,0:T(8,128)(2,1)S(1)}, u32[]{:S(2)}, u32[]{:S(2)}) collective-permute-start(bf16[8,128,128]{2,1,0:T(8,128)(2,1)S(1)} %all_to_all.10.p0), channel_id=1, source_target_pairs={{0,16},{1,5},{2,18},{3,7},{4,20},{5,1},{6,22},{7,3},{8,24},{9,13},... | collective-permute-start | bytes 786440 | tf_op jit(solution)/shard_map/s2/ppermute | solution.py:209
  57.6 7.8 %collective-permute-start.2 = (bf16[8,128,128]{2,1,0:T(8,128)(2,1)S(1)}, bf16[8,128,128]{2,1,0:T(8,128)(2,1)S(1)}, u32[]{:S(2)}, u32[]{:S(2)}) collective-permute-start(bf16[8,128,128]{2,1,0:T(8,128)(2,1)S(1)} %all_to_all.10.p0), channel_id=1, source_target_pairs={{0,8},{1,3},{2,10},{3,5},{4,12},{5,7},{6,14},{7,1},{8,16},{9,11},{... | collective-permute-start | bytes 786440 | tf_op jit(solution)/shard_map/s2/ppermute | solution.py:209
  57.7 7.8 %collective-permute-start.3 = (bf16[8,128,128]{2,1,0:T(8,128)(2,1)S(1)}, bf16[8,128,128]{2,1,0:T(8,128)(2,1)S(1)}, u32[]{:S(2)}, u32[]{:S(2)}) collective-permute-start(bf16[8,128,128]{2,1,0:T(8,128)(2,1)S(1)} %all_to_all.10.p0), channel_id=1, source_target_pairs={{0,24},{1,7},{2,26},{3,1},{4,28},{5,3},{6,30},{7,5},{8,0},{9,15},{... | collective-permute-start | bytes 786440 | tf_op jit(solution)/shard_map/s2/ppermute | solution.py:209
  66.9 5.4 %collective-permute-start.6 = (bf16[64,32,128]{2,1,0:T(8,128)(2,1)S(1)}, bf16[64,32,128]{2,1,0:T(8,128)(2,1)S(1)}, u32[]{:S(2)}, u32[]{:S(2)}) collective-permute-start(bf16[64,32,128]{2,1,0:T(8,128)(2,1)S(1)} %get-tuple-element.14.refs_0_), channel_id=1, source_target_pairs={{0,1},{1,0},{2,3},{3,2},{4,5},{5,4},{6,7},{7,6},{8,9},{9,8},{10,11... | collective-permute-start | bytes 1572872 | tf_op jit(solution)/shard_map/own/ppermute | solution.py:198
  69.5 4.3 %collective-permute-start.7 = (bf16[64,32,128]{2,1,0:T(8,128)(2,1)S(1)}, bf16[64,32,128]{2,1,0:T(8,128)(2,1)S(1)}, u32[]{:S(2)}, u32[]{:S(2)}) collective-permute-start(bf16[64,32,128]{2,1,0:T(8,128)(2,1)S(1)} %get-tuple-element.15.refs_1_), channel_id=1, source_target_pairs={{0,1},{1,0},{2,3},{3,2},{4,5},{5,4},{6,7},{7,6},{8,9},{9,8},{10,11... | collective-permute-start | bytes 1572872 | tf_op jit(solution)/shard_map/own/ppermute | solution.py:198
  69.6 9.5 %collective-permute-start.4 = (bf16[64,32,128]{2,1,0:T(8,128)(2,1)S(1)}, bf16[64,32,128]{2,1,0:T(8,128)(2,1)S(1)}, u32[]{:S(2)}, u32[]{:S(2)}) collective-permute-start(bf16[64,32,128]{2,1,0:T(8,128)(2,1)S(1)} %get-tuple-element.14.refs_0_), channel_id=1, source_target_pairs={{0,2},{1,9},{2,4},{3,11},{4,6},{5,13},{6,0},{7,15},{8,10},{9,17},{... | collective-permute-start | bytes 1572872 | tf_op jit(solution)/shard_map/a1/ppermute | solution.py:202
  70.1 9.1 %collective-permute-start.5 = (bf16[64,32,128]{2,1,0:T(8,128)(2,1)S(1)}, bf16[64,32,128]{2,1,0:T(8,128)(2,1)S(1)}, u32[]{:S(2)}, u32[]{:S(2)}) collective-permute-start(bf16[64,32,128]{2,1,0:T(8,128)(2,1)S(1)} %get-tuple-element.15.refs_1_), channel_id=1, source_target_pairs={{0,6},{1,25},{2,0},{3,27},{4,2},{5,29},{6,4},{7,31},{8,14},{9,1},{... | collective-permute-start | bytes 1572872 | tf_op jit(solution)/shard_map/b3/ppermute | solution.py:202
  72.3 11.8 %collective-permute-start.12 = (bf16[64,32,128]{2,1,0:T(8,128)(2,1)S(1)}, bf16[64,32,128]{2,1,0:T(8,128)(2,1)S(1)}, u32[]{:S(2)}, u32[]{:S(2)}) collective-permute-start(bf16[64,32,128]{2,1,0:T(8,128)(2,1)S(1)} %get-tuple-element.14.refs_0_), channel_id=1, source_target_pairs={{0,6},{1,25},{2,0},{3,27},{4,2},{5,29},{6,4},{7,31},{8,14},{9,1},{... | collective-permute-start | bytes 1572872 | tf_op jit(solution)/shard_map/a3/ppermute | solution.py:202
  72.3 13.3 %collective-permute-start.13 = (bf16[64,32,128]{2,1,0:T(8,128)(2,1)S(1)}, bf16[64,32,128]{2,1,0:T(8,128)(2,1)S(1)}, u32[]{:S(2)}, u32[]{:S(2)}) collective-permute-start(bf16[64,32,128]{2,1,0:T(8,128)(2,1)S(1)} %get-tuple-element.15.refs_1_), channel_id=1, source_target_pairs={{0,2},{1,9},{2,4},{3,11},{4,6},{5,13},{6,0},{7,15},{8,10},{9,17},{... | collective-permute-start | bytes 1572872 | tf_op jit(solution)/shard_map/b1/ppermute | solution.py:202
  79.1 6.9 %collective-permute-start.14 = (bf16[64,32,128]{2,1,0:T(8,128)(2,1)S(1)}, bf16[64,32,128]{2,1,0:T(8,128)(2,1)S(1)}, u32[]{:S(2)}, u32[]{:S(2)}) collective-permute-start(bf16[64,32,128]{2,1,0:T(8,128)(2,1)S(1)} %collective-permute-done.4.refs_0_), channel_id=1, source_target_pairs={{0,1},{1,0},{2,3},{3,2},{4,5},{5,4},{6,7},{7,6},{8,9},{9,8},{10,11... | collective-permute-start | bytes 1572872 | tf_op jit(solution)/shard_map/near/ppermute | solution.py:198
  80.4 10.0 %collective-permute-start.8 = (bf16[64,32,128]{2,1,0:T(8,128)(2,1)S(1)}, bf16[64,32,128]{2,1,0:T(8,128)(2,1)S(1)}, u32[]{:S(2)}, u32[]{:S(2)}) collective-permute-start(bf16[64,32,128]{2,1,0:T(8,128)(2,1)S(1)} %collective-permute-done.4.refs_0_), channel_id=1, source_target_pairs={{0,2},{1,9},{2,4},{3,11},{4,6},{5,13},{6,0},{7,15},{8,10},{9,17},{... | collective-permute-start | bytes 1572872 | tf_op jit(solution)/shard_map/a2/ppermute | solution.py:202
  80.9 10.7 %collective-permute-start.9 = (bf16[64,32,128]{2,1,0:T(8,128)(2,1)S(1)}, bf16[64,32,128]{2,1,0:T(8,128)(2,1)S(1)}, u32[]{:S(2)}, u32[]{:S(2)}) collective-permute-start(bf16[64,32,128]{2,1,0:T(8,128)(2,1)S(1)} %collective-permute-done.5.refs_3_), channel_id=1, source_target_pairs={{0,6},{1,25},{2,0},{3,27},{4,2},{5,29},{6,4},{7,31},{8,14},{9,1},{... | collective-permute-start | bytes 1572872 | tf_op jit(solution)/shard_map/b2/ppermute | solution.py:202
  84.0 7.6 %collective-permute-start.17 = (bf16[64,32,128]{2,1,0:T(8,128)(2,1)S(1)}, bf16[64,32,128]{2,1,0:T(8,128)(2,1)S(1)}, u32[]{:S(2)}, u32[]{:S(2)}) collective-permute-start(bf16[64,32,128]{2,1,0:T(8,128)(2,1)S(1)} %collective-permute-done.5.refs_3_), channel_id=1, source_target_pairs={{0,1},{1,0},{2,3},{3,2},{4,5},{5,4},{6,7},{7,6},{8,9},{9,8},{10,11... | collective-permute-start | bytes 1572872 | tf_op jit(solution)/shard_map/near/ppermute | solution.py:198
  85.6 6.1 %collective-permute-start.15 = (bf16[64,32,128]{2,1,0:T(8,128)(2,1)S(1)}, bf16[64,32,128]{2,1,0:T(8,128)(2,1)S(1)}, u32[]{:S(2)}, u32[]{:S(2)}) collective-permute-start(bf16[64,32,128]{2,1,0:T(8,128)(2,1)S(1)} %collective-permute-done.12.refs_1_), channel_id=1, source_target_pairs={{0,1},{1,0},{2,3},{3,2},{4,5},{5,4},{6,7},{7,6},{8,9},{9,8},{10,11... | collective-permute-start | bytes 1572872 | tf_op jit(solution)/shard_map/near/ppermute | solution.py:198
  86.0 5.6 %collective-permute-start.16 = (bf16[64,32,128]{2,1,0:T(8,128)(2,1)S(1)}, bf16[64,32,128]{2,1,0:T(8,128)(2,1)S(1)}, u32[]{:S(2)}, u32[]{:S(2)}) collective-permute-start(bf16[64,32,128]{2,1,0:T(8,128)(2,1)S(1)} %collective-permute-done.13.refs_2_), channel_id=1, source_target_pairs={{0,1},{1,0},{2,3},{3,2},{4,5},{5,4},{6,7},{7,6},{8,9},{9,8},{10,11... | collective-permute-start | bytes 1572872 | tf_op jit(solution)/shard_map/near/ppermute | solution.py:198
  90.4 3.4 %collective-permute-start.10 = (bf16[64,32,128]{2,1,0:T(8,128)(2,1)S(1)}, bf16[64,32,128]{2,1,0:T(8,128)(2,1)S(1)}, u32[]{:S(2)}, u32[]{:S(2)}) collective-permute-start(bf16[64,32,128]{2,1,0:T(8,128)(2,1)S(1)} %collective-permute-done.8.refs_0_), channel_id=1, source_target_pairs={{0,1},{1,0},{2,3},{3,2},{4,5},{5,4},{6,7},{7,6},{8,9},{9,8},{10,11... | collective-permute-start | bytes 1572872 | tf_op jit(solution)/shard_map/far/ppermute | solution.py:198
  91.6 2.3 %collective-permute-start.11 = (bf16[64,32,128]{2,1,0:T(8,128)(2,1)S(1)}, bf16[64,32,128]{2,1,0:T(8,128)(2,1)S(1)}, u32[]{:S(2)}, u32[]{:S(2)}) collective-permute-start(bf16[64,32,128]{2,1,0:T(8,128)(2,1)S(1)} %collective-permute-done.9.refs_1_), channel_id=1, source_target_pairs={{0,1},{1,0},{2,3},{3,2},{4,5},{5,4},{6,7},{7,6},{8,9},{9,8},{10,11... | collective-permute-start | bytes 1572872 | tf_op jit(solution)/shard_map/far/ppermute | solution.py:198

commit v6 on v5

--- a/solution.py
+++ b/solution.py
@@ -52,18 +52,18 @@
 
 def tiles_kernel(kept_ref, act_ref, cot_ref, out_ref, lefts, rights, stage, sems):
     me = lax.axis_index("dp")
+    whole = pltpu.make_async_copy(cot_ref, rights, sems.at[1])
+    whole.start()
     for k in range(KEPT):
-        tile = kept_ref[k, me]
-        row = pl.multiple_of((tile // COLS) * TILE, TILE)
-        col = pl.multiple_of((tile % COLS) * TILE, TILE)
+        row = pl.multiple_of((kept_ref[k, me] // COLS) * TILE, TILE)
         pltpu.make_async_copy(act_ref.at[:, pl.ds(row, TILE)], lefts.at[k], sems.at[0]).start()
-        pltpu.make_async_copy(cot_ref.at[:, pl.ds(col, TILE)], rights.at[k], sems.at[1]).start()
+    whole.wait()
     pltpu.make_async_copy(lefts, lefts, sems.at[0]).wait()
-    pltpu.make_async_copy(rights, rights, sems.at[1]).wait()
     for k in range(KEPT):
         half = kept_ref[k, me] // HALF_TILES
+        col = pl.multiple_of((kept_ref[k, me] % COLS) * TILE, TILE)
         tile = lax.dot_general(
-            lefts[k], rights[k], (((0,), (0,)), ((), ())), preferred_element_type=jnp.float32
+            lefts[k], rights[:, pl.ds(col, TILE)], (((0,), (0,)), ((), ())), preferred_element_type=jnp.float32
         )
         for p in range(4):
             for q in range(4):
@@ -86,7 +86,7 @@
         out_specs=pl.BlockSpec(memory_space=pltpu.VMEM),
         scratch_shapes=[
             pltpu.VMEM((KEPT, TILE, TILE), jnp.bfloat16),
-            pltpu.VMEM((KEPT, TILE, TILE), jnp.bfloat16),
+            pltpu.VMEM((TILE, COLS * TILE), jnp.bfloat16),
             pltpu.VMEM((KEPT * TILE, TILE), jnp.float32),
             pltpu.SemaphoreType.DMA((2,)),
         ],
@@ -132,7 +132,7 @@
             out_ref[t] = jnp.concatenate(rows, axis=0).astype(jnp.bfloat16)
             return carry
 
-        lax.fori_loop(0, PART, body, 0, unroll=8)
+        lax.fori_loop(0, PART, body, 0, unroll=32)
 
 
 def by_rows(pieces):

time: 95.8 us -> 95.7 us (level)
  no operation moved by 1% of the time
where the time goes in v6:
time: 95.7 us; the launch traced here: 95.3 us
  starting transfers between devices  38.4 us (40%)
  waiting for transfers between devices  25.4 us (27%)
  blocking collectives  14 us (15%)
  Pallas kernels  10 us (10%)
  other arithmetic  6.17 us (6%)
  local copies, waits for them, and re-layouts  1.08 us (1%)
    all_to_all x1, starting transfers between devices, local(): lax.all_to_all(sent, 'dp', 0, 0, axis_index_groups=CHIP_GROUPS, tiled=True)  16.4 us
    all_to_all x1, blocking collectives, local(): lax.all_to_all(jnp.broadcast_to(row[None], (ZN, HALF, TILE)), 'dp', 0, 0,...  14 us
    ppermute x6, waiting for transfers between devices, send(): return lax.ppermute(block, 'dp', ring(step, 1))  9.63 us
    all_to_all x1, waiting for transfers between devices, local(): lax.all_to_all(sent, 'dp', 0, 0, axis_index_groups=CHIP_GROUPS, tiled=True)  9.58 us
    ppermute x8, starting transfers between devices, swap(): return [lax.ppermute(b, 'dp', SWAP) for b in blocks]  6.94 us
    ppermute x6, starting transfers between devices, send(): return lax.ppermute(block, 'dp', ring(step, 1))  6.82 us
    reduce_or x1, other arithmetic, local(): hit = jnp.any(kept_tiles[:, :, None] == chosen[None, None, :], axis=-1)  5.38 us
    ppermute x3, waiting for transfers between devices, local(): pieces = [rows] + [lax.ppermute(rows, 'dp', ring(s, 0)) for s in STEPS[1:]]  5.12 us
  transfers between devices with their start and end apart: 19, of which 8 were waited for; matrix products, arithmetic and copies ran while one was open for 8% of the time, Pallas kernels for 4%

profile of v6, /device:TPU:1, one launch (start us, length us, event | category | flops | bytes accessed | tf_op | source)
XLA Modules:
  0.0 95.3 jit_solution(15539138730246700146)
XLA Ops:
  0.0 3.3 %own_tiles.1 = f32[128,8,128]{2,1,0:T(8,128)} custom-call(s32[8,256]{1,0:T(8,128)} %bitcast.12, bf16[128,8192]{1,0:T(8,128)(2,1)} %act_ref.1, bf16[128,2048]{1,0:T(8,128)(2,1)} %cot_ref.1), custom_call_target="tpu_custom_call" | custom-call | tf_op jit(solution)/shard_map/own_tiles/pallas_call | solution.py:78
  3.3 16.4 %all-to-all-start = ((f32[128,8,128]{2,1,0:T(8,128)}), f32[128,8,128]{2,1,0:T(8,128)S(1)}, u32[]{:S(2)}, u32[]{:S(2)}) async-start(f32[128,8,128]{2,1,0:T(8,128)} %own_tiles.1), calls=%async_computation | async-start | bytes 1048576 | tf_op jit(solution)/shard_map/all_to_all | solution.py:189
  20.5 5.4 %compare_reduce_fusion = pred[256,8]{1,0:T(8,128)(4,1)S(1)} fusion(s32[256]{0:T(256)} %param.9, s32[256,8]{1,0:T(8,128)S(1)} %copy.22), kind=kLoop, calls=%fused_computation | loop fusion | flops 1046528 | bytes 11264 | tf_op jit(solution)/shard_map/reduce_or | solution.py:185
  26.9 9.6 %all-to-all-done = f32[128,8,128]{2,1,0:T(8,128)S(1)} async-done(((f32[128,8,128]{2,1,0:T(8,128)}), f32[128,8,128]{2,1,0:T(8,128)S(1)}, u32[]{:S(2)}, u32[]{:S(2)}) %all-to-all-start) | async-done | bytes 524320 | tf_op jit(solution)/shard_map/all_to_all | solution.py:189
  37.1 3.5 %collective-permute-start = (f32[128,128]{1,0:T(8,128)S(1)}, f32[128,128]{1,0:T(8,128)S(1)}, u32[]{:S(2)}, u32[]{:S(2)}) collective-permute-start(f32[128,128]{1,0:T(8,128)S(1)} %get-tuple-element.13), channel_id=1, source_target_pairs={{0,1},{1,0},{2,3},{3,2},{4,5},{5,4},{6,7},{7,6},{8,9},{9,8},{10,11... | collective-permute-start | bytes 196616 | tf_op jit(solution)/shard_map/ppermute | solution.py:191
  41.6 14.0 %all_to_all.10.p0 = bf16[8,128,128]{2,1,0:T(8,128)(2,1)S(1)} all-to-all(bf16[8,128,128]{2,1,0:T(8,128)(2,1)S(1)} %broadcast_in_dim.3), channel_id=1, replica_groups={{0,32,64,96,128,160,192,224},{1,33,65,97,129,161,193,225},{2,34,66,98,1..., dimensions={0} | all-to-all | bytes 524288 | tf_op jit(solution)/shard_map/all_to_all | solution.py:193
  55.6 2.0 %collective-permute-start.1 = (bf16[8,128,128]{2,1,0:T(8,128)(2,1)S(1)}, bf16[8,128,128]{2,1,0:T(8,128)(2,1)S(1)}, u32[]{:S(2)}, u32[]{:S(2)}) collective-permute-start(bf16[8,128,128]{2,1,0:T(8,128)(2,1)S(1)} %all_to_all.10.p0), channel_id=1, source_target_pairs={{0,16},{1,5},{2,18},{3,7},{4,20},{5,1},{6,22},{7,3},{8,24},{9,13},... | collective-permute-start | bytes 786440 | tf_op jit(solution)/shard_map/s2/ppermute | solution.py:209
  57.7 2.7 %collective-permute-start.3 = (bf16[8,128,128]{2,1,0:T(8,128)(2,1)S(1)}, bf16[8,128,128]{2,1,0:T(8,128)(2,1)S(1)}, u32[]{:S(2)}, u32[]{:S(2)}) collective-permute-start(bf16[8,128,128]{2,1,0:T(8,128)(2,1)S(1)} %all_to_all.10.p0), channel_id=1, source_target_pairs={{0,24},{1,7},{2,26},{3,1},{4,28},{5,3},{6,30},{7,5},{8,0},{9,15},{... | collective-permute-start | bytes 786440 | tf_op jit(solution)/shard_map/s2/ppermute | solution.py:209
  60.3 2.3 %collective-permute-done.1.p1 = bf16[8,128,128]{2,1,0:T(8,128)(2,1)S(1)} collective-permute-done((bf16[8,128,128]{2,1,0:T(8,128)(2,1)S(1)}, bf16[8,128,128]{2,1,0:T(8,128)(2,1)S(1)}, u32[]{:S(2)}, u32[]{:S(2)}) %collective-permute-start.1) | collective-permute-done | bytes 262176 | tf_op jit(solution)/shard_map/s2/ppermute | solution.py:209
  62.6 2.8 %collective-permute-done.2.p2 = bf16[8,128,128]{2,1,0:T(8,128)(2,1)S(1)} collective-permute-done((bf16[8,128,128]{2,1,0:T(8,128)(2,1)S(1)}, bf16[8,128,128]{2,1,0:T(8,128)(2,1)S(1)}, u32[]{:S(2)}, u32[]{:S(2)}) %collective-permute-start.2) | collective-permute-done | bytes 262176 | tf_op jit(solution)/shard_map/s2/ppermute | solution.py:209
  65.5 1.3 %by_rows.1 = (bf16[64,32,128]{2,1,0:T(8,128)(2,1)S(1)}, bf16[64,32,128]{2,1,0:T(8,128)(2,1)S(1)}) custom-call(bf16[8,128,128]{2,1,0:T(8,128)(2,1)S(1)} %all_to_all.10.p0, bf16[8,128,128]{2,1,0:T(8,128)(2,1)S(1)} %collective-permute-done.1.p1, bf16[8,128,128]{2,1,0:T(8,128)(2,1)S(1)} %collective-permute-done.2.p2, ...), custom_call_target="tpu_custom_call" | custom-call | tf_op jit(solution)/shard_map/by_rows/pallas_call | solution.py:139
  66.8 2.6 %collective-permute-start.6 = (bf16[64,32,128]{2,1,0:T(8,128)(2,1)S(1)}, bf16[64,32,128]{2,1,0:T(8,128)(2,1)S(1)}, u32[]{:S(2)}, u32[]{:S(2)}) collective-permute-start(bf16[64,32,128]{2,1,0:T(8,128)(2,1)S(1)} %get-tuple-element.14.refs_0_), channel_id=1, source_target_pairs={{0,1},{1,0},{2,3},{3,2},{4,5},{5,4},{6,7},{7,6},{8,9},{9,8},{10,11... | collective-permute-start | bytes 1572872 | tf_op jit(solution)/shard_map/own/ppermute | solution.py:198
  70.2 2.2 %collective-permute-start.5 = (bf16[64,32,128]{2,1,0:T(8,128)(2,1)S(1)}, bf16[64,32,128]{2,1,0:T(8,128)(2,1)S(1)}, u32[]{:S(2)}, u32[]{:S(2)}) collective-permute-start(bf16[64,32,128]{2,1,0:T(8,128)(2,1)S(1)} %get-tuple-element.15.refs_1_), channel_id=1, source_target_pairs={{0,6},{1,25},{2,0},{3,27},{4,2},{5,29},{6,4},{7,31},{8,14},{9,1},{... | collective-permute-start | bytes 1572872 | tf_op jit(solution)/shard_map/b3/ppermute | solution.py:202
  72.4 1.4 %collective-permute-start.13 = (bf16[64,32,128]{2,1,0:T(8,128)(2,1)S(1)}, bf16[64,32,128]{2,1,0:T(8,128)(2,1)S(1)}, u32[]{:S(2)}, u32[]{:S(2)}) collective-permute-start(bf16[64,32,128]{2,1,0:T(8,128)(2,1)S(1)} %get-tuple-element.15.refs_1_), channel_id=1, source_target_pairs={{0,2},{1,9},{2,4},{3,11},{4,6},{5,13},{6,0},{7,15},{8,10},{9,17},{... | collective-permute-start | bytes 1572872 | tf_op jit(solution)/shard_map/b1/ppermute | solution.py:202
  73.8 1.3 %join.3.refs_8_ = bf16[2,2,64,4,32,128]{5,4,3,2,1,0:T(8,128)(2,1)} custom-call(bf16[64,32,128]{2,1,0:T(8,128)(2,1)S(1)} %get-tuple-element.14.refs_0_, bf16[64,32,128]{2,1,0:T(8,128)(2,1)S(1)} %get-tuple-element.15.refs_1_, bf16[64,32,128]{2,1,0:T(8,128)(2,1)S(1)} %collective-permute-done.6.refs_2_, bf16[64,32,128]{2,1,0:T(8,128)(2,1)S(1)} %collective-permute-done.7.refs_3_), custom_call_target="tpu_custom_call" | custom-call | bytes 4194304 | tf_op jit(solution)/shard_map/join/pallas_call | solution.py:167
  75.2 4.0 %collective-permute-done.4.refs_0_ = bf16[64,32,128]{2,1,0:T(8,128)(2,1)S(1)} collective-permute-done((bf16[64,32,128]{2,1,0:T(8,128)(2,1)S(1)}, bf16[64,32,128]{2,1,0:T(8,128)(2,1)S(1)}, u32[]{:S(2)}, u32[]{:S(2)}) %collective-permute-start.4) | collective-permute-done | bytes 524320 | tf_op jit(solution)/shard_map/a1/ppermute | solution.py:202
  79.2 1.1 %collective-permute-start.14 = (bf16[64,32,128]{2,1,0:T(8,128)(2,1)S(1)}, bf16[64,32,128]{2,1,0:T(8,128)(2,1)S(1)}, u32[]{:S(2)}, u32[]{:S(2)}) collective-permute-start(bf16[64,32,128]{2,1,0:T(8,128)(2,1)S(1)} %collective-permute-done.4.refs_0_), channel_id=1, source_target_pairs={{0,1},{1,0},{2,3},{3,2},{4,5},{5,4},{6,7},{7,6},{8,9},{9,8},{10,11... | collective-permute-start | bytes 1572872 | tf_op jit(solution)/shard_map/near/ppermute | solution.py:198
  80.8 2.2 %collective-permute-start.9 = (bf16[64,32,128]{2,1,0:T(8,128)(2,1)S(1)}, bf16[64,32,128]{2,1,0:T(8,128)(2,1)S(1)}, u32[]{:S(2)}, u32[]{:S(2)}) collective-permute-start(bf16[64,32,128]{2,1,0:T(8,128)(2,1)S(1)} %collective-permute-done.5.refs_3_), channel_id=1, source_target_pairs={{0,6},{1,25},{2,0},{3,27},{4,2},{5,29},{6,4},{7,31},{8,14},{9,1},{... | collective-permute-start | bytes 1572872 | tf_op jit(solution)/shard_map/b2/ppermute | solution.py:202
  83.0 1.1 %collective-permute-done.12.refs_1_ = bf16[64,32,128]{2,1,0:T(8,128)(2,1)S(1)} collective-permute-done((bf16[64,32,128]{2,1,0:T(8,128)(2,1)S(1)}, bf16[64,32,128]{2,1,0:T(8,128)(2,1)S(1)}, u32[]{:S(2)}, u32[]{:S(2)}) %collective-permute-start.12) | collective-permute-done | bytes 524320 | tf_op jit(solution)/shard_map/a3/ppermute | solution.py:202
  84.1 1.4 %collective-permute-start.17 = (bf16[64,32,128]{2,1,0:T(8,128)(2,1)S(1)}, bf16[64,32,128]{2,1,0:T(8,128)(2,1)S(1)}, u32[]{:S(2)}, u32[]{:S(2)}) collective-permute-start(bf16[64,32,128]{2,1,0:T(8,128)(2,1)S(1)} %collective-permute-done.5.refs_3_), channel_id=1, source_target_pairs={{0,1},{1,0},{2,3},{3,2},{4,5},{5,4},{6,7},{7,6},{8,9},{9,8},{10,11... | collective-permute-start | bytes 1572872 | tf_op jit(solution)/shard_map/near/ppermute | solution.py:198
  86.0 4.5 %collective-permute-done.8.refs_0_ = bf16[64,32,128]{2,1,0:T(8,128)(2,1)S(1)} collective-permute-done((bf16[64,32,128]{2,1,0:T(8,128)(2,1)S(1)}, bf16[64,32,128]{2,1,0:T(8,128)(2,1)S(1)}, u32[]{:S(2)}, u32[]{:S(2)}) %collective-permute-start.8) | collective-permute-done | bytes 524320 | tf_op jit(solution)/shard_map/a2/ppermute | solution.py:202
  90.5 1.1 %collective-permute-start.10 = (bf16[64,32,128]{2,1,0:T(8,128)(2,1)S(1)}, bf16[64,32,128]{2,1,0:T(8,128)(2,1)S(1)}, u32[]{:S(2)}, u32[]{:S(2)}) collective-permute-start(bf16[64,32,128]{2,1,0:T(8,128)(2,1)S(1)} %collective-permute-done.8.refs_0_), channel_id=1, source_target_pairs={{0,1},{1,0},{2,3},{3,2},{4,5},{5,4},{6,7},{7,6},{8,9},{9,8},{10,11... | collective-permute-start | bytes 1572872 | tf_op jit(solution)/shard_map/far/ppermute | solution.py:198
  91.6 2.1 %join.4.refs_4_ = bf16[2,2,64,4,32,128]{5,4,3,2,1,0:T(8,128)(2,1)} custom-call(bf16[64,32,128]{2,1,0:T(8,128)(2,1)S(1)} %collective-permute-done.4.refs_0_, bf16[64,32,128]{2,1,0:T(8,128)(2,1)S(1)} %collective-permute-done.12.refs_1_, bf16[64,32,128]{2,1,0:T(8,128)(2,1)S(1)} %collective-permute-done.13.refs_2_, ...), custom_call_target="tpu_custom_call", output_to_operand_aliasing={{}: (8, {})} | custom-call | bytes 8388608 | tf_op jit(solution)/shard_map/join/pallas_call | solution.py:167
  93.8 1.3 %join.5 = bf16[2,2,64,4,32,128]{5,4,3,2,1,0:T(8,128)(2,1)} custom-call(bf16[64,32,128]{2,1,0:T(8,128)(2,1)S(1)} %collective-permute-done.8.refs_0_, bf16[64,32,128]{2,1,0:T(8,128)(2,1)S(1)} %collective-permute-done.9.refs_1_, bf16[64,32,128]{2,1,0:T(8,128)(2,1)S(1)} %collective-permute-done.10.refs_2_, ...), custom_call_target="tpu_custom_call", output_to_operand_aliasing={{}: (4, {})} | custom-call | bytes 4194304 | tf_op jit(solution)/shard_map/join/pallas_call | solution.py:167
  (30 shorter events, 5.3 us)
Async XLA Ops:
  3.3 33.2 %all-to-all-start = ((f32[128,8,128]{2,1,0:T(8,128)}), f32[128,8,128]{2,1,0:T(8,128)S(1)}, u32[]{:S(2)}, u32[]{:S(2)}) async-start(f32[128,8,128]{2,1,0:T(8,128)} %own_tiles.1), calls=%async_computation | async-start | bytes 1048576 | tf_op jit(solution)/shard_map/all_to_all | solution.py:189
  37.1 4.4 %collective-permute-start = (f32[128,128]{1,0:T(8,128)S(1)}, f32[128,128]{1,0:T(8,128)S(1)}, u32[]{:S(2)}, u32[]{:S(2)}) collective-permute-start(f32[128,128]{1,0:T(8,128)S(1)} %get-tuple-element.13), channel_id=1, source_target_pairs={{0,1},{1,0},{2,3},{3,2},{4,5},{5,4},{6,7},{7,6},{8,9},{9,8},{10,11... | collective-permute-start | bytes 196616 | tf_op jit(solution)/shard_map/ppermute | solution.py:191
  55.6 7.0 %collective-permute-start.1 = (bf16[8,128,128]{2,1,0:T(8,128)(2,1)S(1)}, bf16[8,128,128]{2,1,0:T(8,128)(2,1)S(1)}, u32[]{:S(2)}, u32[]{:S(2)}) collective-permute-start(bf16[8,128,128]{2,1,0:T(8,128)(2,1)S(1)} %all_to_all.10.p0), channel_id=1, source_target_pairs={{0,16},{1,5},{2,18},{3,7},{4,20},{5,1},{6,22},{7,3},{8,24},{9,13},... | collective-permute-start | bytes 786440 | tf_op jit(solution)/shard_map/s2/ppermute | solution.py:209
  57.7 7.8 %collective-permute-start.2 = (bf16[8,128,128]{2,1,0:T(8,128)(2,1)S(1)}, bf16[8,128,128]{2,1,0:T(8,128)(2,1)S(1)}, u32[]{:S(2)}, u32[]{:S(2)}) collective-permute-start(bf16[8,128,128]{2,1,0:T(8,128)(2,1)S(1)} %all_to_all.10.p0), channel_id=1, source_target_pairs={{0,8},{1,3},{2,10},{3,5},{4,12},{5,7},{6,14},{7,1},{8,16},{9,11},{... | collective-permute-start | bytes 786440 | tf_op jit(solution)/shard_map/s2/ppermute | solution.py:209
  57.7 7.8 %collective-permute-start.3 = (bf16[8,128,128]{2,1,0:T(8,128)(2,1)S(1)}, bf16[8,128,128]{2,1,0:T(8,128)(2,1)S(1)}, u32[]{:S(2)}, u32[]{:S(2)}) collective-permute-start(bf16[8,128,128]{2,1,0:T(8,128)(2,1)S(1)} %all_to_all.10.p0), channel_id=1, source_target_pairs={{0,24},{1,7},{2,26},{3,1},{4,28},{5,3},{6,30},{7,5},{8,0},{9,15},{... | collective-permute-start | bytes 786440 | tf_op jit(solution)/shard_map/s2/ppermute | solution.py:209
  66.8 5.6 %collective-permute-start.6 = (bf16[64,32,128]{2,1,0:T(8,128)(2,1)S(1)}, bf16[64,32,128]{2,1,0:T(8,128)(2,1)S(1)}, u32[]{:S(2)}, u32[]{:S(2)}) collective-permute-start(bf16[64,32,128]{2,1,0:T(8,128)(2,1)S(1)} %get-tuple-element.14.refs_0_), channel_id=1, source_target_pairs={{0,1},{1,0},{2,3},{3,2},{4,5},{5,4},{6,7},{7,6},{8,9},{9,8},{10,11... | collective-permute-start | bytes 1572872 | tf_op jit(solution)/shard_map/own/ppermute | solution.py:198
  69.4 4.4 %collective-permute-start.7 = (bf16[64,32,128]{2,1,0:T(8,128)(2,1)S(1)}, bf16[64,32,128]{2,1,0:T(8,128)(2,1)S(1)}, u32[]{:S(2)}, u32[]{:S(2)}) collective-permute-start(bf16[64,32,128]{2,1,0:T(8,128)(2,1)S(1)} %get-tuple-element.15.refs_1_), channel_id=1, source_target_pairs={{0,1},{1,0},{2,3},{3,2},{4,5},{5,4},{6,7},{7,6},{8,9},{9,8},{10,11... | collective-permute-start | bytes 1572872 | tf_op jit(solution)/shard_map/own/ppermute | solution.py:198
  69.7 9.5 %collective-permute-start.4 = (bf16[64,32,128]{2,1,0:T(8,128)(2,1)S(1)}, bf16[64,32,128]{2,1,0:T(8,128)(2,1)S(1)}, u32[]{:S(2)}, u32[]{:S(2)}) collective-permute-start(bf16[64,32,128]{2,1,0:T(8,128)(2,1)S(1)} %get-tuple-element.14.refs_0_), channel_id=1, source_target_pairs={{0,2},{1,9},{2,4},{3,11},{4,6},{5,13},{6,0},{7,15},{8,10},{9,17},{... | collective-permute-start | bytes 1572872 | tf_op jit(solution)/shard_map/a1/ppermute | solution.py:202
  70.2 9.1 %collective-permute-start.5 = (bf16[64,32,128]{2,1,0:T(8,128)(2,1)S(1)}, bf16[64,32,128]{2,1,0:T(8,128)(2,1)S(1)}, u32[]{:S(2)}, u32[]{:S(2)}) collective-permute-start(bf16[64,32,128]{2,1,0:T(8,128)(2,1)S(1)} %get-tuple-element.15.refs_1_), channel_id=1, source_target_pairs={{0,6},{1,25},{2,0},{3,27},{4,2},{5,29},{6,4},{7,31},{8,14},{9,1},{... | collective-permute-start | bytes 1572872 | tf_op jit(solution)/shard_map/b3/ppermute | solution.py:202
  72.4 11.7 %collective-permute-start.12 = (bf16[64,32,128]{2,1,0:T(8,128)(2,1)S(1)}, bf16[64,32,128]{2,1,0:T(8,128)(2,1)S(1)}, u32[]{:S(2)}, u32[]{:S(2)}) collective-permute-start(bf16[64,32,128]{2,1,0:T(8,128)(2,1)S(1)} %get-tuple-element.14.refs_0_), channel_id=1, source_target_pairs={{0,6},{1,25},{2,0},{3,27},{4,2},{5,29},{6,4},{7,31},{8,14},{9,1},{... | collective-permute-start | bytes 1572872 | tf_op jit(solution)/shard_map/a3/ppermute | solution.py:202
  72.4 13.1 %collective-permute-start.13 = (bf16[64,32,128]{2,1,0:T(8,128)(2,1)S(1)}, bf16[64,32,128]{2,1,0:T(8,128)(2,1)S(1)}, u32[]{:S(2)}, u32[]{:S(2)}) collective-permute-start(bf16[64,32,128]{2,1,0:T(8,128)(2,1)S(1)} %get-tuple-element.15.refs_1_), channel_id=1, source_target_pairs={{0,2},{1,9},{2,4},{3,11},{4,6},{5,13},{6,0},{7,15},{8,10},{9,17},{... | collective-permute-start | bytes 1572872 | tf_op jit(solution)/shard_map/b1/ppermute | solution.py:202
  79.2 6.7 %collective-permute-start.14 = (bf16[64,32,128]{2,1,0:T(8,128)(2,1)S(1)}, bf16[64,32,128]{2,1,0:T(8,128)(2,1)S(1)}, u32[]{:S(2)}, u32[]{:S(2)}) collective-permute-start(bf16[64,32,128]{2,1,0:T(8,128)(2,1)S(1)} %collective-permute-done.4.refs_0_), channel_id=1, source_target_pairs={{0,1},{1,0},{2,3},{3,2},{4,5},{5,4},{6,7},{7,6},{8,9},{9,8},{10,11... | collective-permute-start | bytes 1572872 | tf_op jit(solution)/shard_map/near/ppermute | solution.py:198
  80.3 10.1 %collective-permute-start.8 = (bf16[64,32,128]{2,1,0:T(8,128)(2,1)S(1)}, bf16[64,32,128]{2,1,0:T(8,128)(2,1)S(1)}, u32[]{:S(2)}, u32[]{:S(2)}) collective-permute-start(bf16[64,32,128]{2,1,0:T(8,128)(2,1)S(1)} %collective-permute-done.4.refs_0_), channel_id=1, source_target_pairs={{0,2},{1,9},{2,4},{3,11},{4,6},{5,13},{6,0},{7,15},{8,10},{9,17},{... | collective-permute-start | bytes 1572872 | tf_op jit(solution)/shard_map/a2/ppermute | solution.py:202
  80.8 10.8 %collective-permute-start.9 = (bf16[64,32,128]{2,1,0:T(8,128)(2,1)S(1)}, bf16[64,32,128]{2,1,0:T(8,128)(2,1)S(1)}, u32[]{:S(2)}, u32[]{:S(2)}) collective-permute-start(bf16[64,32,128]{2,1,0:T(8,128)(2,1)S(1)} %collective-permute-done.5.refs_3_), channel_id=1, source_target_pairs={{0,6},{1,25},{2,0},{3,27},{4,2},{5,29},{6,4},{7,31},{8,14},{9,1},{... | collective-permute-start | bytes 1572872 | tf_op jit(solution)/shard_map/b2/ppermute | solution.py:202
  84.1 7.4 %collective-permute-start.17 = (bf16[64,32,128]{2,1,0:T(8,128)(2,1)S(1)}, bf16[64,32,128]{2,1,0:T(8,128)(2,1)S(1)}, u32[]{:S(2)}, u32[]{:S(2)}) collective-permute-start(bf16[64,32,128]{2,1,0:T(8,128)(2,1)S(1)} %collective-permute-done.5.refs_3_), channel_id=1, source_target_pairs={{0,1},{1,0},{2,3},{3,2},{4,5},{5,4},{6,7},{7,6},{8,9},{9,8},{10,11... | collective-permute-start | bytes 1572872 | tf_op jit(solution)/shard_map/near/ppermute | solution.py:198
  85.5 6.1 %collective-permute-start.15 = (bf16[64,32,128]{2,1,0:T(8,128)(2,1)S(1)}, bf16[64,32,128]{2,1,0:T(8,128)(2,1)S(1)}, u32[]{:S(2)}, u32[]{:S(2)}) collective-permute-start(bf16[64,32,128]{2,1,0:T(8,128)(2,1)S(1)} %collective-permute-done.12.refs_1_), channel_id=1, source_target_pairs={{0,1},{1,0},{2,3},{3,2},{4,5},{5,4},{6,7},{7,6},{8,9},{9,8},{10,11... | collective-permute-start | bytes 1572872 | tf_op jit(solution)/shard_map/near/ppermute | solution.py:198
  85.9 5.6 %collective-permute-start.16 = (bf16[64,32,128]{2,1,0:T(8,128)(2,1)S(1)}, bf16[64,32,128]{2,1,0:T(8,128)(2,1)S(1)}, u32[]{:S(2)}, u32[]{:S(2)}) collective-permute-start(bf16[64,32,128]{2,1,0:T(8,128)(2,1)S(1)} %collective-permute-done.13.refs_2_), channel_id=1, source_target_pairs={{0,1},{1,0},{2,3},{3,2},{4,5},{5,4},{6,7},{7,6},{8,9},{9,8},{10,11... | collective-permute-start | bytes 1572872 | tf_op jit(solution)/shard_map/near/ppermute | solution.py:198
  90.5 3.2 %collective-permute-start.10 = (bf16[64,32,128]{2,1,0:T(8,128)(2,1)S(1)}, bf16[64,32,128]{2,1,0:T(8,128)(2,1)S(1)}, u32[]{:S(2)}, u32[]{:S(2)}) collective-permute-start(bf16[64,32,128]{2,1,0:T(8,128)(2,1)S(1)} %collective-permute-done.8.refs_0_), channel_id=1, source_target_pairs={{0,1},{1,0},{2,3},{3,2},{4,5},{5,4},{6,7},{7,6},{8,9},{9,8},{10,11... | collective-permute-start | bytes 1572872 | tf_op jit(solution)/shard_map/far/ppermute | solution.py:198
  91.6 2.3 %collective-permute-start.11 = (bf16[64,32,128]{2,1,0:T(8,128)(2,1)S(1)}, bf16[64,32,128]{2,1,0:T(8,128)(2,1)S(1)}, u32[]{:S(2)}, u32[]{:S(2)}) collective-permute-start(bf16[64,32,128]{2,1,0:T(8,128)(2,1)S(1)} %collective-permute-done.9.refs_1_), channel_id=1, source_target_pairs={{0,1},{1,0},{2,3},{3,2},{4,5},{5,4},{6,7},{7,6},{8,9},{9,8},{10,11... | collective-permute-start | bytes 1572872 | tf_op jit(solution)/shard_map/far/ppermute | solution.py:198

commit v7 on v5

--- a/solution.py
+++ b/solution.py
@@ -27,7 +27,8 @@
 
 
 DEVS = [(z, y, x, c) for z in range(ZN) for y in range(YN) for x in range(XN) for c in range(CN)]
-CHIP_GROUPS = [[dev(z, y, x, c) for y in range(YN) for z in range(ZN) for x in range(XN)] for c in range(CN)]
+ORDER = [37 * i % CHIPS for i in range(CHIPS)]
+CHIP_GROUPS = [[chip * CN + c for chip in ORDER] for c in range(CN)]
 Z_GROUPS = [[dev(z, y, x, c) for z in range(ZN)] for y in range(YN) for x in range(XN) for c in range(CN)]
 SWAP = [(d, d ^ 1) for d in range(N_DP)]
 
@@ -70,7 +71,8 @@
                 there = jnp.where(half == 0, p * 32 + q * 8, q * 32 + p * 8) + k * TILE
                 here = p * 32 + q * 8
                 stage[pl.ds(pl.multiple_of(there, 8), 8), :] = tile[here:here + 8, :]
-    for i, (y, z, x) in enumerate(np.ndindex(YN, ZN, XN)):
+    for i, chip in enumerate(ORDER):
+        z, y, x = chip // 16, (chip // 4) % 4, chip % 4
         out_ref[i] = stage[pl.ds(x * 32 + y * 8 + z, KEPT, stride=TILE), :]
 
 
@@ -183,9 +185,9 @@
     sent = own_tiles(kept_tiles.T, activations, cotangent)
     live = jnp.arange(KEPT, dtype=jnp.int32)[None, :] < kept_counts[:, None]
     hit = jnp.any(kept_tiles[:, :, None] == chosen[None, None, :], axis=-1)
-    region = jnp.where(live & hit, kept_tiles // REGION, -1).reshape(ZN, YN, XN, CN, KEPT)
-    region = lax.dynamic_index_in_dim(region, core, 3, keepdims=False)
-    region = region.transpose(1, 0, 2, 3).reshape(1, CHIPS * KEPT)
+    region = jnp.where(live & hit, kept_tiles // REGION, -1).reshape(CHIPS, CN, KEPT)
+    region = lax.dynamic_index_in_dim(region, core, 1, keepdims=False)
+    region = region[np.array(ORDER)].reshape(1, CHIPS * KEPT)
     got = lax.all_to_all(sent, "dp", 0, 0, axis_index_groups=CHIP_GROUPS, tiled=True)
     mine, theirs = sum_tiles(region, got.reshape(CHIPS * KEPT, TILE))
     row = (mine + lax.ppermute(theirs, "dp", SWAP)).astype(jnp.bfloat16)

time: 95.8 us -> 96 us (level)
  starting transfers between devices: 38.7 us -> 35.4 us
  waiting for transfers between devices: 25 us -> 26.7 us
    ppermute x3, starting transfers between devices: 4.71 us -> 2.68 us  [local(): pieces = [rows] + [lax.ppermute(rows, 'dp', ring(s, 0)) for s in STEPS[1:]]]
    ppermute x3, waiting for transfers between devices: 5.12 us -> 6.86 us  [local(): pieces = [rows] + [lax.ppermute(rows, 'dp', ring(s, 0)) for s in STEPS[1:]]]
  transfers between devices with their start and end apart: 19 -> 19, of which waited for: 8 -> 8; matrix products, arithmetic and copies ran while one was open for 8% -> 9% of each run, Pallas kernels for 4% -> 4%
where the time goes in v7:
time: 96 us; the launch traced here: 95.7 us
  starting transfers between devices  35.4 us (37%)
  waiting for transfers between devices  26.7 us (28%)
  blocking collectives  14.8 us (15%)
  Pallas kernels  10.1 us (11%)
  other arithmetic  6.84 us (7%)
  local copies, waits for them, and re-layouts  1.66 us (2%)
    all_to_all x1, starting transfers between devices, local(): lax.all_to_all(sent, 'dp', 0, 0, axis_index_groups=CHIP_GROUPS, tiled=True)  16.4 us
    all_to_all x1, blocking collectives, local(): lax.all_to_all(jnp.broadcast_to(row[None], (ZN, HALF, TILE)), 'dp', 0, 0,...  14.8 us
    all_to_all x1, waiting for transfers between devices, local(): lax.all_to_all(sent, 'dp', 0, 0, axis_index_groups=CHIP_GROUPS, tiled=True)  9.49 us
    ppermute x6, waiting for transfers between devices, send(): return lax.ppermute(block, 'dp', ring(step, 1))  9.27 us
    ppermute x3, waiting for transfers between devices, local(): pieces = [rows] + [lax.ppermute(rows, 'dp', ring(s, 0)) for s in STEPS[1:]]  6.86 us
    ppermute x6, starting transfers between devices, send(): return lax.ppermute(block, 'dp', ring(step, 1))  6.82 us
    ppermute x8, starting transfers between devices, swap(): return [lax.ppermute(b, 'dp', SWAP) for b in blocks]  6.39 us
    reduce_or x1, other arithmetic, local(): hit = jnp.any(kept_tiles[:, :, None] == chosen[None, None, :], axis=-1)  5.37 us
  transfers between devices with their start and end apart: 19, of which 8 were waited for; matrix products, arithmetic and copies ran while one was open for 9% of the time, Pallas kernels for 4%

profile of v7, /device:TPU:1, one launch (start us, length us, event | category | flops | bytes accessed | tf_op | source)
XLA Modules:
  0.0 95.7 jit_solution(5763918052126530253)
XLA Ops:
  0.0 3.3 %own_tiles.1 = f32[128,8,128]{2,1,0:T(8,128)} custom-call(s32[8,256]{1,0:T(8,128)} %bitcast.8, bf16[128,8192]{1,0:T(8,128)(2,1)} %act_ref.1, bf16[128,2048]{1,0:T(8,128)(2,1)} %cot_ref.1), custom_call_target="tpu_custom_call" | custom-call | tf_op jit(solution)/shard_map/own_tiles/pallas_call | solution.py:80
  3.3 16.4 %all-to-all-start = ((f32[128,8,128]{2,1,0:T(8,128)}), f32[128,8,128]{2,1,0:T(8,128)S(1)}, u32[]{:S(2)}, u32[]{:S(2)}) async-start(f32[128,8,128]{2,1,0:T(8,128)} %own_tiles.1), calls=%async_computation | async-start | bytes 1048576 | tf_op jit(solution)/shard_map/all_to_all | solution.py:191
  21.3 5.4 %compare_reduce_fusion = pred[256,8]{1,0:T(8,128)(4,1)S(1)} fusion(s32[256]{0:T(256)} %param.11, s32[256,8]{1,0:T(8,128)S(1)} %copy.14), kind=kLoop, calls=%fused_computation.1 | loop fusion | flops 1046528 | bytes 11264 | tf_op jit(solution)/shard_map/reduce_or | solution.py:187
  28.2 9.5 %all-to-all-done = f32[128,8,128]{2,1,0:T(8,128)S(1)} async-done(((f32[128,8,128]{2,1,0:T(8,128)}), f32[128,8,128]{2,1,0:T(8,128)S(1)}, u32[]{:S(2)}, u32[]{:S(2)}) %all-to-all-start) | async-done | bytes 524320 | tf_op jit(solution)/shard_map/all_to_all | solution.py:191
  38.3 3.0 %collective-permute-start = (f32[128,128]{1,0:T(8,128)S(1)}, f32[128,128]{1,0:T(8,128)S(1)}, u32[]{:S(2)}, u32[]{:S(2)}) collective-permute-start(f32[128,128]{1,0:T(8,128)S(1)} %get-tuple-element.13), channel_id=1, source_target_pairs={{0,1},{1,0},{2,3},{3,2},{4,5},{5,4},{6,7},{7,6},{8,9},{9,8},{10,11... | collective-permute-start | bytes 196616 | tf_op jit(solution)/shard_map/ppermute | solution.py:193
  41.4 0.9 collective-permute-done
  42.3 14.8 %all_to_all.10.p0 = bf16[8,128,128]{2,1,0:T(8,128)(2,1)S(1)} all-to-all(bf16[8,128,128]{2,1,0:T(8,128)(2,1)S(1)} %broadcast_in_dim.7), channel_id=1, replica_groups={{0,32,64,96,128,160,192,224},{1,33,65,97,129,161,193,225},{2,34,66,98,1..., dimensions={0} | all-to-all | bytes 524288 | tf_op jit(solution)/shard_map/all_to_all | solution.py:195
  57.1 2.7 %collective-permute-start.3 = (bf16[8,128,128]{2,1,0:T(8,128)(2,1)S(1)}, bf16[8,128,128]{2,1,0:T(8,128)(2,1)S(1)}, u32[]{:S(2)}, u32[]{:S(2)}) collective-permute-start(bf16[8,128,128]{2,1,0:T(8,128)(2,1)S(1)} %all_to_all.10.p0), channel_id=1, source_target_pairs={{0,24},{1,7},{2,26},{3,1},{4,28},{5,3},{6,30},{7,5},{8,0},{9,15},{... | collective-permute-start | bytes 786440 | tf_op jit(solution)/shard_map/s2/ppermute | solution.py:211
  59.8 4.4 %collective-permute-done.1.p1 = bf16[8,128,128]{2,1,0:T(8,128)(2,1)S(1)} collective-permute-done((bf16[8,128,128]{2,1,0:T(8,128)(2,1)S(1)}, bf16[8,128,128]{2,1,0:T(8,128)(2,1)S(1)}, u32[]{:S(2)}, u32[]{:S(2)}) %collective-permute-start.1) | collective-permute-done | bytes 262176 | tf_op jit(solution)/shard_map/s2/ppermute | solution.py:211
  64.1 2.5 %collective-permute-done.2.p2 = bf16[8,128,128]{2,1,0:T(8,128)(2,1)S(1)} collective-permute-done((bf16[8,128,128]{2,1,0:T(8,128)(2,1)S(1)}, bf16[8,128,128]{2,1,0:T(8,128)(2,1)S(1)}, u32[]{:S(2)}, u32[]{:S(2)}) %collective-permute-start.2) | collective-permute-done | bytes 262176 | tf_op jit(solution)/shard_map/s2/ppermute | solution.py:211
  66.6 1.4 %by_rows.1 = (bf16[64,32,128]{2,1,0:T(8,128)(2,1)S(1)}, bf16[64,32,128]{2,1,0:T(8,128)(2,1)S(1)}) custom-call(bf16[8,128,128]{2,1,0:T(8,128)(2,1)S(1)} %all_to_all.10.p0, bf16[8,128,128]{2,1,0:T(8,128)(2,1)S(1)} %collective-permute-done.1.p1, bf16[8,128,128]{2,1,0:T(8,128)(2,1)S(1)} %collective-permute-done.2.p2, ...), custom_call_target="tpu_custom_call" | custom-call | tf_op jit(solution)/shard_map/by_rows/pallas_call | solution.py:141
  68.0 1.7 %collective-permute-start.6 = (bf16[64,32,128]{2,1,0:T(8,128)(2,1)S(1)}, bf16[64,32,128]{2,1,0:T(8,128)(2,1)S(1)}, u32[]{:S(2)}, u32[]{:S(2)}) collective-permute-start(bf16[64,32,128]{2,1,0:T(8,128)(2,1)S(1)} %get-tuple-element.14.refs_0_), channel_id=1, source_target_pairs={{0,1},{1,0},{2,3},{3,2},{4,5},{5,4},{6,7},{7,6},{8,9},{9,8},{10,11... | collective-permute-start | bytes 1572872 | tf_op jit(solution)/shard_map/own/ppermute | solution.py:200
  69.9 2.7 %collective-permute-start.5 = (bf16[64,32,128]{2,1,0:T(8,128)(2,1)S(1)}, bf16[64,32,128]{2,1,0:T(8,128)(2,1)S(1)}, u32[]{:S(2)}, u32[]{:S(2)}) collective-permute-start(bf16[64,32,128]{2,1,0:T(8,128)(2,1)S(1)} %get-tuple-element.15.refs_1_), channel_id=1, source_target_pairs={{0,6},{1,25},{2,0},{3,27},{4,2},{5,29},{6,4},{7,31},{8,14},{9,1},{... | collective-permute-start | bytes 1572872 | tf_op jit(solution)/shard_map/b3/ppermute | solution.py:204
  72.6 1.4 %collective-permute-start.13 = (bf16[64,32,128]{2,1,0:T(8,128)(2,1)S(1)}, bf16[64,32,128]{2,1,0:T(8,128)(2,1)S(1)}, u32[]{:S(2)}, u32[]{:S(2)}) collective-permute-start(bf16[64,32,128]{2,1,0:T(8,128)(2,1)S(1)} %get-tuple-element.15.refs_1_), channel_id=1, source_target_pairs={{0,2},{1,9},{2,4},{3,11},{4,6},{5,13},{6,0},{7,15},{8,10},{9,17},{... | collective-permute-start | bytes 1572872 | tf_op jit(solution)/shard_map/b1/ppermute | solution.py:204
  74.0 1.3 %join.3.refs_8_ = bf16[2,2,64,4,32,128]{5,4,3,2,1,0:T(8,128)(2,1)} custom-call(bf16[64,32,128]{2,1,0:T(8,128)(2,1)S(1)} %get-tuple-element.14.refs_0_, bf16[64,32,128]{2,1,0:T(8,128)(2,1)S(1)} %get-tuple-element.15.refs_1_, bf16[64,32,128]{2,1,0:T(8,128)(2,1)S(1)} %collective-permute-done.6.refs_2_, bf16[64,32,128]{2,1,0:T(8,128)(2,1)S(1)} %collective-permute-done.7.refs_3_), custom_call_target="tpu_custom_call" | custom-call | bytes 4194304 | tf_op jit(solution)/shard_map/join/pallas_call | solution.py:169
  75.4 4.0 %collective-permute-done.4.refs_0_ = bf16[64,32,128]{2,1,0:T(8,128)(2,1)S(1)} collective-permute-done((bf16[64,32,128]{2,1,0:T(8,128)(2,1)S(1)}, bf16[64,32,128]{2,1,0:T(8,128)(2,1)S(1)}, u32[]{:S(2)}, u32[]{:S(2)}) %collective-permute-start.4) | collective-permute-done | bytes 524320 | tf_op jit(solution)/shard_map/a1/ppermute | solution.py:204
  79.4 1.3 %collective-permute-start.14 = (bf16[64,32,128]{2,1,0:T(8,128)(2,1)S(1)}, bf16[64,32,128]{2,1,0:T(8,128)(2,1)S(1)}, u32[]{:S(2)}, u32[]{:S(2)}) collective-permute-start(bf16[64,32,128]{2,1,0:T(8,128)(2,1)S(1)} %collective-permute-done.4.refs_0_), channel_id=1, source_target_pairs={{0,1},{1,0},{2,3},{3,2},{4,5},{5,4},{6,7},{7,6},{8,9},{9,8},{10,11... | collective-permute-start | bytes 1572872 | tf_op jit(solution)/shard_map/near/ppermute | solution.py:200
  80.7 2.7 %collective-permute-start.9 = (bf16[64,32,128]{2,1,0:T(8,128)(2,1)S(1)}, bf16[64,32,128]{2,1,0:T(8,128)(2,1)S(1)}, u32[]{:S(2)}, u32[]{:S(2)}) collective-permute-start(bf16[64,32,128]{2,1,0:T(8,128)(2,1)S(1)} %collective-permute-done.5.refs_3_), channel_id=1, source_target_pairs={{0,6},{1,25},{2,0},{3,27},{4,2},{5,29},{6,4},{7,31},{8,14},{9,1},{... | collective-permute-start | bytes 1572872 | tf_op jit(solution)/shard_map/b2/ppermute | solution.py:204
  83.3 0.9 collective-permute-done.12.refs_1_
  84.3 1.5 %collective-permute-start.17 = (bf16[64,32,128]{2,1,0:T(8,128)(2,1)S(1)}, bf16[64,32,128]{2,1,0:T(8,128)(2,1)S(1)}, u32[]{:S(2)}, u32[]{:S(2)}) collective-permute-start(bf16[64,32,128]{2,1,0:T(8,128)(2,1)S(1)} %collective-permute-done.5.refs_3_), channel_id=1, source_target_pairs={{0,1},{1,0},{2,3},{3,2},{4,5},{5,4},{6,7},{7,6},{8,9},{9,8},{10,11... | collective-permute-start | bytes 1572872 | tf_op jit(solution)/shard_map/near/ppermute | solution.py:200
  86.3 4.3 %collective-permute-done.8.refs_0_ = bf16[64,32,128]{2,1,0:T(8,128)(2,1)S(1)} collective-permute-done((bf16[64,32,128]{2,1,0:T(8,128)(2,1)S(1)}, bf16[64,32,128]{2,1,0:T(8,128)(2,1)S(1)}, u32[]{:S(2)}, u32[]{:S(2)}) %collective-permute-start.8) | collective-permute-done | bytes 524320 | tf_op jit(solution)/shard_map/a2/ppermute | solution.py:204
  90.6 1.3 %collective-permute-start.10 = (bf16[64,32,128]{2,1,0:T(8,128)(2,1)S(1)}, bf16[64,32,128]{2,1,0:T(8,128)(2,1)S(1)}, u32[]{:S(2)}, u32[]{:S(2)}) collective-permute-start(bf16[64,32,128]{2,1,0:T(8,128)(2,1)S(1)} %collective-permute-done.8.refs_0_), channel_id=1, source_target_pairs={{0,1},{1,0},{2,3},{3,2},{4,5},{5,4},{6,7},{7,6},{8,9},{9,8},{10,11... | collective-permute-start | bytes 1572872 | tf_op jit(solution)/shard_map/far/ppermute | solution.py:200
  91.9 2.1 %join.4.refs_4_ = bf16[2,2,64,4,32,128]{5,4,3,2,1,0:T(8,128)(2,1)} custom-call(bf16[64,32,128]{2,1,0:T(8,128)(2,1)S(1)} %collective-permute-done.4.refs_0_, bf16[64,32,128]{2,1,0:T(8,128)(2,1)S(1)} %collective-permute-done.12.refs_1_, bf16[64,32,128]{2,1,0:T(8,128)(2,1)S(1)} %collective-permute-done.13.refs_2_, ...), custom_call_target="tpu_custom_call", output_to_operand_aliasing={{}: (8, {})} | custom-call | bytes 8388608 | tf_op jit(solution)/shard_map/join/pallas_call | solution.py:169
  94.2 1.3 %join.5 = bf16[2,2,64,4,32,128]{5,4,3,2,1,0:T(8,128)(2,1)} custom-call(bf16[64,32,128]{2,1,0:T(8,128)(2,1)S(1)} %collective-permute-done.8.refs_0_, bf16[64,32,128]{2,1,0:T(8,128)(2,1)S(1)} %collective-permute-done.9.refs_1_, bf16[64,32,128]{2,1,0:T(8,128)(2,1)S(1)} %collective-permute-done.10.refs_2_, ...), custom_call_target="tpu_custom_call", output_to_operand_aliasing={{}: (4, {})} | custom-call | bytes 4194304 | tf_op jit(solution)/shard_map/join/pallas_call | solution.py:169
  (30 shorter events, 4.5 us)
Async XLA Ops:
  3.3 34.4 %all-to-all-start = ((f32[128,8,128]{2,1,0:T(8,128)}), f32[128,8,128]{2,1,0:T(8,128)S(1)}, u32[]{:S(2)}, u32[]{:S(2)}) async-start(f32[128,8,128]{2,1,0:T(8,128)} %own_tiles.1), calls=%async_computation | async-start | bytes 1048576 | tf_op jit(solution)/shard_map/all_to_all | solution.py:191
  38.3 3.9 %collective-permute-start = (f32[128,128]{1,0:T(8,128)S(1)}, f32[128,128]{1,0:T(8,128)S(1)}, u32[]{:S(2)}, u32[]{:S(2)}) collective-permute-start(f32[128,128]{1,0:T(8,128)S(1)} %get-tuple-element.13), channel_id=1, source_target_pairs={{0,1},{1,0},{2,3},{3,2},{4,5},{5,4},{6,7},{7,6},{8,9},{9,8},{10,11... | collective-permute-start | bytes 196616 | tf_op jit(solution)/shard_map/ppermute | solution.py:193
  57.1 7.1 %collective-permute-start.1 = (bf16[8,128,128]{2,1,0:T(8,128)(2,1)S(1)}, bf16[8,128,128]{2,1,0:T(8,128)(2,1)S(1)}, u32[]{:S(2)}, u32[]{:S(2)}) collective-permute-start(bf16[8,128,128]{2,1,0:T(8,128)(2,1)S(1)} %all_to_all.10.p0), channel_id=1, source_target_pairs={{0,16},{1,5},{2,18},{3,7},{4,20},{5,1},{6,22},{7,3},{8,24},{9,13},... | collective-permute-start | bytes 786440 | tf_op jit(solution)/shard_map/s2/ppermute | solution.py:211
  57.1 9.5 %collective-permute-start.2 = (bf16[8,128,128]{2,1,0:T(8,128)(2,1)S(1)}, bf16[8,128,128]{2,1,0:T(8,128)(2,1)S(1)}, u32[]{:S(2)}, u32[]{:S(2)}) collective-permute-start(bf16[8,128,128]{2,1,0:T(8,128)(2,1)S(1)} %all_to_all.10.p0), channel_id=1, source_target_pairs={{0,8},{1,3},{2,10},{3,5},{4,12},{5,7},{6,14},{7,1},{8,16},{9,11},{... | collective-permute-start | bytes 786440 | tf_op jit(solution)/shard_map/s2/ppermute | solution.py:211
  57.1 9.5 %collective-permute-start.3 = (bf16[8,128,128]{2,1,0:T(8,128)(2,1)S(1)}, bf16[8,128,128]{2,1,0:T(8,128)(2,1)S(1)}, u32[]{:S(2)}, u32[]{:S(2)}) collective-permute-start(bf16[8,128,128]{2,1,0:T(8,128)(2,1)S(1)} %all_to_all.10.p0), channel_id=1, source_target_pairs={{0,24},{1,7},{2,26},{3,1},{4,28},{5,3},{6,30},{7,5},{8,0},{9,15},{... | collective-permute-start | bytes 786440 | tf_op jit(solution)/shard_map/s2/ppermute | solution.py:211
  68.0 4.5 %collective-permute-start.6 = (bf16[64,32,128]{2,1,0:T(8,128)(2,1)S(1)}, bf16[64,32,128]{2,1,0:T(8,128)(2,1)S(1)}, u32[]{:S(2)}, u32[]{:S(2)}) collective-permute-start(bf16[64,32,128]{2,1,0:T(8,128)(2,1)S(1)} %get-tuple-element.14.refs_0_), channel_id=1, source_target_pairs={{0,1},{1,0},{2,3},{3,2},{4,5},{5,4},{6,7},{7,6},{8,9},{9,8},{10,11... | collective-permute-start | bytes 1572872 | tf_op jit(solution)/shard_map/own/ppermute | solution.py:200
  69.7 4.3 %collective-permute-start.7 = (bf16[64,32,128]{2,1,0:T(8,128)(2,1)S(1)}, bf16[64,32,128]{2,1,0:T(8,128)(2,1)S(1)}, u32[]{:S(2)}, u32[]{:S(2)}) collective-permute-start(bf16[64,32,128]{2,1,0:T(8,128)(2,1)S(1)} %get-tuple-element.15.refs_1_), channel_id=1, source_target_pairs={{0,1},{1,0},{2,3},{3,2},{4,5},{5,4},{6,7},{7,6},{8,9},{9,8},{10,11... | collective-permute-start | bytes 1572872 | tf_op jit(solution)/shard_map/own/ppermute | solution.py:200
  69.8 9.5 %collective-permute-start.4 = (bf16[64,32,128]{2,1,0:T(8,128)(2,1)S(1)}, bf16[64,32,128]{2,1,0:T(8,128)(2,1)S(1)}, u32[]{:S(2)}, u32[]{:S(2)}) collective-permute-start(bf16[64,32,128]{2,1,0:T(8,128)(2,1)S(1)} %get-tuple-element.14.refs_0_), channel_id=1, source_target_pairs={{0,2},{1,9},{2,4},{3,11},{4,6},{5,13},{6,0},{7,15},{8,10},{9,17},{... | collective-permute-start | bytes 1572872 | tf_op jit(solution)/shard_map/a1/ppermute | solution.py:204
  69.9 9.5 %collective-permute-start.5 = (bf16[64,32,128]{2,1,0:T(8,128)(2,1)S(1)}, bf16[64,32,128]{2,1,0:T(8,128)(2,1)S(1)}, u32[]{:S(2)}, u32[]{:S(2)}) collective-permute-start(bf16[64,32,128]{2,1,0:T(8,128)(2,1)S(1)} %get-tuple-element.15.refs_1_), channel_id=1, source_target_pairs={{0,6},{1,25},{2,0},{3,27},{4,2},{5,29},{6,4},{7,31},{8,14},{9,1},{... | collective-permute-start | bytes 1572872 | tf_op jit(solution)/shard_map/b3/ppermute | solution.py:204
  72.5 11.7 %collective-permute-start.12 = (bf16[64,32,128]{2,1,0:T(8,128)(2,1)S(1)}, bf16[64,32,128]{2,1,0:T(8,128)(2,1)S(1)}, u32[]{:S(2)}, u32[]{:S(2)}) collective-permute-start(bf16[64,32,128]{2,1,0:T(8,128)(2,1)S(1)} %get-tuple-element.14.refs_0_), channel_id=1, source_target_pairs={{0,6},{1,25},{2,0},{3,27},{4,2},{5,29},{6,4},{7,31},{8,14},{9,1},{... | collective-permute-start | bytes 1572872 | tf_op jit(solution)/shard_map/a3/ppermute | solution.py:204
  72.6 13.3 %collective-permute-start.13 = (bf16[64,32,128]{2,1,0:T(8,128)(2,1)S(1)}, bf16[64,32,128]{2,1,0:T(8,128)(2,1)S(1)}, u32[]{:S(2)}, u32[]{:S(2)}) collective-permute-start(bf16[64,32,128]{2,1,0:T(8,128)(2,1)S(1)} %get-tuple-element.15.refs_1_), channel_id=1, source_target_pairs={{0,2},{1,9},{2,4},{3,11},{4,6},{5,13},{6,0},{7,15},{8,10},{9,17},{... | collective-permute-start | bytes 1572872 | tf_op jit(solution)/shard_map/b1/ppermute | solution.py:204
  79.4 6.9 %collective-permute-start.14 = (bf16[64,32,128]{2,1,0:T(8,128)(2,1)S(1)}, bf16[64,32,128]{2,1,0:T(8,128)(2,1)S(1)}, u32[]{:S(2)}, u32[]{:S(2)}) collective-permute-start(bf16[64,32,128]{2,1,0:T(8,128)(2,1)S(1)} %collective-permute-done.4.refs_0_), channel_id=1, source_target_pairs={{0,1},{1,0},{2,3},{3,2},{4,5},{5,4},{6,7},{7,6},{8,9},{9,8},{10,11... | collective-permute-start | bytes 1572872 | tf_op jit(solution)/shard_map/near/ppermute | solution.py:200
  80.7 10.0 %collective-permute-start.8 = (bf16[64,32,128]{2,1,0:T(8,128)(2,1)S(1)}, bf16[64,32,128]{2,1,0:T(8,128)(2,1)S(1)}, u32[]{:S(2)}, u32[]{:S(2)}) collective-permute-start(bf16[64,32,128]{2,1,0:T(8,128)(2,1)S(1)} %collective-permute-done.4.refs_0_), channel_id=1, source_target_pairs={{0,2},{1,9},{2,4},{3,11},{4,6},{5,13},{6,0},{7,15},{8,10},{9,17},{... | collective-permute-start | bytes 1572872 | tf_op jit(solution)/shard_map/a2/ppermute | solution.py:204
  80.7 11.2 %collective-permute-start.9 = (bf16[64,32,128]{2,1,0:T(8,128)(2,1)S(1)}, bf16[64,32,128]{2,1,0:T(8,128)(2,1)S(1)}, u32[]{:S(2)}, u32[]{:S(2)}) collective-permute-start(bf16[64,32,128]{2,1,0:T(8,128)(2,1)S(1)} %collective-permute-done.5.refs_3_), channel_id=1, source_target_pairs={{0,6},{1,25},{2,0},{3,27},{4,2},{5,29},{6,4},{7,31},{8,14},{9,1},{... | collective-permute-start | bytes 1572872 | tf_op jit(solution)/shard_map/b2/ppermute | solution.py:204
  84.3 7.6 %collective-permute-start.17 = (bf16[64,32,128]{2,1,0:T(8,128)(2,1)S(1)}, bf16[64,32,128]{2,1,0:T(8,128)(2,1)S(1)}, u32[]{:S(2)}, u32[]{:S(2)}) collective-permute-start(bf16[64,32,128]{2,1,0:T(8,128)(2,1)S(1)} %collective-permute-done.5.refs_3_), channel_id=1, source_target_pairs={{0,1},{1,0},{2,3},{3,2},{4,5},{5,4},{6,7},{7,6},{8,9},{9,8},{10,11... | collective-permute-start | bytes 1572872 | tf_op jit(solution)/shard_map/near/ppermute | solution.py:200
  85.8 6.1 %collective-permute-start.15 = (bf16[64,32,128]{2,1,0:T(8,128)(2,1)S(1)}, bf16[64,32,128]{2,1,0:T(8,128)(2,1)S(1)}, u32[]{:S(2)}, u32[]{:S(2)}) collective-permute-start(bf16[64,32,128]{2,1,0:T(8,128)(2,1)S(1)} %collective-permute-done.12.refs_1_), channel_id=1, source_target_pairs={{0,1},{1,0},{2,3},{3,2},{4,5},{5,4},{6,7},{7,6},{8,9},{9,8},{10,11... | collective-permute-start | bytes 1572872 | tf_op jit(solution)/shard_map/near/ppermute | solution.py:200
  86.3 5.6 %collective-permute-start.16 = (bf16[64,32,128]{2,1,0:T(8,128)(2,1)S(1)}, bf16[64,32,128]{2,1,0:T(8,128)(2,1)S(1)}, u32[]{:S(2)}, u32[]{:S(2)}) collective-permute-start(bf16[64,32,128]{2,1,0:T(8,128)(2,1)S(1)} %collective-permute-done.13.refs_2_), channel_id=1, source_target_pairs={{0,1},{1,0},{2,3},{3,2},{4,5},{5,4},{6,7},{7,6},{8,9},{9,8},{10,11... | collective-permute-start | bytes 1572872 | tf_op jit(solution)/shard_map/near/ppermute | solution.py:200
  90.6 3.4 %collective-permute-start.10 = (bf16[64,32,128]{2,1,0:T(8,128)(2,1)S(1)}, bf16[64,32,128]{2,1,0:T(8,128)(2,1)S(1)}, u32[]{:S(2)}, u32[]{:S(2)}) collective-permute-start(bf16[64,32,128]{2,1,0:T(8,128)(2,1)S(1)} %collective-permute-done.8.refs_0_), channel_id=1, source_target_pairs={{0,1},{1,0},{2,3},{3,2},{4,5},{5,4},{6,7},{7,6},{8,9},{9,8},{10,11... | collective-permute-start | bytes 1572872 | tf_op jit(solution)/shard_map/far/ppermute | solution.py:200
  91.9 2.3 %collective-permute-start.11 = (bf16[64,32,128]{2,1,0:T(8,128)(2,1)S(1)}, bf16[64,32,128]{2,1,0:T(8,128)(2,1)S(1)}, u32[]{:S(2)}, u32[]{:S(2)}) collective-permute-start(bf16[64,32,128]{2,1,0:T(8,128)(2,1)S(1)} %collective-permute-done.9.refs_1_), channel_id=1, source_target_pairs={{0,1},{1,0},{2,3},{3,2},{4,5},{5,4},{6,7},{7,6},{8,9},{9,8},{10,11... | collective-permute-start | bytes 1572872 | tf_op jit(solution)/shard_map/far/ppermute | solution.py:200
